TPU v7x, 32 devices: a whole 2x2x4 slice. The times are simulated.
32 devices in a mesh: region: 8 (over z, core), group: 4 (over y, x).
Axes of the slice: x: 2, y: 2, z: 4, core: 2. Of those that a mesh axis runs over, the one named last changes fastest.
Arguments:
- features: bfloat16 [12288, 2048], P(('region', 'group')), may hold values from -1.5 to 1.5
- memory: bfloat16 [4096, 2048], P(('region', 'group')), may hold values from -1 to 1
- requests: int32 [32, 2], P(('region', 'group')), may hold values from 0 to 3, as said below
- owners: int32 [8, 4], P('region'), may hold values from 0 to 3, as said below
- labels: int32 [32, 384], P(('region', 'group')), may hold values from 0 to 1023, as said below
Outputs:
- feat_grad: bfloat16 [12288, 2048], P(('region', 'group'))
- new_memory: bfloat16 [4096, 2048], P(('region', 'group'))
Inputs may be any that keep to these rules, and one draw needn't show every extreme that they name: `owners`: each row of a region is a permutation. `requests`: the 2 numbers of a device are distinct blocks of its region. At most 96 crops of one device carry labels of one region, and every device reaches that bound for some region.
All inputs are finite; a program needn't handle non-finite values.
Results may differ from a plain program's by a relative error of at most 0.006.
Values may be sent and summed in bfloat16 or wider, within the bound.
No kernel may reach another device: no remote copies, remote signals or barrier semaphores. Data moves between devices by JAX's collectives and lax.ppermute only.
A program may use at most 64 MiB of HBM per device.

v0:
```python
import functools

import jax
import jax.numpy as jnp
from jax import lax
from jax.experimental import pallas as pl
from jax.experimental.pallas import tpu as pltpu
from jax.sharding import PartitionSpec as P

D = 2048
CORES = 2
WIDE = 4
LANES = 128
HALVES = 2
EXTRA = 16
BASE = 8

exponent_sharpness = 0.05
smoothing = 0.1
momentum_keep = 0.2

VMEM = pl.BlockSpec(memory_space=pltpu.VMEM)
SMEM = pl.BlockSpec(memory_space=pltpu.SMEM)
PARAMS = pltpu.CompilerParams(vmem_limit_bytes=16 * 2**20)


def write_sums(base, labels_ref, features_ref, block_rows, came, store, ready=None):
    crop_count, feat_width = features_ref.shape
    half_rows = block_rows // HALVES
    slabs = feat_width // LANES
    value = base + lax.broadcasted_iota(jnp.int32, (block_rows, crop_count), 0)
    match = jnp.where(labels_ref[...] == value, 1.0, 0.0).astype(jnp.bfloat16)

    def put(h, first, part):
        if came is not None:
            part = part + came(h, first, part.shape[0]).astype(jnp.float32)
        store(h, first, part.astype(jnp.bfloat16))

    wide = WIDE
    for s in range(0, slabs, wide):
        if ready is not None:
            ready(s // wide)
        part = jnp.dot(
            match,
            features_ref[:, s * LANES : (s + wide) * LANES],
            preferred_element_type=jnp.float32,
        )
        for h in range(HALVES):
            for i in range(wide):
                put(
                    h,
                    (s + i) * half_rows,
                    part[h * half_rows : (h + 1) * half_rows, i * LANES : (i + 1) * LANES],
                )
    counts = lax.dot_general(
        jnp.ones((EXTRA, crop_count), jnp.bfloat16),
        match,
        (((1,), (1,)), ((), ())),
        preferred_element_type=jnp.float32,
    )
    high = jnp.floor(counts * (1.0 / BASE))
    digit = lax.broadcasted_iota(jnp.int32, counts.shape, 0)
    digits = jnp.where(digit == 0, counts - BASE * high, jnp.where(digit == 1, high, 0.0))
    for h in range(HALVES):
        put(h, slabs * half_rows, digits)


def layer_at(place, layers):
    layer = lax.axis_index("region") // CORES
    return jnp.where(layer < layers // 2, layers - 1 - place, place)


def base_at(place, layers, core, block_rows):
    return (layer_at(place, layers) * CORES + core) * block_rows


def block_of(ref, *at):
    def store(h, first, part):
        ref[(*at, h, pl.ds(first, part.shape[0]), slice(None))] = part

    return store


def came_at(ref, *at):
    return lambda h, first, rows: ref[(*at, h, pl.ds(first, rows), slice(None))]


def away_kernel(
    layers, block_rows, labels_hbm, features_hbm, first_ref, rest_ref, labels_ref, features_ref, sems
):
    columns = WIDE * LANES
    copies = [pltpu.make_async_copy(labels_hbm, labels_ref, sems.at[0])]
    for i in range(features_ref.shape[1] // columns):
        part = (slice(None), pl.ds(i * columns, columns))
        copies.append(
            pltpu.make_async_copy(features_hbm.at[part], features_ref.at[part], sems.at[i + 1])
        )
    for copy in copies:
        copy.start()
    copies[0].wait()
    core = 1 - lax.axis_index("region") % CORES
    write_sums(
        base_at(0, layers, core, block_rows),
        labels_ref,
        features_ref,
        block_rows,
        None,
        block_of(first_ref, 0),
        lambda i: copies[i + 1].wait(),
    )

    def one(p, carry):
        base = base_at(p + 1, layers, core, block_rows)
        write_sums(base, labels_ref, features_ref, block_rows, None, block_of(rest_ref, p))
        return carry

    lax.fori_loop(0, layers - 1, one, 0)


def chip_kernel(layers, block_rows, start, labels_ref, features_ref, came_ref, out_ref):
    core = lax.axis_index("region") % CORES

    def one(p, carry):
        base = base_at(p + start, layers, core, block_rows)
        write_sums(
            base, labels_ref, features_ref, block_rows, came_at(came_ref, p), block_of(out_ref, p)
        )
        return carry

    lax.fori_loop(0, out_ref.shape[0], one, 0)


def join_kernel(layers, hop, odd, first_ref, rest_ref, came_ref, out_ref):
    layer = lax.axis_index("region") // CORES
    up = (layer % 2 == 1) if odd else (layer % 2 == 0)
    target = jnp.where(up, layers - 1 - hop + layer, hop - (layers - 1 - layer))
    target = jnp.clip(target, 0, layers - 1)
    place = jnp.where(layer < layers // 2, layers - 1 - target, target)

    def add(mine):
        out_ref[0] = (
            mine.astype(jnp.float32) + came_ref[0].astype(jnp.float32)
        ).astype(jnp.bfloat16)

    @pl.when(place == 0)
    def _():
        add(first_ref[0])

    @pl.when(place > 0)
    def _():
        add(rest_ref[jnp.maximum(place - 1, 0)])


def join_first_kernel(first_ref, came_ref, rest_ref, out_ref, second_ref):
    out_ref[...] = (
        first_ref[...].astype(jnp.float32) + came_ref[...].astype(jnp.float32)
    ).astype(jnp.bfloat16)
    second_ref[0] = rest_ref[0]


def update_kernel(layers, memory_ref, rest_ref, *rest):
    layer = lax.axis_index("region") // CORES
    place = jnp.where(layer < layers // 2, layers - 1 - layer, layer) - 1
    came_refs, out_ref, mixed_ref = rest[:-2], rest[-2], rest[-1]
    block_rows, feat_width = memory_ref.shape
    half_rows = block_rows // HALVES
    slabs = feat_width // LANES
    for h in range(HALVES):

        def total(first, rows):
            t = rest_ref[place, h, pl.ds(first, rows), :].astype(jnp.float32)
            for ref in came_refs:
                t = t + ref[0, h, pl.ds(first, rows), :].astype(jnp.float32)
            return t

        digits = total(slabs * half_rows, EXTRA)
        counts_row = digits[0:1, :] + BASE * digits[1:2, :]
        row = lax.broadcasted_iota(jnp.int32, (half_rows, LANES), 0) + h * half_rows
        lane = lax.broadcasted_iota(jnp.int32, (half_rows, LANES), 1)
        counts = jnp.sum(jnp.where(row == lane, counts_row, 0.0), axis=1, keepdims=True)
        seen = counts > 0
        divisor = jnp.maximum(counts, 1.0)
        squares = jnp.zeros((half_rows, LANES), jnp.float32)
        for s in range(slabs):
            old = memory_ref[pl.ds(h * half_rows, half_rows), pl.ds(s * LANES, LANES)].astype(
                jnp.float32
            )
            averaged = total(s * half_rows, half_rows) / divisor
            mixed = jnp.where(seen, momentum_keep * old + (1.0 - momentum_keep) * averaged, old)
            mixed_ref[:, pl.ds(s * LANES, LANES)] = mixed
            squares = squares + mixed * mixed
        mean = jnp.sum(squares, axis=1, keepdims=True) * (1.0 / feat_width)
        scale = lax.rsqrt(mean + 1e-06) * D ** (-0.5)
        out_ref[pl.ds(h * half_rows, half_rows), :] = (mixed_ref[...] * scale).astype(jnp.bfloat16)


def grad_kernel(requests_ref, owners_ref, features_ref, *rest):
    group = lax.axis_index("group")
    out_ref, candidates_ref, sems = rest[-3:]
    blocks = rest[:-3]
    block_rows = blocks[0].shape[0]
    cand_count = candidates_ref.shape[0]
    wanted_count = cand_count // block_rows

    def copy(j, k):
        return pltpu.make_async_copy(
            blocks[j], candidates_ref.at[pl.ds(k * block_rows, block_rows), :], sems.at[k]
        )

    for k in range(wanted_count):
        place = owners_ref[0, requests_ref[0, k]] ^ group
        for j in range(len(blocks)):
            @pl.when(place == j)
            def _():
                copy(j, k).start()
    for k in range(wanted_count):
        copy(0, k).wait()
    scores = (
        lax.dot_general(
            features_ref[...],
            candidates_ref[...],
            (((1,), (1,)), ((), ())),
            preferred_element_type=jnp.float32,
        )
        / exponent_sharpness
    )
    expo = jnp.exp(scores - jnp.max(scores, axis=1, keepdims=True))
    likelihoods = expo / jnp.sum(expo, axis=1, keepdims=True)
    column = lax.broadcasted_iota(jnp.int32, (1, cand_count), 1)
    target = jnp.where(column < block_rows, (1.0 - smoothing) / block_rows, 0.0) + (
        smoothing / cand_count
    )
    logit_grad = ((likelihoods - target) / exponent_sharpness).astype(jnp.bfloat16)
    wide = 512
    for n in range(0, out_ref.shape[1], wide):
        out_ref[:, n : n + wide] = jnp.dot(
            logit_grad, candidates_ref[:, n : n + wide], preferred_element_type=jnp.float32
        ).astype(jnp.bfloat16)


def on_device(features, memory, requests, owners, labels):
    group_count = lax.axis_size("group")
    region_count = lax.axis_size("region")
    layers = region_count // CORES
    crop_count, feat_width = features.shape
    block_rows = memory.shape[0]
    half_rows = block_rows // HALVES
    pay_rows = feat_width // LANES * half_rows + EXTRA
    bf16 = jnp.bfloat16
    after = lax.optimization_barrier

    def call(kernel, name, out_shape, operands, flops, scratch=(), smem=0, any_from=None, params=PARAMS):
        outs = out_shape if isinstance(out_shape, list) else [out_shape]
        flat, tree = jax.tree.flatten(operands)
        specs = [SMEM if i < smem else VMEM for i in range(len(flat))]
        if any_from is not None:
            specs[any_from:] = [pl.BlockSpec(memory_space=pl.ANY)] * (len(flat) - any_from)
        return pl.pallas_call(
            kernel,
            out_shape=out_shape,
            in_specs=specs,
            out_specs=[VMEM] * len(outs) if isinstance(out_shape, list) else VMEM,
            scratch_shapes=list(scratch),
            compiler_params=params,
            cost_estimate=pl.CostEstimate(
                flops=flops,
                bytes_accessed=sum(2 * x.size for x in [*flat, *outs]),
                transcendentals=0,
            ),
            name=name,
        )(*flat)

    swap = [(r, r ^ 1) for r in range(region_count)]
    block_flops = 2 * block_rows * crop_count * feat_width
    part = functools.partial

    def payloads(count):
        return jax.ShapeDtypeStruct((count, HALVES, pay_rows, LANES), bf16)

    away_first, away_rest = call(
        part(away_kernel, layers, block_rows),
        "away",
        [payloads(1), payloads(layers - 1)],
        (labels, features),
        block_flops * layers,
        scratch=(
            pltpu.VMEM(labels.shape, labels.dtype),
            pltpu.VMEM(features.shape, bf16),
            pltpu.SemaphoreType.DMA((feat_width // (WIDE * LANES) + 1,)),
        ),
        any_from=0,
        params=pltpu.CompilerParams(vmem_limit_bytes=60 * 2**20),
    )
    came_first = lax.ppermute(away_first, "region", swap)
    first = call(
        part(chip_kernel, layers, block_rows, 0),
        "chip_first",
        payloads(1),
        (labels, features, came_first),
        block_flops,
    )
    first, away_rest, sent_memory = after((first, away_rest, memory))
    rest = call(
        part(chip_kernel, layers, block_rows, 1),
        "chip_rest",
        payloads(layers - 1),
        (labels, features, lax.ppermute(away_rest, "region", swap)),
        block_flops * (layers - 1),
    )

    blocks = {0: sent_memory}
    near = [k for k in range(1, group_count) if k & (k - 1) == 0]
    far = [k for k in range(1, group_count) if k & (k - 1)]

    def fetch(ks):
        for k in ks:
            bit = 1 << (k.bit_length() - 1)
            blocks[k] = lax.ppermute(
                blocks[k ^ bit], "group", [(g, g ^ bit) for g in range(group_count)]
            )

    even = [(r, ((r // CORES) ^ 1) * CORES + r % CORES) for r in range(region_count)]
    odd = []
    for z in range(1, layers - 1):
        other = z + 1 if z % 2 else z - 1
        odd += [(z * CORES + c, other * CORES + c) for c in range(CORES)]

    def joined(hop, is_odd, came):
        return call(
            part(join_kernel, layers, hop, is_odd),
            "join_odd" if is_odd else "join_even",
            payloads(1),
            (first, rest, came),
            HALVES * pay_rows * LANES,
        )

    even_came = lax.ppermute(first, "region", even)
    fetch(near)
    odd_next, even_next = call(
        join_first_kernel,
        "join_first",
        [payloads(1), payloads(1)],
        (first, even_came, rest),
        HALVES * pay_rows * LANES,
    )
    tied = after((even_next, odd_next, {k: blocks[k] for k in near}))
    even_next, odd_next = tied[:2]
    blocks.update(tied[2])
    odd_came = lax.ppermute(odd_next, "region", odd)
    even_came = lax.ppermute(even_next, "region", even)
    fetch(far)
    for hop in range(2, layers - 1):
        even_next, odd_next = joined(hop, False, odd_came), joined(hop, True, even_came)
        if hop == 2:
            tied = after((even_next, odd_next, {k: blocks[k] for k in far}))
            even_next, odd_next = tied[:2]
            blocks.update(tied[2])
        even_came = lax.ppermute(even_next, "region", even)
        odd_came = lax.ppermute(odd_next, "region", odd)

    cand_count = requests.shape[1] * block_rows
    feat_grad = call(
        grad_kernel,
        "feat_grad",
        jax.ShapeDtypeStruct(features.shape, bf16),
        (requests, owners, features, *[blocks[k] for k in range(group_count)]),
        4 * crop_count * cand_count * feat_width,
        scratch=(
            pltpu.VMEM((cand_count, feat_width), bf16),
            pltpu.SemaphoreType.DMA((requests.shape[1],)),
        ),
        smem=2,
        any_from=3,
    )

    new_memory = call(
        part(update_kernel, layers),
        "update",
        jax.ShapeDtypeStruct(memory.shape, bf16),
        (memory, rest, even_came, odd_came),
        10 * block_rows * feat_width,
        scratch=(pltpu.VMEM((half_rows, feat_width), jnp.float32),),
    )
    return (feat_grad, new_memory)


def solution(mesh):
    placed = (
        P(("region", "group"), None),
        P(("region", "group"), None),
        P(("region", "group"), None),
        P("region", None),
        P(("region", "group"), None),
    )
    return jax.shard_map(
        on_device,
        mesh=mesh,
        in_specs=placed,
        out_specs=(P(("region", "group"), None), P(("region", "group"), None)),
        check_vma=False,
    )
```

profile of v0, /device:TPU:10, one launch (start us, length us, event | category | flops | bytes accessed | tf_op | source)
XLA Modules:
  0.0 56.2 jit_solution(13292805916746998247)
XLA Ops:
  0.6 0.0 copy-start
  0.6 0.0 copy-start.2
  0.6 4.7 %away.1 = (bf16[1,2,1040,128]{3,2,1,0:T(8,128)(2,1)}, bf16[3,2,1040,128]{3,2,1,0:T(8,128)(2,1)}) custom-call(s32[1,384]{1,0:T(1,128)} %labels_ref.3, bf16[384,2048]{1,0:T(8,128)(2,1)} %features_ref.5), custom_call_target="tpu_custom_call" | custom-call | flops 805306368 | bytes 3703552 | tf_op jit(solution)/shard_map/away/pallas_call | solution.py:258
  5.3 0.0 copy-start.5
  5.3 0.0 copy-start.1
  5.3 0.1 collective-permute-start
  5.4 2.1 %collective-permute-done.came_ref = bf16[1,2,1040,128]{3,2,1,0:T(8,128)(2,1)S(1)} collective-permute-done((bf16[1,2,1040,128]{3,2,1,0:T(8,128)(2,1)}, bf16[1,2,1040,128]{3,2,1,0:T(8,128)(2,1)S(1)}, u32[]{:S(2)}, u32[]{:S(2)}) %collective-permute-start) | collective-permute-done | bytes 532512 | tf_op jit(solution)/shard_map/ppermute | solution.py:294
  7.5 0.0 copy-done
  7.5 0.0 copy-done.2
  7.5 0.4 chip_first.1.first_ref
  8.0 0.0 copy-done.5
  8.0 0.2 collective-permute-start.2
  8.2 0.5 collective-permute-start.1
  8.7 0.0 copy-done.1
  8.7 0.1 collective-permute-start.3
  8.8 1.9 %collective-permute-start.4 = (bf16[128,2048]{1,0:T(8,128)(2,1)S(1)}, bf16[128,2048]{1,0:T(8,128)(2,1)S(1)}, u32[]{:S(2)}, u32[]{:S(2)}) collective-permute-start(bf16[128,2048]{1,0:T(8,128)(2,1)S(1)} %copy-done.1), channel_id=1, source_target_pairs={{0,2},{1,3},{2,0},{3,1},{4,6},{5,7},{6,4},{7,5},{8,10},{9,11},{10,... | collective-permute-start | bytes 1572872 | tf_op jit(solution)/shard_map/ppermute | solution.py:318
  10.7 0.8 %collective-permute-done.2.came_ref = bf16[3,2,1040,128]{3,2,1,0:T(8,128)(2,1)S(1)} collective-permute-done((bf16[3,2,1040,128]{3,2,1,0:T(8,128)(2,1)S(1)}, bf16[3,2,1040,128]{3,2,1,0:T(8,128)(2,1)S(1)}, u32[]{:S(2)}, u32[]{:S(2)}) %collective-permute-start.2) | collective-permute-done | bytes 1597472 | tf_op jit(solution)/shard_map/ppermute | solution.py:307
  11.5 1.4 %chip_rest.1.rest_ref = bf16[3,2,1040,128]{3,2,1,0:T(8,128)(2,1)S(1)} custom-call(s32[1,384]{1,0:T(1,128)S(1)} %copy-done.2, bf16[384,2048]{1,0:T(8,128)(2,1)S(1)} %copy-done, bf16[3,2,1040,128]{3,2,1,0:T(8,128)(2,1)S(1)} %collective-permute-done.2.came_ref), custom_call_target="tpu_custom_call" | custom-call | flops 603979776 | bytes 4768512 | tf_op jit(solution)/shard_map/chip_rest/pallas_call | solution.py:258
  12.9 9.7 %collective-permute-done.1.came_ref = bf16[1,2,1040,128]{3,2,1,0:T(8,128)(2,1)S(1)} collective-permute-done((bf16[1,2,1040,128]{3,2,1,0:T(8,128)(2,1)S(1)}, bf16[1,2,1040,128]{3,2,1,0:T(8,128)(2,1)S(1)}, u32[]{:S(2)}, u32[]{:S(2)}) %collective-permute-start.1) | collective-permute-done | bytes 532512 | tf_op jit(solution)/shard_map/ppermute | solution.py:337
  22.6 0.2 join_first.1
  22.8 0.0 collective-permute-done.3.rest_1_
  22.8 0.0 collective-permute-done.4.rest_2_
  22.8 1.7 %collective-permute-start.6 = (bf16[1,2,1040,128]{3,2,1,0:T(8,128)(2,1)S(1)}, bf16[1,2,1040,128]{3,2,1,0:T(8,128)(2,1)S(1)}, u32[]{:S(2)}, u32[]{:S(2)}) collective-permute-start(bf16[1,2,1040,128]{3,2,1,0:T(8,128)(2,1)S(1)} %get-tuple-element.26), channel_id=1, source_target_pairs={{0,8},{4,12},{8,0},{12,4},{16,24},{20,28},{24,16},{28,20},{1,9},{5... | collective-permute-start | bytes 1597448 | tf_op jit(solution)/shard_map/ppermute | solution.py:350
  24.4 3.5 %collective-permute-start.5 = (bf16[1,2,1040,128]{3,2,1,0:T(8,128)(2,1)S(1)}, bf16[1,2,1040,128]{3,2,1,0:T(8,128)(2,1)S(1)}, u32[]{:S(2)}, u32[]{:S(2)}) collective-permute-start(bf16[1,2,1040,128]{3,2,1,0:T(8,128)(2,1)S(1)} %get-tuple-element.25), channel_id=1, source_target_pairs={{8,16},{12,20},{16,8},{20,12},{9,17},{13,21},{17,9},{21,13},{10,18... | collective-permute-start | bytes 1597448 | tf_op jit(solution)/shard_map/ppermute | solution.py:349
  27.9 1.6 %collective-permute-start.7 = (bf16[128,2048]{1,0:T(8,128)(2,1)S(1)}, bf16[128,2048]{1,0:T(8,128)(2,1)S(1)}, u32[]{:S(2)}, u32[]{:S(2)}) collective-permute-start(bf16[128,2048]{1,0:T(8,128)(2,1)S(1)} %collective-permute-done.3.rest_1_), channel_id=1, source_target_pairs={{0,2},{1,3},{2,0},{3,1},{4,6},{5,7},{6,4},{7,5},{8,10},{9,11},{10,... | collective-permute-start | bytes 1572872 | tf_op jit(solution)/shard_map/ppermute | solution.py:318
  29.5 6.9 %collective-permute-done.6.came_ref = bf16[1,2,1040,128]{3,2,1,0:T(8,128)(2,1)S(1)} collective-permute-done((bf16[1,2,1040,128]{3,2,1,0:T(8,128)(2,1)S(1)}, bf16[1,2,1040,128]{3,2,1,0:T(8,128)(2,1)S(1)}, u32[]{:S(2)}, u32[]{:S(2)}) %collective-permute-start.6) | collective-permute-done | bytes 532512 | tf_op jit(solution)/shard_map/ppermute | solution.py:350
  36.4 0.1 join_odd.1
  36.5 0.0 copy-start.3
  36.5 0.0 copy-start.4
  36.6 2.9 %collective-permute-done.5.came_ref = bf16[1,2,1040,128]{3,2,1,0:T(8,128)(2,1)S(1)} collective-permute-done((bf16[1,2,1040,128]{3,2,1,0:T(8,128)(2,1)S(1)}, bf16[1,2,1040,128]{3,2,1,0:T(8,128)(2,1)S(1)}, u32[]{:S(2)}, u32[]{:S(2)}) %collective-permute-start.5) | collective-permute-done | bytes 532512 | tf_op jit(solution)/shard_map/ppermute | solution.py:349
  39.4 0.1 join_even.1
  39.6 1.2 %collective-permute-done.7.rest_3_ = bf16[128,2048]{1,0:T(8,128)(2,1)S(1)} collective-permute-done((bf16[128,2048]{1,0:T(8,128)(2,1)S(1)}, bf16[128,2048]{1,0:T(8,128)(2,1)S(1)}, u32[]{:S(2)}, u32[]{:S(2)}) %collective-permute-start.7) | collective-permute-done | bytes 524320 | tf_op jit(solution)/shard_map/ppermute | solution.py:318
  40.8 0.0 collective-permute-start.8
  40.8 2.5 %collective-permute-start.9 = (bf16[1,2,1040,128]{3,2,1,0:T(8,128)(2,1)S(1)}, bf16[1,2,1040,128]{3,2,1,0:T(8,128)(2,1)S(1)}, u32[]{:S(2)}, u32[]{:S(2)}) collective-permute-start(bf16[1,2,1040,128]{3,2,1,0:T(8,128)(2,1)S(1)} %join_odd.1), channel_id=1, source_target_pairs={{8,16},{12,20},{16,8},{20,12},{9,17},{13,21},{17,9},{21,13},{10,18... | collective-permute-start | bytes 1597448 | tf_op jit(solution)/shard_map/ppermute | solution.py:359
  43.3 0.0 copy-done.3
  43.3 0.0 copy-done.4
  43.3 3.9 %feat_grad.1 = bf16[384,2048]{1,0:T(8,128)(2,1)} custom-call(s32[1,2]{1,0:T(1,128)S(1)} %copy-done.3, s32[1,4]{1,0:T(1,128)S(1)} %copy-done.4, bf16[384,2048]{1,0:T(8,128)(2,1)S(1)} %copy-done, bf16[128,2048]{1,0:T(8,128)(2,1)S(1)} %copy-done.1, bf16[128,2048]{1,0:T(8,128)(2,1)S(1)} %collective-permute-done.3.rest_1_, ...), custom_call_target="tpu_custom_call" | custom-call | flops 805306368 | bytes 5242892 | tf_op jit(solution)/shard_map/feat_grad/pallas_call | solution.py:258
  47.2 5.7 %collective-permute-done.8.rest_0_ = bf16[1,2,1040,128]{3,2,1,0:T(8,128)(2,1)S(1)} collective-permute-done((bf16[1,2,1040,128]{3,2,1,0:T(8,128)(2,1)S(1)}, bf16[1,2,1040,128]{3,2,1,0:T(8,128)(2,1)S(1)}, u32[]{:S(2)}, u32[]{:S(2)}) %collective-permute-start.8) | collective-permute-done | bytes 532512 | tf_op jit(solution)/shard_map/ppermute | solution.py:358
  52.9 1.9 %collective-permute-done.9.rest_1_ = bf16[1,2,1040,128]{3,2,1,0:T(8,128)(2,1)S(1)} collective-permute-done((bf16[1,2,1040,128]{3,2,1,0:T(8,128)(2,1)S(1)}, bf16[1,2,1040,128]{3,2,1,0:T(8,128)(2,1)S(1)}, u32[]{:S(2)}, u32[]{:S(2)}) %collective-permute-start.9) | collective-permute-done | bytes 532512 | tf_op jit(solution)/shard_map/ppermute | solution.py:359
  54.8 1.4 %update.1 = bf16[128,2048]{1,0:T(8,128)(2,1)} custom-call(bf16[128,2048]{1,0:T(8,128)(2,1)S(1)} %copy-done.1, bf16[3,2,1040,128]{3,2,1,0:T(8,128)(2,1)S(1)} %chip_rest.1.rest_ref, bf16[1,2,1040,128]{3,2,1,0:T(8,128)(2,1)S(1)} %collective-permute-done.8.rest_0_, bf16[1,2,1040,128]{3,2,1,0:T(8,128)(2,1)S(1)} %collective-permute-done.9.rest_1_), custom_call_target="tpu_custom_call" | custom-call | flops 2621440 | bytes 3710976 | tf_op jit(solution)/shard_map/update/pallas_call | solution.py:258
Async XLA Ops:
  0.6 6.9 %copy-start = (bf16[384,2048]{1,0:T(8,128)(2,1)S(1)}, bf16[384,2048]{1,0:T(8,128)(2,1)}, u32[]{:S(2)}) copy-start(bf16[384,2048]{1,0:T(8,128)(2,1)} %features_ref.5) | copy-start | bytes 4718596
  0.6 6.9 %copy-start.2 = (s32[1,384]{1,0:T(1,128)S(1)}, s32[1,384]{1,0:T(1,128)}, u32[]{:S(2)}) copy-start(s32[1,384]{1,0:T(1,128)} %labels_ref.3) | copy-start | bytes 4612
  5.3 2.7 %copy-start.5 = (bf16[3,2,1040,128]{3,2,1,0:T(8,128)(2,1)S(1)}, bf16[3,2,1040,128]{3,2,1,0:T(8,128)(2,1)}, u32[]{:S(2)}) copy-start(bf16[3,2,1040,128]{3,2,1,0:T(8,128)(2,1)} %get-tuple-element.20) | copy-start | bytes 4792324
  5.3 3.3 %copy-start.1 = (bf16[128,2048]{1,0:T(8,128)(2,1)S(1)}, bf16[128,2048]{1,0:T(8,128)(2,1)}, u32[]{:S(2)}) copy-start(bf16[128,2048]{1,0:T(8,128)(2,1)} %memory_ref.1) | copy-start | bytes 1572868
  5.3 2.2 %collective-permute-start = (bf16[1,2,1040,128]{3,2,1,0:T(8,128)(2,1)}, bf16[1,2,1040,128]{3,2,1,0:T(8,128)(2,1)S(1)}, u32[]{:S(2)}, u32[]{:S(2)}) collective-permute-start(bf16[1,2,1040,128]{3,2,1,0:T(8,128)(2,1)} %get-tuple-element.16), channel_id=1, source_target_pairs={{0,4},{4,0},{8,12},{12,8},{16,20},{20,16},{24,28},{28,24},{1,5},{5... | collective-permute-start | bytes 1597448 | tf_op jit(solution)/shard_map/ppermute | solution.py:294
  8.0 3.5 %collective-permute-start.2 = (bf16[3,2,1040,128]{3,2,1,0:T(8,128)(2,1)S(1)}, bf16[3,2,1040,128]{3,2,1,0:T(8,128)(2,1)S(1)}, u32[]{:S(2)}, u32[]{:S(2)}) collective-permute-start(bf16[3,2,1040,128]{3,2,1,0:T(8,128)(2,1)S(1)} %copy-done.5), channel_id=1, source_target_pairs={{0,4},{4,0},{8,12},{12,8},{16,20},{20,16},{24,28},{28,24},{1,5},{5... | collective-permute-start | bytes 4792328 | tf_op jit(solution)/shard_map/ppermute | solution.py:307
  8.2 14.4 %collective-permute-start.1 = (bf16[1,2,1040,128]{3,2,1,0:T(8,128)(2,1)S(1)}, bf16[1,2,1040,128]{3,2,1,0:T(8,128)(2,1)S(1)}, u32[]{:S(2)}, u32[]{:S(2)}) collective-permute-start(bf16[1,2,1040,128]{3,2,1,0:T(8,128)(2,1)S(1)} %chip_first.1.first_ref), channel_id=1, source_target_pairs={{0,8},{4,12},{8,0},{12,4},{16,24},{20,28},{24,16},{28,20},{1,9},{5... | collective-permute-start | bytes 1597448 | tf_op jit(solution)/shard_map/ppermute | solution.py:337
  8.7 14.1 %collective-permute-start.3 = (bf16[128,2048]{1,0:T(8,128)(2,1)S(1)}, bf16[128,2048]{1,0:T(8,128)(2,1)S(1)}, u32[]{:S(2)}, u32[]{:S(2)}) collective-permute-start(bf16[128,2048]{1,0:T(8,128)(2,1)S(1)} %copy-done.1), channel_id=1, source_target_pairs={{0,1},{1,0},{2,3},{3,2},{4,5},{5,4},{6,7},{7,6},{8,9},{9,8},{10,11... | collective-permute-start | bytes 1572872 | tf_op jit(solution)/shard_map/ppermute | solution.py:318
  8.8 14.0 %collective-permute-start.4 = (bf16[128,2048]{1,0:T(8,128)(2,1)S(1)}, bf16[128,2048]{1,0:T(8,128)(2,1)S(1)}, u32[]{:S(2)}, u32[]{:S(2)}) collective-permute-start(bf16[128,2048]{1,0:T(8,128)(2,1)S(1)} %copy-done.1), channel_id=1, source_target_pairs={{0,2},{1,3},{2,0},{3,1},{4,6},{5,7},{6,4},{7,5},{8,10},{9,11},{10,... | collective-permute-start | bytes 1572872 | tf_op jit(solution)/shard_map/ppermute | solution.py:318
  22.8 13.6 %collective-permute-start.6 = (bf16[1,2,1040,128]{3,2,1,0:T(8,128)(2,1)S(1)}, bf16[1,2,1040,128]{3,2,1,0:T(8,128)(2,1)S(1)}, u32[]{:S(2)}, u32[]{:S(2)}) collective-permute-start(bf16[1,2,1040,128]{3,2,1,0:T(8,128)(2,1)S(1)} %get-tuple-element.26), channel_id=1, source_target_pairs={{0,8},{4,12},{8,0},{12,4},{16,24},{20,28},{24,16},{28,20},{1,9},{5... | collective-permute-start | bytes 1597448 | tf_op jit(solution)/shard_map/ppermute | solution.py:350
  24.4 15.0 %collective-permute-start.5 = (bf16[1,2,1040,128]{3,2,1,0:T(8,128)(2,1)S(1)}, bf16[1,2,1040,128]{3,2,1,0:T(8,128)(2,1)S(1)}, u32[]{:S(2)}, u32[]{:S(2)}) collective-permute-start(bf16[1,2,1040,128]{3,2,1,0:T(8,128)(2,1)S(1)} %get-tuple-element.25), channel_id=1, source_target_pairs={{8,16},{12,20},{16,8},{20,12},{9,17},{13,21},{17,9},{21,13},{10,18... | collective-permute-start | bytes 1597448 | tf_op jit(solution)/shard_map/ppermute | solution.py:349
  27.9 12.9 %collective-permute-start.7 = (bf16[128,2048]{1,0:T(8,128)(2,1)S(1)}, bf16[128,2048]{1,0:T(8,128)(2,1)S(1)}, u32[]{:S(2)}, u32[]{:S(2)}) collective-permute-start(bf16[128,2048]{1,0:T(8,128)(2,1)S(1)} %collective-permute-done.3.rest_1_), channel_id=1, source_target_pairs={{0,2},{1,3},{2,0},{3,1},{4,6},{5,7},{6,4},{7,5},{8,10},{9,11},{10,... | collective-permute-start | bytes 1572872 | tf_op jit(solution)/shard_map/ppermute | solution.py:318
  36.5 6.8 %copy-start.3 = (s32[1,2]{1,0:T(1,128)S(1)}, s32[1,2]{1,0:T(1,128)}, u32[]{:S(2)}) copy-start(s32[1,2]{1,0:T(1,128)} %requests_ref.1) | copy-start | bytes 28
  36.5 6.8 %copy-start.4 = (s32[1,4]{1,0:T(1,128)S(1)}, s32[1,4]{1,0:T(1,128)}, u32[]{:S(2)}) copy-start(s32[1,4]{1,0:T(1,128)} %owners_ref.1) | copy-start | bytes 52
  40.8 12.1 %collective-permute-start.8 = (bf16[1,2,1040,128]{3,2,1,0:T(8,128)(2,1)S(1)}, bf16[1,2,1040,128]{3,2,1,0:T(8,128)(2,1)S(1)}, u32[]{:S(2)}, u32[]{:S(2)}) collective-permute-start(bf16[1,2,1040,128]{3,2,1,0:T(8,128)(2,1)S(1)} %join_even.1), channel_id=1, source_target_pairs={{0,8},{4,12},{8,0},{12,4},{16,24},{20,28},{24,16},{28,20},{1,9},{5... | collective-permute-start | bytes 1597448 | tf_op jit(solution)/shard_map/ppermute | solution.py:358
  40.8 14.0 %collective-permute-start.9 = (bf16[1,2,1040,128]{3,2,1,0:T(8,128)(2,1)S(1)}, bf16[1,2,1040,128]{3,2,1,0:T(8,128)(2,1)S(1)}, u32[]{:S(2)}, u32[]{:S(2)}) collective-permute-start(bf16[1,2,1040,128]{3,2,1,0:T(8,128)(2,1)S(1)} %join_odd.1), channel_id=1, source_target_pairs={{8,16},{12,20},{16,8},{20,12},{9,17},{13,21},{17,9},{21,13},{10,18... | collective-permute-start | bytes 1597448 | tf_op jit(solution)/shard_map/ppermute | solution.py:359
where the time goes:
time: 56.3 us; the launch traced here: 56.2 us
  waiting for transfers between devices  31.2 us (55%)
  Pallas kernels  12.2 us (22%)
  starting transfers between devices  12 us (21%)
  between operations  0.79 us (1%)
    ppermute x2, waiting for transfers between devices, on_device(): even_came = lax.ppermute(even_next, 'region', even)  12.6 us
    pallas_call x8, Pallas kernels, call(): pl.pallas_call(kernel, out_shape=out_shape, in_specs=specs, out_specs=[VM...  12.2 us
    ppermute x1, waiting for transfers between devices, on_device(): even_came = lax.ppermute(first, 'region', even)  9.69 us
    ppermute x2, starting transfers between devices, on_device(): odd_came = lax.ppermute(odd_next, 'region', odd)  5.96 us
    ppermute x2, waiting for transfers between devices, on_device(): odd_came = lax.ppermute(odd_next, 'region', odd)  4.76 us
    ppermute x3, starting transfers between devices, fetch(): lax.ppermute(blocks[k ^ bit], 'group', [(g, g ^ bit) for g in range(group...  3.64 us
    ppermute x1, waiting for transfers between devices, on_device(): came_first = lax.ppermute(away_first, 'region', swap)  2.12 us
    ppermute x2, starting transfers between devices, on_device(): even_came = lax.ppermute(even_next, 'region', even)  1.66 us
  transfers between devices with their start and end apart: 10, of which 8 were waited for; matrix products, arithmetic and copies ran while one was open for 0% of the time, Pallas kernels for 10%

commit v1 on v0

--- a/solution.py
+++ b/solution.py
@@ -85,8 +85,8 @@
     return lambda h, first, rows: ref[(*at, h, pl.ds(first, rows), slice(None))]
 
 
-def away_kernel(
-    layers, block_rows, labels_hbm, features_hbm, first_ref, rest_ref, labels_ref, features_ref, sems
+def away_first_kernel(
+    layers, block_rows, labels_hbm, features_hbm, out_ref, labels_ref, features_ref, sems
 ):
     columns = WIDE * LANES
     copies = [pltpu.make_async_copy(labels_hbm, labels_ref, sems.at[0])]
@@ -105,32 +105,58 @@
         features_ref,
         block_rows,
         None,
-        block_of(first_ref, 0),
+        block_of(out_ref, 0),
         lambda i: copies[i + 1].wait(),
     )
+
+
+def away_rest_kernel(layers, block_rows, labels_ref, features_ref, out_ref):
+    core = 1 - lax.axis_index("region") % CORES
 
     def one(p, carry):
         base = base_at(p + 1, layers, core, block_rows)
-        write_sums(base, labels_ref, features_ref, block_rows, None, block_of(rest_ref, p))
+        write_sums(base, labels_ref, features_ref, block_rows, None, block_of(out_ref, p))
         return carry
 
     lax.fori_loop(0, layers - 1, one, 0)
 
 
-def chip_kernel(layers, block_rows, start, labels_ref, features_ref, came_ref, out_ref):
+def chip_first_kernel(layers, block_rows, labels_ref, features_ref, came_ref, *outs):
+    base = base_at(0, layers, lax.axis_index("region") % CORES, block_rows)
+
+    def store(h, first, part):
+        outs[h][pl.ds(first, part.shape[0]), :] = part
+
+    write_sums(base, labels_ref, features_ref, block_rows, came_at(came_ref, 0), store)
+
+
+def chip_rest_kernel(layers, block_rows, labels_ref, features_ref, came_ref, second_ref, out_ref):
     core = lax.axis_index("region") % CORES
 
     def one(p, carry):
-        base = base_at(p + start, layers, core, block_rows)
+        base = base_at(p + 1, layers, core, block_rows)
         write_sums(
             base, labels_ref, features_ref, block_rows, came_at(came_ref, p), block_of(out_ref, p)
         )
         return carry
 
-    lax.fori_loop(0, out_ref.shape[0], one, 0)
-
-
-def join_kernel(layers, hop, odd, first_ref, rest_ref, came_ref, out_ref):
+    lax.fori_loop(0, layers - 1, one, 0)
+    second_ref[0] = out_ref[0]
+
+
+def join_half_kernel(mine_ref, came_ref, out_ref):
+    out_ref[...] = (
+        mine_ref[...].astype(jnp.float32) + came_ref[...].astype(jnp.float32)
+    ).astype(jnp.bfloat16)
+
+
+def join_kernel(layers, hop, odd, *refs):
+    first_refs, rest_ref, came_refs, out_ref = (
+        refs[:HALVES],
+        refs[HALVES],
+        refs[HALVES + 1 : -1],
+        refs[-1],
+    )
     layer = lax.axis_index("region") // CORES
     up = (layer % 2 == 1) if odd else (layer % 2 == 0)
     target = jnp.where(up, layers - 1 - hop + layer, hop - (layers - 1 - layer))
@@ -138,24 +164,19 @@
     place = jnp.where(layer < layers // 2, layers - 1 - target, target)
 
     def add(mine):
-        out_ref[0] = (
-            mine.astype(jnp.float32) + came_ref[0].astype(jnp.float32)
-        ).astype(jnp.bfloat16)
+        for h in range(HALVES):
+            came = came_refs[h][...] if len(came_refs) > 1 else came_refs[0][0, h]
+            out_ref[0, h] = (mine(h).astype(jnp.float32) + came.astype(jnp.float32)).astype(
+                jnp.bfloat16
+            )
 
     @pl.when(place == 0)
     def _():
-        add(first_ref[0])
+        add(lambda h: first_refs[h][...])
 
     @pl.when(place > 0)
     def _():
-        add(rest_ref[jnp.maximum(place - 1, 0)])
-
-
-def join_first_kernel(first_ref, came_ref, rest_ref, out_ref, second_ref):
-    out_ref[...] = (
-        first_ref[...].astype(jnp.float32) + came_ref[...].astype(jnp.float32)
-    ).astype(jnp.bfloat16)
-    second_ref[0] = rest_ref[0]
+        add(lambda h: rest_ref[jnp.maximum(place - 1, 0), h])
 
 
 def update_kernel(layers, memory_ref, rest_ref, *rest):
@@ -277,12 +298,12 @@
     def payloads(count):
         return jax.ShapeDtypeStruct((count, HALVES, pay_rows, LANES), bf16)
 
-    away_first, away_rest = call(
-        part(away_kernel, layers, block_rows),
-        "away",
-        [payloads(1), payloads(layers - 1)],
+    away_first = call(
+        part(away_first_kernel, layers, block_rows),
+        "away_first",
+        payloads(1),
         (labels, features),
-        block_flops * layers,
+        block_flops,
         scratch=(
             pltpu.VMEM(labels.shape, labels.dtype),
             pltpu.VMEM(features.shape, bf16),
@@ -292,32 +313,34 @@
         params=pltpu.CompilerParams(vmem_limit_bytes=60 * 2**20),
     )
     came_first = lax.ppermute(away_first, "region", swap)
+    later_labels, away_first = after((labels, away_first))
+    away_rest = call(
+        part(away_rest_kernel, layers, block_rows),
+        "away_rest",
+        payloads(layers - 1),
+        (later_labels, features),
+        block_flops * (layers - 1),
+    )
     first = call(
-        part(chip_kernel, layers, block_rows, 0),
+        part(chip_first_kernel, layers, block_rows),
         "chip_first",
-        payloads(1),
+        [jax.ShapeDtypeStruct((pay_rows, LANES), bf16)] * HALVES,
         (labels, features, came_first),
         block_flops,
     )
     first, away_rest, sent_memory = after((first, away_rest, memory))
-    rest = call(
-        part(chip_kernel, layers, block_rows, 1),
+    second, rest = call(
+        part(chip_rest_kernel, layers, block_rows),
         "chip_rest",
-        payloads(layers - 1),
+        [payloads(1), payloads(layers - 1)],
         (labels, features, lax.ppermute(away_rest, "region", swap)),
         block_flops * (layers - 1),
     )
 
-    blocks = {0: sent_memory}
-    near = [k for k in range(1, group_count) if k & (k - 1) == 0]
-    far = [k for k in range(1, group_count) if k & (k - 1)]
-
-    def fetch(ks):
-        for k in ks:
-            bit = 1 << (k.bit_length() - 1)
-            blocks[k] = lax.ppermute(
-                blocks[k ^ bit], "group", [(g, g ^ bit) for g in range(group_count)]
-            )
+    blocks = {0: memory}
+
+    def fetch(k, block):
+        blocks[k] = lax.ppermute(block, "group", [(g, g ^ k) for g in range(group_count)])
 
     even = [(r, ((r // CORES) ^ 1) * CORES + r % CORES) for r in range(region_count)]
     odd = []
@@ -330,33 +353,33 @@
             part(join_kernel, layers, hop, is_odd),
             "join_odd" if is_odd else "join_even",
             payloads(1),
-            (first, rest, came),
+            (*first, rest, *came),
             HALVES * pay_rows * LANES,
         )
 
-    even_came = lax.ppermute(first, "region", even)
-    fetch(near)
-    odd_next, even_next = call(
-        join_first_kernel,
-        "join_first",
-        [payloads(1), payloads(1)],
-        (first, even_came, rest),
-        HALVES * pay_rows * LANES,
-    )
-    tied = after((even_next, odd_next, {k: blocks[k] for k in near}))
-    even_next, odd_next = tied[:2]
-    blocks.update(tied[2])
-    odd_came = lax.ppermute(odd_next, "region", odd)
-    even_came = lax.ppermute(even_next, "region", even)
-    fetch(far)
+    even_came = [lax.ppermute(x, "region", even) for x in first]
+    for k in range(1, group_count):
+        if k & (k - 1) == 0:
+            fetch(k, sent_memory)
+    odd_came = []
+    for h in range(HALVES):
+        leaves = call(
+            join_half_kernel,
+            "join_half",
+            jax.ShapeDtypeStruct((pay_rows, LANES), bf16),
+            (first[h], even_came[h]),
+            pay_rows * LANES,
+        )
+        odd_came.append(lax.ppermute(leaves, "region", odd))
+    later_memory, even_came[-1] = after((sent_memory, even_came[-1]))
+    for k in range(1, group_count):
+        if k & (k - 1):
+            fetch(k, later_memory)
+    even_came = [lax.ppermute(second, "region", even)]
     for hop in range(2, layers - 1):
         even_next, odd_next = joined(hop, False, odd_came), joined(hop, True, even_came)
-        if hop == 2:
-            tied = after((even_next, odd_next, {k: blocks[k] for k in far}))
-            even_next, odd_next = tied[:2]
-            blocks.update(tied[2])
-        even_came = lax.ppermute(even_next, "region", even)
-        odd_came = lax.ppermute(odd_next, "region", odd)
+        even_came = [lax.ppermute(even_next, "region", even)]
+        odd_came = [lax.ppermute(odd_next, "region", odd)]
 
     cand_count = requests.shape[1] * block_rows
     feat_grad = call(
@@ -377,7 +400,7 @@
         part(update_kernel, layers),
         "update",
         jax.ShapeDtypeStruct(memory.shape, bf16),
-        (memory, rest, even_came, odd_came),
+        (memory, rest, *even_came, *odd_came),
         10 * block_rows * feat_width,
         scratch=(pltpu.VMEM((half_rows, feat_width), jnp.float32),),
     )

time: 56.3 us -> 55.5 us (0.986)
  waiting for transfers between devices: 31.2 us -> 25.6 us
  starting transfers between devices: 12 us -> 16.9 us
    ppermute x8 -> x10, starting transfers between devices: 11.7 us -> 16.6 us  [the longest x2 6.96 us: on_device(): odd_came.append(lax.ppermute(leaves, 'region', odd))]
    ppermute x8 -> x10, waiting for transfers between devices: 28.3 us -> 23.6 us  [the longest x3 13.4 us: fetch(): lax.ppermute(block, 'group', [(g, g ^ k) for g in range(group_count)])]
    ppermute x1, waiting for transfers between devices: 2.12 us -> 0.72 us  [on_device(): came_first = lax.ppermute(away_first, 'region', swap)]
    pallas_call x8 -> x10, Pallas kernels: 12.2 us -> 11.8 us  [call(): pl.pallas_call(kernel, out_shape=out_shape, in_specs=specs, out_specs=[VM...]
  transfers between devices with their start and end apart: 10 -> 12, of which waited for: 8 -> 9; matrix products, arithmetic and copies ran while one was open for 0% -> 0% of each run, Pallas kernels for 10% -> 13%
where the time goes in v1:
time: 55.5 us; the launch traced here: 55.1 us
  waiting for transfers between devices  25.6 us (46%)
  starting transfers between devices  16.9 us (30%)
  Pallas kernels  11.8 us (21%)
  between operations  0.81 us (1%)
    ppermute x3, waiting for transfers between devices, fetch(): lax.ppermute(block, 'group', [(g, g ^ k) for g in range(group_count)])  13.4 us
    pallas_call x10, Pallas kernels, call(): pl.pallas_call(kernel, out_shape=out_shape, in_specs=specs, out_specs=[VM...  11.8 us
    ppermute x2, starting transfers between devices, on_device(): odd_came.append(lax.ppermute(leaves, 'region', odd))  6.96 us
    ppermute x2, waiting for transfers between devices, on_device(): even_came = [lax.ppermute(x, 'region', even) for x in first]  6.14 us
    ppermute x3, starting transfers between devices, fetch(): lax.ppermute(block, 'group', [(g, g ^ k) for g in range(group_count)])  3.55 us
    ppermute x1, starting transfers between devices, on_device(): odd_came = [lax.ppermute(odd_next, 'region', odd)]  3.48 us
    ppermute x2, waiting for transfers between devices, on_device(): odd_came.append(lax.ppermute(leaves, 'region', odd))  2.15 us
    ppermute x2, starting transfers between devices, on_device(): even_came = [lax.ppermute(x, 'region', even) for x in first]  2.05 us
  transfers between devices with their start and end apart: 12, of which 9 were waited for; matrix products, arithmetic and copies ran while one was open for 0% of the time, Pallas kernels for 13%

profile of v1, /device:TPU:10, one launch (start us, length us, event | category | flops | bytes accessed | tf_op | source)
XLA Modules:
  0.0 55.1 jit_solution(1927178400067660953)
XLA Ops:
  0.6 0.0 copy-start
  0.6 0.0 copy-start.2
  0.6 2.9 %away_first.1 = bf16[1,2,1040,128]{3,2,1,0:T(8,128)(2,1)} custom-call(s32[1,384]{1,0:T(1,128)} %labels_ref.4, bf16[384,2048]{1,0:T(8,128)(2,1)} %features_ref.7), custom_call_target="tpu_custom_call" | custom-call | flops 201326592 | bytes 2106112 | tf_op jit(solution)/shard_map/away_first/pallas_call | solution.py:279
  3.6 0.1 collective-permute-start
  3.7 0.0 copy-done
  3.7 0.0 copy-done.2
  3.7 1.4 %away_rest.1 = bf16[3,2,1040,128]{3,2,1,0:T(8,128)(2,1)S(1)} custom-call(s32[1,384]{1,0:T(1,128)S(1)} %copy-done.2, bf16[384,2048]{1,0:T(8,128)(2,1)S(1)} %copy-done), custom_call_target="tpu_custom_call" | custom-call | flops 603979776 | bytes 3171072 | tf_op jit(solution)/shard_map/away_rest/pallas_call | solution.py:279
  5.1 0.7 %collective-permute-done.came_ref = bf16[1,2,1040,128]{3,2,1,0:T(8,128)(2,1)S(1)} collective-permute-done((bf16[1,2,1040,128]{3,2,1,0:T(8,128)(2,1)}, bf16[1,2,1040,128]{3,2,1,0:T(8,128)(2,1)S(1)}, u32[]{:S(2)}, u32[]{:S(2)}) %collective-permute-start) | collective-permute-done | bytes 532512 | tf_op jit(solution)/shard_map/ppermute | solution.py:315
  5.8 0.5 chip_first.1
  6.2 0.0 copy-start.1
  6.3 0.2 collective-permute-start.5
  6.4 0.5 collective-permute-start.3
  6.9 1.6 %collective-permute-start.6 = (bf16[1040,128]{1,0:T(8,128)(2,1)S(1)}, bf16[1040,128]{1,0:T(8,128)(2,1)S(1)}, u32[]{:S(2)}, u32[]{:S(2)}) collective-permute-start(bf16[1040,128]{1,0:T(8,128)(2,1)S(1)} %get-tuple-element.20.mine_ref.refs_0_), channel_id=1, source_target_pairs={{0,8},{4,12},{8,0},{12,4},{16,24},{20,28},{24,16},{28,20},{1,9},{5... | collective-permute-start | bytes 798728 | tf_op jit(solution)/shard_map/ppermute | solution.py:360
  8.5 1.3 %collective-permute-done.5.came_ref = bf16[3,2,1040,128]{3,2,1,0:T(8,128)(2,1)S(1)} collective-permute-done((bf16[3,2,1040,128]{3,2,1,0:T(8,128)(2,1)S(1)}, bf16[3,2,1040,128]{3,2,1,0:T(8,128)(2,1)S(1)}, u32[]{:S(2)}, u32[]{:S(2)}) %collective-permute-start.5) | collective-permute-done | bytes 1597472 | tf_op jit(solution)/shard_map/ppermute | solution.py:336
  9.8 1.4 %chip_rest.1 = (bf16[1,2,1040,128]{3,2,1,0:T(8,128)(2,1)S(1)}, bf16[3,2,1040,128]{3,2,1,0:T(8,128)(2,1)S(1)}) custom-call(s32[1,384]{1,0:T(1,128)S(1)} %copy-done.2, bf16[384,2048]{1,0:T(8,128)(2,1)S(1)} %copy-done, bf16[3,2,1040,128]{3,2,1,0:T(8,128)(2,1)S(1)} %collective-permute-done.5.came_ref), custom_call_target="tpu_custom_call" | custom-call | flops 603979776 | bytes 5300992 | tf_op jit(solution)/shard_map/chip_rest/pallas_call | solution.py:279
  11.2 0.5 collective-permute-start.10
  11.7 4.0 %collective-permute-done.3.came_ref = bf16[1040,128]{1,0:T(8,128)(2,1)S(1)} collective-permute-done((bf16[1040,128]{1,0:T(8,128)(2,1)S(1)}, bf16[1040,128]{1,0:T(8,128)(2,1)S(1)}, u32[]{:S(2)}, u32[]{:S(2)}) %collective-permute-start.3) | collective-permute-done | bytes 266272 | tf_op jit(solution)/shard_map/ppermute | solution.py:360
  15.7 0.1 join_half.3
  15.7 3.5 %collective-permute-start.8 = (bf16[1040,128]{1,0:T(8,128)(2,1)S(1)}, bf16[1040,128]{1,0:T(8,128)(2,1)S(1)}, u32[]{:S(2)}, u32[]{:S(2)}) collective-permute-start(bf16[1040,128]{1,0:T(8,128)(2,1)S(1)} %join_half.3), channel_id=1, source_target_pairs={{8,16},{12,20},{16,8},{20,12},{9,17},{13,21},{17,9},{21,13},{10,18... | collective-permute-start | bytes 798728 | tf_op jit(solution)/shard_map/ppermute | solution.py:373
  19.2 2.2 %collective-permute-done.6.came_ref = bf16[1040,128]{1,0:T(8,128)(2,1)S(1)} collective-permute-done((bf16[1040,128]{1,0:T(8,128)(2,1)S(1)}, bf16[1040,128]{1,0:T(8,128)(2,1)S(1)}, u32[]{:S(2)}, u32[]{:S(2)}) %collective-permute-start.6) | collective-permute-done | bytes 266272 | tf_op jit(solution)/shard_map/ppermute | solution.py:360
  21.4 0.1 join_half.2
  21.4 3.5 %collective-permute-start.7 = (bf16[1040,128]{1,0:T(8,128)(2,1)S(1)}, bf16[1040,128]{1,0:T(8,128)(2,1)S(1)}, u32[]{:S(2)}, u32[]{:S(2)}) collective-permute-start(bf16[1040,128]{1,0:T(8,128)(2,1)S(1)} %join_half.2), channel_id=1, source_target_pairs={{8,16},{12,20},{16,8},{20,12},{9,17},{13,21},{17,9},{21,13},{10,18... | collective-permute-start | bytes 798728 | tf_op jit(solution)/shard_map/ppermute | solution.py:373
  24.9 0.0 copy-done.1
  24.9 0.6 %collective-permute-start.1 = (bf16[128,2048]{1,0:T(8,128)(2,1)S(1)}, bf16[128,2048]{1,0:T(8,128)(2,1)S(1)}, u32[]{:S(2)}, u32[]{:S(2)}) collective-permute-start(bf16[128,2048]{1,0:T(8,128)(2,1)S(1)} %copy-done.1), channel_id=1, source_target_pairs={{0,1},{1,0},{2,3},{3,2},{4,5},{5,4},{6,7},{7,6},{8,9},{9,8},{10,11... | collective-permute-start | bytes 1572872 | tf_op jit(solution)/shard_map/ppermute | solution.py:343
  25.5 1.5 %collective-permute-start.2 = (bf16[128,2048]{1,0:T(8,128)(2,1)S(1)}, bf16[128,2048]{1,0:T(8,128)(2,1)S(1)}, u32[]{:S(2)}, u32[]{:S(2)}) collective-permute-start(bf16[128,2048]{1,0:T(8,128)(2,1)S(1)} %copy-done.1), channel_id=1, source_target_pairs={{0,2},{1,3},{2,0},{3,1},{4,6},{5,7},{6,4},{7,5},{8,10},{9,11},{10,... | collective-permute-start | bytes 1572872 | tf_op jit(solution)/shard_map/ppermute | solution.py:343
  27.1 0.0 collective-permute-done.8.refs_4_
  27.1 1.4 %collective-permute-start.4 = (bf16[128,2048]{1,0:T(8,128)(2,1)S(1)}, bf16[128,2048]{1,0:T(8,128)(2,1)S(1)}, u32[]{:S(2)}, u32[]{:S(2)}) collective-permute-start(bf16[128,2048]{1,0:T(8,128)(2,1)S(1)} %copy-done.1), channel_id=1, source_target_pairs={{0,3},{1,2},{2,1},{3,0},{4,7},{5,6},{6,5},{7,4},{8,11},{9,10},{10,... | collective-permute-start | bytes 1572872 | tf_op jit(solution)/shard_map/ppermute | solution.py:343
  28.5 2.2 %collective-permute-done.7.refs_3_ = bf16[1040,128]{1,0:T(8,128)(2,1)S(1)} collective-permute-done((bf16[1040,128]{1,0:T(8,128)(2,1)S(1)}, bf16[1040,128]{1,0:T(8,128)(2,1)S(1)}, u32[]{:S(2)}, u32[]{:S(2)}) %collective-permute-start.7) | collective-permute-done | bytes 266272 | tf_op jit(solution)/shard_map/ppermute | solution.py:373
  30.7 0.1 join_even.1
  30.8 0.0 copy-start.3
  30.8 0.0 copy-start.4
  30.8 0.1 collective-permute-start.9
  30.9 1.9 %collective-permute-done.10.refs_3_ = bf16[1,2,1040,128]{3,2,1,0:T(8,128)(2,1)S(1)} collective-permute-done((bf16[1,2,1040,128]{3,2,1,0:T(8,128)(2,1)S(1)}, bf16[1,2,1040,128]{3,2,1,0:T(8,128)(2,1)S(1)}, u32[]{:S(2)}, u32[]{:S(2)}) %collective-permute-start.10) | collective-permute-done | bytes 532512 | tf_op jit(solution)/shard_map/ppermute | solution.py:378
  32.8 0.1 join_odd.1
  32.9 3.5 %collective-permute-start.11 = (bf16[1,2,1040,128]{3,2,1,0:T(8,128)(2,1)S(1)}, bf16[1,2,1040,128]{3,2,1,0:T(8,128)(2,1)S(1)}, u32[]{:S(2)}, u32[]{:S(2)}) collective-permute-start(bf16[1,2,1040,128]{3,2,1,0:T(8,128)(2,1)S(1)} %join_odd.1), channel_id=1, source_target_pairs={{8,16},{12,20},{16,8},{20,12},{9,17},{13,21},{17,9},{21,13},{10,18... | collective-permute-start | bytes 1597448 | tf_op jit(solution)/shard_map/ppermute | solution.py:382
  36.4 3.5 %collective-permute-done.1.rest_1_ = bf16[128,2048]{1,0:T(8,128)(2,1)S(1)} collective-permute-done((bf16[128,2048]{1,0:T(8,128)(2,1)S(1)}, bf16[128,2048]{1,0:T(8,128)(2,1)S(1)}, u32[]{:S(2)}, u32[]{:S(2)}) %collective-permute-start.1) | collective-permute-done | bytes 524320 | tf_op jit(solution)/shard_map/ppermute | solution.py:343
  39.9 8.3 %collective-permute-done.2.rest_2_ = bf16[128,2048]{1,0:T(8,128)(2,1)S(1)} collective-permute-done((bf16[128,2048]{1,0:T(8,128)(2,1)S(1)}, bf16[128,2048]{1,0:T(8,128)(2,1)S(1)}, u32[]{:S(2)}, u32[]{:S(2)}) %collective-permute-start.2) | collective-permute-done | bytes 524320 | tf_op jit(solution)/shard_map/ppermute | solution.py:343
  48.1 1.6 %collective-permute-done.4.rest_3_ = bf16[128,2048]{1,0:T(8,128)(2,1)S(1)} collective-permute-done((bf16[128,2048]{1,0:T(8,128)(2,1)S(1)}, bf16[128,2048]{1,0:T(8,128)(2,1)S(1)}, u32[]{:S(2)}, u32[]{:S(2)}) %collective-permute-start.4) | collective-permute-done | bytes 524320 | tf_op jit(solution)/shard_map/ppermute | solution.py:343
  49.8 0.0 copy-done.3
  49.8 0.0 copy-done.4
  49.8 3.9 %feat_grad.1 = bf16[384,2048]{1,0:T(8,128)(2,1)} custom-call(s32[1,2]{1,0:T(1,128)S(1)} %copy-done.3, s32[1,4]{1,0:T(1,128)S(1)} %copy-done.4, bf16[384,2048]{1,0:T(8,128)(2,1)S(1)} %copy-done, bf16[128,2048]{1,0:T(8,128)(2,1)S(1)} %copy-done.1, bf16[128,2048]{1,0:T(8,128)(2,1)S(1)} %collective-permute-done.1.rest_1_, ...), custom_call_target="tpu_custom_call" | custom-call | flops 805306368 | bytes 5242892 | tf_op jit(solution)/shard_map/feat_grad/pallas_call | solution.py:279
  53.7 0.0 collective-permute-done.9.rest_0_
  53.7 0.0 collective-permute-done.11.rest_1_
  53.7 1.4 %update.1 = bf16[128,2048]{1,0:T(8,128)(2,1)} custom-call(bf16[128,2048]{1,0:T(8,128)(2,1)S(1)} %copy-done.1, bf16[3,2,1040,128]{3,2,1,0:T(8,128)(2,1)S(1)} %get-tuple-element.19.refs_2_.rest_ref, bf16[1,2,1040,128]{3,2,1,0:T(8,128)(2,1)S(1)} %collective-permute-done.9.rest_0_, bf16[1,2,1040,128]{3,2,1,0:T(8,128)(2,1)S(1)} %collective-permute-done.11.rest_1_), custom_call_target="tpu_custom_call" | custom-call | flops 2621440 | bytes 3710976 | tf_op jit(solution)/shard_map/update/pallas_call | solution.py:279
Async XLA Ops:
  0.6 3.0 %copy-start = (bf16[384,2048]{1,0:T(8,128)(2,1)S(1)}, bf16[384,2048]{1,0:T(8,128)(2,1)}, u32[]{:S(2)}) copy-start(bf16[384,2048]{1,0:T(8,128)(2,1)} %features_ref.7) | copy-start | bytes 4718596
  0.6 3.0 %copy-start.2 = (s32[1,384]{1,0:T(1,128)S(1)}, s32[1,384]{1,0:T(1,128)}, u32[]{:S(2)}) copy-start(s32[1,384]{1,0:T(1,128)} %labels_ref.4) | copy-start | bytes 4612
  3.6 2.2 %collective-permute-start = (bf16[1,2,1040,128]{3,2,1,0:T(8,128)(2,1)}, bf16[1,2,1040,128]{3,2,1,0:T(8,128)(2,1)S(1)}, u32[]{:S(2)}, u32[]{:S(2)}) collective-permute-start(bf16[1,2,1040,128]{3,2,1,0:T(8,128)(2,1)} %away_first.1), channel_id=1, source_target_pairs={{0,4},{4,0},{8,12},{12,8},{16,20},{20,16},{24,28},{28,24},{1,5},{5... | collective-permute-start | bytes 1597448 | tf_op jit(solution)/shard_map/ppermute | solution.py:315
  6.2 18.7 %copy-start.1 = (bf16[128,2048]{1,0:T(8,128)(2,1)S(1)}, bf16[128,2048]{1,0:T(8,128)(2,1)}, u32[]{:S(2)}) copy-start(bf16[128,2048]{1,0:T(8,128)(2,1)} %memory_ref.1) | copy-start | bytes 1572868
  6.3 3.5 %collective-permute-start.5 = (bf16[3,2,1040,128]{3,2,1,0:T(8,128)(2,1)S(1)}, bf16[3,2,1040,128]{3,2,1,0:T(8,128)(2,1)S(1)}, u32[]{:S(2)}, u32[]{:S(2)}) collective-permute-start(bf16[3,2,1040,128]{3,2,1,0:T(8,128)(2,1)S(1)} %away_rest.1), channel_id=1, source_target_pairs={{0,4},{4,0},{8,12},{12,8},{16,20},{20,16},{24,28},{28,24},{1,5},{5... | collective-permute-start | bytes 4792328 | tf_op jit(solution)/shard_map/ppermute | solution.py:336
  6.4 9.2 %collective-permute-start.3 = (bf16[1040,128]{1,0:T(8,128)(2,1)S(1)}, bf16[1040,128]{1,0:T(8,128)(2,1)S(1)}, u32[]{:S(2)}, u32[]{:S(2)}) collective-permute-start(bf16[1040,128]{1,0:T(8,128)(2,1)S(1)} %get-tuple-element.16.mine_ref.refs_1_), channel_id=1, source_target_pairs={{0,8},{4,12},{8,0},{12,4},{16,24},{20,28},{24,16},{28,20},{1,9},{5... | collective-permute-start | bytes 798728 | tf_op jit(solution)/shard_map/ppermute | solution.py:360
  6.9 14.5 %collective-permute-start.6 = (bf16[1040,128]{1,0:T(8,128)(2,1)S(1)}, bf16[1040,128]{1,0:T(8,128)(2,1)S(1)}, u32[]{:S(2)}, u32[]{:S(2)}) collective-permute-start(bf16[1040,128]{1,0:T(8,128)(2,1)S(1)} %get-tuple-element.20.mine_ref.refs_0_), channel_id=1, source_target_pairs={{0,8},{4,12},{8,0},{12,4},{16,24},{20,28},{24,16},{28,20},{1,9},{5... | collective-permute-start | bytes 798728 | tf_op jit(solution)/shard_map/ppermute | solution.py:360
  11.2 21.6 %collective-permute-start.10 = (bf16[1,2,1040,128]{3,2,1,0:T(8,128)(2,1)S(1)}, bf16[1,2,1040,128]{3,2,1,0:T(8,128)(2,1)S(1)}, u32[]{:S(2)}, u32[]{:S(2)}) collective-permute-start(bf16[1,2,1040,128]{3,2,1,0:T(8,128)(2,1)S(1)} %get-tuple-element.21), channel_id=1, source_target_pairs={{0,8},{4,12},{8,0},{12,4},{16,24},{20,28},{24,16},{28,20},{1,9},{5... | collective-permute-start | bytes 1597448 | tf_op jit(solution)/shard_map/ppermute | solution.py:378
  15.7 11.3 %collective-permute-start.8 = (bf16[1040,128]{1,0:T(8,128)(2,1)S(1)}, bf16[1040,128]{1,0:T(8,128)(2,1)S(1)}, u32[]{:S(2)}, u32[]{:S(2)}) collective-permute-start(bf16[1040,128]{1,0:T(8,128)(2,1)S(1)} %join_half.3), channel_id=1, source_target_pairs={{8,16},{12,20},{16,8},{20,12},{9,17},{13,21},{17,9},{21,13},{10,18... | collective-permute-start | bytes 798728 | tf_op jit(solution)/shard_map/ppermute | solution.py:373
  21.4 9.2 %collective-permute-start.7 = (bf16[1040,128]{1,0:T(8,128)(2,1)S(1)}, bf16[1040,128]{1,0:T(8,128)(2,1)S(1)}, u32[]{:S(2)}, u32[]{:S(2)}) collective-permute-start(bf16[1040,128]{1,0:T(8,128)(2,1)S(1)} %join_half.2), channel_id=1, source_target_pairs={{8,16},{12,20},{16,8},{20,12},{9,17},{13,21},{17,9},{21,13},{10,18... | collective-permute-start | bytes 798728 | tf_op jit(solution)/shard_map/ppermute | solution.py:373
  24.9 14.9 %collective-permute-start.1 = (bf16[128,2048]{1,0:T(8,128)(2,1)S(1)}, bf16[128,2048]{1,0:T(8,128)(2,1)S(1)}, u32[]{:S(2)}, u32[]{:S(2)}) collective-permute-start(bf16[128,2048]{1,0:T(8,128)(2,1)S(1)} %copy-done.1), channel_id=1, source_target_pairs={{0,1},{1,0},{2,3},{3,2},{4,5},{5,4},{6,7},{7,6},{8,9},{9,8},{10,11... | collective-permute-start | bytes 1572872 | tf_op jit(solution)/shard_map/ppermute | solution.py:343
  25.5 22.6 %collective-permute-start.2 = (bf16[128,2048]{1,0:T(8,128)(2,1)S(1)}, bf16[128,2048]{1,0:T(8,128)(2,1)S(1)}, u32[]{:S(2)}, u32[]{:S(2)}) collective-permute-start(bf16[128,2048]{1,0:T(8,128)(2,1)S(1)} %copy-done.1), channel_id=1, source_target_pairs={{0,2},{1,3},{2,0},{3,1},{4,6},{5,7},{6,4},{7,5},{8,10},{9,11},{10,... | collective-permute-start | bytes 1572872 | tf_op jit(solution)/shard_map/ppermute | solution.py:343
  27.1 22.7 %collective-permute-start.4 = (bf16[128,2048]{1,0:T(8,128)(2,1)S(1)}, bf16[128,2048]{1,0:T(8,128)(2,1)S(1)}, u32[]{:S(2)}, u32[]{:S(2)}) collective-permute-start(bf16[128,2048]{1,0:T(8,128)(2,1)S(1)} %copy-done.1), channel_id=1, source_target_pairs={{0,3},{1,2},{2,1},{3,0},{4,7},{5,6},{6,5},{7,4},{8,11},{9,10},{10,... | collective-permute-start | bytes 1572872 | tf_op jit(solution)/shard_map/ppermute | solution.py:343
  30.8 19.0 %copy-start.3 = (s32[1,2]{1,0:T(1,128)S(1)}, s32[1,2]{1,0:T(1,128)}, u32[]{:S(2)}) copy-start(s32[1,2]{1,0:T(1,128)} %requests_ref.1) | copy-start | bytes 28
  30.8 19.0 %copy-start.4 = (s32[1,4]{1,0:T(1,128)S(1)}, s32[1,4]{1,0:T(1,128)}, u32[]{:S(2)}) copy-start(s32[1,4]{1,0:T(1,128)} %owners_ref.1) | copy-start | bytes 52
  30.8 22.9 %collective-permute-start.9 = (bf16[1,2,1040,128]{3,2,1,0:T(8,128)(2,1)S(1)}, bf16[1,2,1040,128]{3,2,1,0:T(8,128)(2,1)S(1)}, u32[]{:S(2)}, u32[]{:S(2)}) collective-permute-start(bf16[1,2,1040,128]{3,2,1,0:T(8,128)(2,1)S(1)} %join_even.1), channel_id=1, source_target_pairs={{0,8},{4,12},{8,0},{12,4},{16,24},{20,28},{24,16},{28,20},{1,9},{5... | collective-permute-start | bytes 1597448 | tf_op jit(solution)/shard_map/ppermute | solution.py:381
  32.9 20.7 %collective-permute-start.11 = (bf16[1,2,1040,128]{3,2,1,0:T(8,128)(2,1)S(1)}, bf16[1,2,1040,128]{3,2,1,0:T(8,128)(2,1)S(1)}, u32[]{:S(2)}, u32[]{:S(2)}) collective-permute-start(bf16[1,2,1040,128]{3,2,1,0:T(8,128)(2,1)S(1)} %join_odd.1), channel_id=1, source_target_pairs={{8,16},{12,20},{16,8},{20,12},{9,17},{13,21},{17,9},{21,13},{10,18... | collective-permute-start | bytes 1597448 | tf_op jit(solution)/shard_map/ppermute | solution.py:382

commit v2 on v1

--- a/solution.py
+++ b/solution.py
@@ -24,7 +24,7 @@
 PARAMS = pltpu.CompilerParams(vmem_limit_bytes=16 * 2**20)
 
 
-def write_sums(base, labels_ref, features_ref, block_rows, came, store, ready=None):
+def write_sums(base, labels_ref, features_ref, block_rows, came, store):
     crop_count, feat_width = features_ref.shape
     half_rows = block_rows // HALVES
     slabs = feat_width // LANES
@@ -36,17 +36,14 @@
             part = part + came(h, first, part.shape[0]).astype(jnp.float32)
         store(h, first, part.astype(jnp.bfloat16))
 
-    wide = WIDE
-    for s in range(0, slabs, wide):
-        if ready is not None:
-            ready(s // wide)
+    for s in range(0, slabs, WIDE):
         part = jnp.dot(
             match,
-            features_ref[:, s * LANES : (s + wide) * LANES],
+            features_ref[:, s * LANES : (s + WIDE) * LANES],
             preferred_element_type=jnp.float32,
         )
         for h in range(HALVES):
-            for i in range(wide):
+            for i in range(WIDE):
                 put(
                     h,
                     (s + i) * half_rows,
@@ -85,29 +82,10 @@
     return lambda h, first, rows: ref[(*at, h, pl.ds(first, rows), slice(None))]
 
 
-def away_first_kernel(
-    layers, block_rows, labels_hbm, features_hbm, out_ref, labels_ref, features_ref, sems
-):
-    columns = WIDE * LANES
-    copies = [pltpu.make_async_copy(labels_hbm, labels_ref, sems.at[0])]
-    for i in range(features_ref.shape[1] // columns):
-        part = (slice(None), pl.ds(i * columns, columns))
-        copies.append(
-            pltpu.make_async_copy(features_hbm.at[part], features_ref.at[part], sems.at[i + 1])
-        )
-    for copy in copies:
-        copy.start()
-    copies[0].wait()
+def away_first_kernel(layers, block_rows, labels_ref, features_ref, out_ref):
     core = 1 - lax.axis_index("region") % CORES
-    write_sums(
-        base_at(0, layers, core, block_rows),
-        labels_ref,
-        features_ref,
-        block_rows,
-        None,
-        block_of(out_ref, 0),
-        lambda i: copies[i + 1].wait(),
-    )
+    base = base_at(0, layers, core, block_rows)
+    write_sums(base, labels_ref, features_ref, block_rows, None, block_of(out_ref, 0))
 
 
 def away_rest_kernel(layers, block_rows, labels_ref, features_ref, out_ref):
@@ -142,6 +120,11 @@
 
     lax.fori_loop(0, layers - 1, one, 0)
     second_ref[0] = out_ref[0]
+
+
+def has_odd(layers):
+    layer = lax.axis_index("region") // CORES
+    return (layer > 0) & (layer < layers - 1)
 
 
 def join_half_kernel(mine_ref, came_ref, out_ref):
@@ -166,9 +149,10 @@
     def add(mine):
         for h in range(HALVES):
             came = came_refs[h][...] if len(came_refs) > 1 else came_refs[0][0, h]
-            out_ref[0, h] = (mine(h).astype(jnp.float32) + came.astype(jnp.float32)).astype(
-                jnp.bfloat16
-            )
+            came = came.astype(jnp.float32)
+            if not odd:
+                came = jnp.where(has_odd(layers), came, 0.0)
+            out_ref[0, h] = (mine(h).astype(jnp.float32) + came).astype(jnp.bfloat16)
 
     @pl.when(place == 0)
     def _():
@@ -183,6 +167,7 @@
     layer = lax.axis_index("region") // CORES
     place = jnp.where(layer < layers // 2, layers - 1 - layer, layer) - 1
     came_refs, out_ref, mixed_ref = rest[:-2], rest[-2], rest[-1]
+    linked = has_odd(layers)
     block_rows, feat_width = memory_ref.shape
     half_rows = block_rows // HALVES
     slabs = feat_width // LANES
@@ -190,8 +175,8 @@
 
         def total(first, rows):
             t = rest_ref[place, h, pl.ds(first, rows), :].astype(jnp.float32)
-            for ref in came_refs:
-                t = t + ref[0, h, pl.ds(first, rows), :].astype(jnp.float32)
+            even, odd = (ref[0, h, pl.ds(first, rows), :].astype(jnp.float32) for ref in came_refs)
+            t = t + even + jnp.where(linked, odd, 0.0)
             return t
 
         digits = total(slabs * half_rows, EXTRA)
@@ -270,7 +255,7 @@
     bf16 = jnp.bfloat16
     after = lax.optimization_barrier
 
-    def call(kernel, name, out_shape, operands, flops, scratch=(), smem=0, any_from=None, params=PARAMS):
+    def call(kernel, name, out_shape, operands, flops, scratch=(), smem=0, any_from=None):
         outs = out_shape if isinstance(out_shape, list) else [out_shape]
         flat, tree = jax.tree.flatten(operands)
         specs = [SMEM if i < smem else VMEM for i in range(len(flat))]
@@ -282,7 +267,7 @@
             in_specs=specs,
             out_specs=[VMEM] * len(outs) if isinstance(out_shape, list) else VMEM,
             scratch_shapes=list(scratch),
-            compiler_params=params,
+            compiler_params=PARAMS,
             cost_estimate=pl.CostEstimate(
                 flops=flops,
                 bytes_accessed=sum(2 * x.size for x in [*flat, *outs]),
@@ -304,13 +289,6 @@
         payloads(1),
         (labels, features),
         block_flops,
-        scratch=(
-            pltpu.VMEM(labels.shape, labels.dtype),
-            pltpu.VMEM(features.shape, bf16),
-            pltpu.SemaphoreType.DMA((feat_width // (WIDE * LANES) + 1,)),
-        ),
-        any_from=0,
-        params=pltpu.CompilerParams(vmem_limit_bytes=60 * 2**20),
     )
     came_first = lax.ppermute(away_first, "region", swap)
     later_labels, away_first = after((labels, away_first))
@@ -347,6 +325,8 @@
     for z in range(1, layers - 1):
         other = z + 1 if z % 2 else z - 1
         odd += [(z * CORES + c, other * CORES + c) for c in range(CORES)]
+    for z in (0, layers - 1):
+        odd += [(z * CORES + c, z * CORES + (c ^ 1)) for c in range(CORES)]
 
     def joined(hop, is_odd, came):
         return call(
@@ -371,13 +351,16 @@
             pay_rows * LANES,
         )
         odd_came.append(lax.ppermute(leaves, "region", odd))
-    later_memory, even_came[-1] = after((sent_memory, even_came[-1]))
-    for k in range(1, group_count):
-        if k & (k - 1):
-            fetch(k, later_memory)
     even_came = [lax.ppermute(second, "region", even)]
     for hop in range(2, layers - 1):
-        even_next, odd_next = joined(hop, False, odd_came), joined(hop, True, even_came)
+        even_next = joined(hop, False, odd_came)
+        if hop == 2:
+            even_next, sent_memory, near = after((even_next, sent_memory, dict(blocks)))
+            blocks.update(near)
+            for k in range(1, group_count):
+                if k & (k - 1):
+                    fetch(k, sent_memory)
+        odd_next = joined(hop, True, even_came)
         even_came = [lax.ppermute(even_next, "region", even)]
         odd_came = [lax.ppermute(odd_next, "region", odd)]
 

time: 55.5 us -> 47.1 us (0.85)
  starting transfers between devices: 16.9 us -> 11.4 us
  waiting for transfers between devices: 25.6 us -> 23.1 us
  Pallas kernels: 11.8 us -> 9.39 us
  local copies, waits for them, and re-layouts: 0.03 us -> 2.11 us
    ppermute x3, waiting for transfers between devices: 13.4 us -> 7.32 us  [fetch(): lax.ppermute(block, 'group', [(g, g ^ k) for g in range(group_count)])]
    ppermute x2, starting transfers between devices: 6.96 us -> 3.3 us  [on_device(): odd_came.append(lax.ppermute(leaves, 'region', odd))]
    ppermute x2, waiting for transfers between devices: 2.15 us -> 5.7 us  [on_device(): odd_came.append(lax.ppermute(leaves, 'region', odd))]
    pallas_call x10, Pallas kernels: 11.8 us -> 9.39 us  [call(): pl.pallas_call(kernel, out_shape=out_shape, in_specs=specs, out_specs=[VM...]
    unnamed x10 -> x12, local copies, waits for them, and re-layouts: 0.03 us -> 2.11 us
    ppermute x1, starting transfers between devices: 3.48 us -> 1.65 us  [on_device(): odd_came = [lax.ppermute(odd_next, 'region', odd)]]
    ppermute x1, waiting for transfers between devices: 1.27 us -> 0.01 us  [on_device(): lax.ppermute(away_rest, 'region', swap)]
    ppermute x2, waiting for transfers between devices: 6.14 us -> 7.19 us  [on_device(): even_came = [lax.ppermute(x, 'region', even) for x in first]]
  transfers between devices with their start and end apart: 12 -> 12, of which waited for: 9 -> 7; matrix products, arithmetic and copies ran while one was open for 0% -> 0% of each run, Pallas kernels for 13% -> 15%
where the time goes in v2:
time: 47.1 us; the launch traced here: 46.8 us
  waiting for transfers between devices  23.1 us (49%)
  starting transfers between devices  11.4 us (24%)
  Pallas kernels  9.39 us (20%)
  local copies, waits for them, and re-layouts  2.11 us (4%)
  between operations  0.76 us (2%)
    pallas_call x10, Pallas kernels, call(): pl.pallas_call(kernel, out_shape=out_shape, in_specs=specs, out_specs=[VM...  9.39 us
    ppermute x3, waiting for transfers between devices, fetch(): lax.ppermute(block, 'group', [(g, g ^ k) for g in range(group_count)])  7.32 us
    ppermute x2, waiting for transfers between devices, on_device(): even_came = [lax.ppermute(x, 'region', even) for x in first]  7.19 us
    ppermute x2, waiting for transfers between devices, on_device(): odd_came.append(lax.ppermute(leaves, 'region', odd))  5.7 us
    ppermute x3, starting transfers between devices, fetch(): lax.ppermute(block, 'group', [(g, g ^ k) for g in range(group_count)])  3.65 us
    ppermute x2, starting transfers between devices, on_device(): odd_came.append(lax.ppermute(leaves, 'region', odd))  3.3 us
    ppermute x1, waiting for transfers between devices, on_device(): even_came = [lax.ppermute(second, 'region', even)]  2.18 us
    unnamed x12, local copies, waits for them, and re-layouts  2.11 us
  transfers between devices with their start and end apart: 12, of which 7 were waited for; matrix products, arithmetic and copies ran while one was open for 0% of the time, Pallas kernels for 15%

profile of v2, /device:TPU:10, one launch (start us, length us, event | category | flops | bytes accessed | tf_op | source)
XLA Modules:
  0.0 46.8 jit_solution(2837901046900980649)
XLA Ops:
  0.6 0.0 copy-start
  0.6 1.4 %copy-done = bf16[384,2048]{1,0:T(8,128)(2,1)S(1)} copy-done((bf16[384,2048]{1,0:T(8,128)(2,1)S(1)}, bf16[384,2048]{1,0:T(8,128)(2,1)}, u32[]{:S(2)}) %copy-start) | copy-done | bytes 1572888
  2.0 0.0 copy-start.3
  2.0 0.7 %copy-done.3 = s32[1,384]{1,0:T(1,128)S(1)} copy-done((s32[1,384]{1,0:T(1,128)S(1)}, s32[1,384]{1,0:T(1,128)}, u32[]{:S(2)}) %copy-start.3) | copy-done | bytes 1560
  2.7 0.4 away_first.1
  3.2 0.1 collective-permute-start
  3.3 1.4 %away_rest.1 = bf16[3,2,1040,128]{3,2,1,0:T(8,128)(2,1)S(1)} custom-call(s32[1,384]{1,0:T(1,128)S(1)} %copy-done.3, bf16[384,2048]{1,0:T(8,128)(2,1)S(1)} %copy-done), custom_call_target="tpu_custom_call" | custom-call | flops 603979776 | bytes 3171072 | tf_op jit(solution)/shard_map/away_rest/pallas_call | solution.py:264
  4.6 0.0 copy-start.2
  4.6 0.5 %collective-permute-done.came_ref = bf16[1,2,1040,128]{3,2,1,0:T(8,128)(2,1)S(1)} collective-permute-done((bf16[1,2,1040,128]{3,2,1,0:T(8,128)(2,1)S(1)}, bf16[1,2,1040,128]{3,2,1,0:T(8,128)(2,1)S(1)}, u32[]{:S(2)}, u32[]{:S(2)}) %collective-permute-start) | collective-permute-done | bytes 532512 | tf_op jit(solution)/shard_map/ppermute | solution.py:293
  5.2 0.4 chip_first.1
  5.6 0.2 collective-permute-start.1
  5.8 0.5 collective-permute-start.2
  6.3 1.6 %collective-permute-start.4 = (bf16[1040,128]{1,0:T(8,128)(2,1)S(1)}, bf16[1040,128]{1,0:T(8,128)(2,1)S(1)}, u32[]{:S(2)}, u32[]{:S(2)}) collective-permute-start(bf16[1040,128]{1,0:T(8,128)(2,1)S(1)} %get-tuple-element.20.mine_ref.refs_1_), channel_id=1, source_target_pairs={{0,8},{4,12},{8,0},{12,4},{16,24},{20,28},{24,16},{28,20},{1,9},{5... | collective-permute-start | bytes 798728 | tf_op jit(solution)/shard_map/ppermute | solution.py:340
  7.9 0.0 copy-done.2
  7.9 0.5 %collective-permute-start.6 = (bf16[128,2048]{1,0:T(8,128)(2,1)S(1)}, bf16[128,2048]{1,0:T(8,128)(2,1)S(1)}, u32[]{:S(2)}, u32[]{:S(2)}) collective-permute-start(bf16[128,2048]{1,0:T(8,128)(2,1)S(1)} %copy-done.2), channel_id=1, source_target_pairs={{0,1},{1,0},{2,3},{3,2},{4,5},{5,4},{6,7},{7,6},{8,9},{9,8},{10,11... | collective-permute-start | bytes 1572872 | tf_op jit(solution)/shard_map/ppermute | solution.py:321
  8.4 1.5 %collective-permute-start.7 = (bf16[128,2048]{1,0:T(8,128)(2,1)S(1)}, bf16[128,2048]{1,0:T(8,128)(2,1)S(1)}, u32[]{:S(2)}, u32[]{:S(2)}) collective-permute-start(bf16[128,2048]{1,0:T(8,128)(2,1)S(1)} %copy-done.2), channel_id=1, source_target_pairs={{0,2},{1,3},{2,0},{3,1},{4,6},{5,7},{6,4},{7,5},{8,10},{9,11},{10,... | collective-permute-start | bytes 1572872 | tf_op jit(solution)/shard_map/ppermute | solution.py:321
  9.9 0.0 collective-permute-done.1.came_ref
  9.9 1.4 %chip_rest.1 = (bf16[1,2,1040,128]{3,2,1,0:T(8,128)(2,1)S(1)}, bf16[3,2,1040,128]{3,2,1,0:T(8,128)(2,1)S(1)}) custom-call(s32[1,384]{1,0:T(1,128)S(1)} %copy-done.3, bf16[384,2048]{1,0:T(8,128)(2,1)S(1)} %copy-done, bf16[3,2,1040,128]{3,2,1,0:T(8,128)(2,1)S(1)} %collective-permute-done.1.came_ref), custom_call_target="tpu_custom_call" | custom-call | flops 603979776 | bytes 5300992 | tf_op jit(solution)/shard_map/chip_rest/pallas_call | solution.py:264
  11.3 0.5 %collective-permute-start.10 = (bf16[1,2,1040,128]{3,2,1,0:T(8,128)(2,1)S(1)}, bf16[1,2,1040,128]{3,2,1,0:T(8,128)(2,1)S(1)}, u32[]{:S(2)}, u32[]{:S(2)}) collective-permute-start(bf16[1,2,1040,128]{3,2,1,0:T(8,128)(2,1)S(1)} %get-tuple-element.29), channel_id=1, source_target_pairs={{0,8},{4,12},{8,0},{12,4},{16,24},{20,28},{24,16},{28,20},{1,9},{5... | collective-permute-start | bytes 1597448 | tf_op jit(solution)/shard_map/ppermute | solution.py:354
  11.8 3.2 %collective-permute-done.2.came_ref = bf16[1040,128]{1,0:T(8,128)(2,1)S(1)} collective-permute-done((bf16[1040,128]{1,0:T(8,128)(2,1)S(1)}, bf16[1040,128]{1,0:T(8,128)(2,1)S(1)}, u32[]{:S(2)}, u32[]{:S(2)}) %collective-permute-start.2) | collective-permute-done | bytes 266272 | tf_op jit(solution)/shard_map/ppermute | solution.py:340
  15.0 0.1 join_half.2
  15.1 1.6 %collective-permute-start.3 = (bf16[1040,128]{1,0:T(8,128)(2,1)S(1)}, bf16[1040,128]{1,0:T(8,128)(2,1)S(1)}, u32[]{:S(2)}, u32[]{:S(2)}) collective-permute-start(bf16[1040,128]{1,0:T(8,128)(2,1)S(1)} %join_half.2), channel_id=1, source_target_pairs={{8,16},{12,20},{16,8},{20,12},{0,4},{4,0},{24,28},{28,24},{9,17},{... | collective-permute-start | bytes 798728 | tf_op jit(solution)/shard_map/ppermute | solution.py:353
  16.8 4.0 %collective-permute-done.4.came_ref = bf16[1040,128]{1,0:T(8,128)(2,1)S(1)} collective-permute-done((bf16[1040,128]{1,0:T(8,128)(2,1)S(1)}, bf16[1040,128]{1,0:T(8,128)(2,1)S(1)}, u32[]{:S(2)}, u32[]{:S(2)}) %collective-permute-start.4) | collective-permute-done | bytes 266272 | tf_op jit(solution)/shard_map/ppermute | solution.py:340
  20.8 0.1 join_half.3
  20.8 1.6 %collective-permute-start.5 = (bf16[1040,128]{1,0:T(8,128)(2,1)S(1)}, bf16[1040,128]{1,0:T(8,128)(2,1)S(1)}, u32[]{:S(2)}, u32[]{:S(2)}) collective-permute-start(bf16[1040,128]{1,0:T(8,128)(2,1)S(1)} %join_half.3), channel_id=1, source_target_pairs={{8,16},{12,20},{16,8},{20,12},{0,4},{4,0},{24,28},{28,24},{9,17},{... | collective-permute-start | bytes 798728 | tf_op jit(solution)/shard_map/ppermute | solution.py:353
  22.5 0.0 collective-permute-done.3.refs_3_
  22.5 5.7 %collective-permute-done.5.refs_4_ = bf16[1040,128]{1,0:T(8,128)(2,1)S(1)} collective-permute-done((bf16[1040,128]{1,0:T(8,128)(2,1)S(1)}, bf16[1040,128]{1,0:T(8,128)(2,1)S(1)}, u32[]{:S(2)}, u32[]{:S(2)}) %collective-permute-start.5) | collective-permute-done | bytes 266272 | tf_op jit(solution)/shard_map/ppermute | solution.py:353
  28.2 0.2 join_even.1
  28.3 0.0 copy-start.1
  28.3 0.0 copy-start.4
  28.4 0.0 copy-start.5
  28.4 0.0 collective-permute-done.6.rest_1_
  28.4 0.0 collective-permute-done.7.rest_2_
  28.4 1.6 %collective-permute-start.8 = (bf16[128,2048]{1,0:T(8,128)(2,1)S(1)}, bf16[128,2048]{1,0:T(8,128)(2,1)S(1)}, u32[]{:S(2)}, u32[]{:S(2)}) collective-permute-start(bf16[128,2048]{1,0:T(8,128)(2,1)S(1)} %copy-done.2), channel_id=1, source_target_pairs={{0,3},{1,2},{2,1},{3,0},{4,7},{5,6},{6,5},{7,4},{8,11},{9,10},{10,... | collective-permute-start | bytes 1572872 | tf_op jit(solution)/shard_map/ppermute | solution.py:321
  30.0 0.0 collective-permute-start.9
  30.0 2.2 %collective-permute-done.10.refs_3_ = bf16[1,2,1040,128]{3,2,1,0:T(8,128)(2,1)S(1)} collective-permute-done((bf16[1,2,1040,128]{3,2,1,0:T(8,128)(2,1)S(1)}, bf16[1,2,1040,128]{3,2,1,0:T(8,128)(2,1)S(1)}, u32[]{:S(2)}, u32[]{:S(2)}) %collective-permute-start.10) | collective-permute-done | bytes 532512 | tf_op jit(solution)/shard_map/ppermute | solution.py:354
  32.2 0.1 join_odd.1
  32.3 1.6 %collective-permute-start.11 = (bf16[1,2,1040,128]{3,2,1,0:T(8,128)(2,1)S(1)}, bf16[1,2,1040,128]{3,2,1,0:T(8,128)(2,1)S(1)}, u32[]{:S(2)}, u32[]{:S(2)}) collective-permute-start(bf16[1,2,1040,128]{3,2,1,0:T(8,128)(2,1)S(1)} %join_odd.1), channel_id=1, source_target_pairs={{8,16},{12,20},{16,8},{20,12},{0,4},{4,0},{24,28},{28,24},{9,17},{... | collective-permute-start | bytes 1597448 | tf_op jit(solution)/shard_map/ppermute | solution.py:365
  33.9 7.3 %collective-permute-done.8.rest_3_ = bf16[128,2048]{1,0:T(8,128)(2,1)S(1)} collective-permute-done((bf16[128,2048]{1,0:T(8,128)(2,1)S(1)}, bf16[128,2048]{1,0:T(8,128)(2,1)S(1)}, u32[]{:S(2)}, u32[]{:S(2)}) %collective-permute-start.8) | collective-permute-done | bytes 524320 | tf_op jit(solution)/shard_map/ppermute | solution.py:321
  41.3 0.0 copy-done.1
  41.3 0.0 copy-done.4
  41.3 0.0 copy-done.5
  41.3 3.9 %feat_grad.1 = bf16[384,2048]{1,0:T(8,128)(2,1)} custom-call(s32[1,2]{1,0:T(1,128)S(1)} %copy-done.4, s32[1,4]{1,0:T(1,128)S(1)} %copy-done.5, bf16[384,2048]{1,0:T(8,128)(2,1)S(1)} %copy-done.1, bf16[128,2048]{1,0:T(8,128)(2,1)S(1)} %copy-done.2, bf16[128,2048]{1,0:T(8,128)(2,1)S(1)} %collective-permute-done.6.rest_1_, ...), custom_call_target="tpu_custom_call" | custom-call | flops 805306368 | bytes 5242892 | tf_op jit(solution)/shard_map/feat_grad/pallas_call | solution.py:264
  45.1 0.0 collective-permute-done.9.rest_0_
  45.2 0.2 collective-permute-done.11.rest_1_
  45.4 1.4 %update.1 = bf16[128,2048]{1,0:T(8,128)(2,1)} custom-call(bf16[128,2048]{1,0:T(8,128)(2,1)S(1)} %copy-done.2, bf16[3,2,1040,128]{3,2,1,0:T(8,128)(2,1)S(1)} %get-tuple-element.22.refs_2_.rest_ref, bf16[1,2,1040,128]{3,2,1,0:T(8,128)(2,1)S(1)} %collective-permute-done.9.rest_0_, bf16[1,2,1040,128]{3,2,1,0:T(8,128)(2,1)S(1)} %collective-permute-done.11.rest_1_), custom_call_target="tpu_custom_call" | custom-call | flops 2621440 | bytes 3710976 | tf_op jit(solution)/shard_map/update/pallas_call | solution.py:264
Async XLA Ops:
  0.6 1.4 %copy-start = (bf16[384,2048]{1,0:T(8,128)(2,1)S(1)}, bf16[384,2048]{1,0:T(8,128)(2,1)}, u32[]{:S(2)}) copy-start(bf16[384,2048]{1,0:T(8,128)(2,1)} %features_ref.9) | copy-start | bytes 4718596
  2.0 0.7 %copy-start.3 = (s32[1,384]{1,0:T(1,128)S(1)}, s32[1,384]{1,0:T(1,128)}, u32[]{:S(2)}) copy-start(s32[1,384]{1,0:T(1,128)} %labels_ref.6) | copy-start | bytes 4612
  3.2 2.0 %collective-permute-start = (bf16[1,2,1040,128]{3,2,1,0:T(8,128)(2,1)S(1)}, bf16[1,2,1040,128]{3,2,1,0:T(8,128)(2,1)S(1)}, u32[]{:S(2)}, u32[]{:S(2)}) collective-permute-start(bf16[1,2,1040,128]{3,2,1,0:T(8,128)(2,1)S(1)} %away_first.1), channel_id=1, source_target_pairs={{0,4},{4,0},{8,12},{12,8},{16,20},{20,16},{24,28},{28,24},{1,5},{5... | collective-permute-start | bytes 1597448 | tf_op jit(solution)/shard_map/ppermute | solution.py:293
  4.6 3.2 %copy-start.2 = (bf16[128,2048]{1,0:T(8,128)(2,1)S(1)}, bf16[128,2048]{1,0:T(8,128)(2,1)}, u32[]{:S(2)}) copy-start(bf16[128,2048]{1,0:T(8,128)(2,1)} %memory_ref.1) | copy-start | bytes 1572868
  5.6 4.3 %collective-permute-start.1 = (bf16[3,2,1040,128]{3,2,1,0:T(8,128)(2,1)S(1)}, bf16[3,2,1040,128]{3,2,1,0:T(8,128)(2,1)S(1)}, u32[]{:S(2)}, u32[]{:S(2)}) collective-permute-start(bf16[3,2,1040,128]{3,2,1,0:T(8,128)(2,1)S(1)} %away_rest.1), channel_id=1, source_target_pairs={{0,4},{4,0},{8,12},{12,8},{16,20},{20,16},{24,28},{28,24},{1,5},{5... | collective-permute-start | bytes 4792328 | tf_op jit(solution)/shard_map/ppermute | solution.py:314
  5.8 9.2 %collective-permute-start.2 = (bf16[1040,128]{1,0:T(8,128)(2,1)S(1)}, bf16[1040,128]{1,0:T(8,128)(2,1)S(1)}, u32[]{:S(2)}, u32[]{:S(2)}) collective-permute-start(bf16[1040,128]{1,0:T(8,128)(2,1)S(1)} %get-tuple-element.19.mine_ref.refs_0_), channel_id=1, source_target_pairs={{0,8},{4,12},{8,0},{12,4},{16,24},{20,28},{24,16},{28,20},{1,9},{5... | collective-permute-start | bytes 798728 | tf_op jit(solution)/shard_map/ppermute | solution.py:340
  6.3 14.5 %collective-permute-start.4 = (bf16[1040,128]{1,0:T(8,128)(2,1)S(1)}, bf16[1040,128]{1,0:T(8,128)(2,1)S(1)}, u32[]{:S(2)}, u32[]{:S(2)}) collective-permute-start(bf16[1040,128]{1,0:T(8,128)(2,1)S(1)} %get-tuple-element.20.mine_ref.refs_1_), channel_id=1, source_target_pairs={{0,8},{4,12},{8,0},{12,4},{16,24},{20,28},{24,16},{28,20},{1,9},{5... | collective-permute-start | bytes 798728 | tf_op jit(solution)/shard_map/ppermute | solution.py:340
  7.9 20.5 %collective-permute-start.6 = (bf16[128,2048]{1,0:T(8,128)(2,1)S(1)}, bf16[128,2048]{1,0:T(8,128)(2,1)S(1)}, u32[]{:S(2)}, u32[]{:S(2)}) collective-permute-start(bf16[128,2048]{1,0:T(8,128)(2,1)S(1)} %copy-done.2), channel_id=1, source_target_pairs={{0,1},{1,0},{2,3},{3,2},{4,5},{5,4},{6,7},{7,6},{8,9},{9,8},{10,11... | collective-permute-start | bytes 1572872 | tf_op jit(solution)/shard_map/ppermute | solution.py:321
  8.4 20.0 %collective-permute-start.7 = (bf16[128,2048]{1,0:T(8,128)(2,1)S(1)}, bf16[128,2048]{1,0:T(8,128)(2,1)S(1)}, u32[]{:S(2)}, u32[]{:S(2)}) collective-permute-start(bf16[128,2048]{1,0:T(8,128)(2,1)S(1)} %copy-done.2), channel_id=1, source_target_pairs={{0,2},{1,3},{2,0},{3,1},{4,6},{5,7},{6,4},{7,5},{8,10},{9,11},{10,... | collective-permute-start | bytes 1572872 | tf_op jit(solution)/shard_map/ppermute | solution.py:321
  11.3 20.8 %collective-permute-start.10 = (bf16[1,2,1040,128]{3,2,1,0:T(8,128)(2,1)S(1)}, bf16[1,2,1040,128]{3,2,1,0:T(8,128)(2,1)S(1)}, u32[]{:S(2)}, u32[]{:S(2)}) collective-permute-start(bf16[1,2,1040,128]{3,2,1,0:T(8,128)(2,1)S(1)} %get-tuple-element.29), channel_id=1, source_target_pairs={{0,8},{4,12},{8,0},{12,4},{16,24},{20,28},{24,16},{28,20},{1,9},{5... | collective-permute-start | bytes 1597448 | tf_op jit(solution)/shard_map/ppermute | solution.py:354
  15.1 7.4 %collective-permute-start.3 = (bf16[1040,128]{1,0:T(8,128)(2,1)S(1)}, bf16[1040,128]{1,0:T(8,128)(2,1)S(1)}, u32[]{:S(2)}, u32[]{:S(2)}) collective-permute-start(bf16[1040,128]{1,0:T(8,128)(2,1)S(1)} %join_half.2), channel_id=1, source_target_pairs={{8,16},{12,20},{16,8},{20,12},{0,4},{4,0},{24,28},{28,24},{9,17},{... | collective-permute-start | bytes 798728 | tf_op jit(solution)/shard_map/ppermute | solution.py:353
  20.8 7.4 %collective-permute-start.5 = (bf16[1040,128]{1,0:T(8,128)(2,1)S(1)}, bf16[1040,128]{1,0:T(8,128)(2,1)S(1)}, u32[]{:S(2)}, u32[]{:S(2)}) collective-permute-start(bf16[1040,128]{1,0:T(8,128)(2,1)S(1)} %join_half.3), channel_id=1, source_target_pairs={{8,16},{12,20},{16,8},{20,12},{0,4},{4,0},{24,28},{28,24},{9,17},{... | collective-permute-start | bytes 798728 | tf_op jit(solution)/shard_map/ppermute | solution.py:353
  28.3 12.9 %copy-start.1 = (bf16[384,2048]{1,0:T(8,128)(2,1)S(1)}, bf16[384,2048]{1,0:T(8,128)(2,1)}, u32[]{:S(2)}) copy-start(bf16[384,2048]{1,0:T(8,128)(2,1)} %features_ref.9) | copy-start | bytes 4718596
  28.3 12.9 %copy-start.4 = (s32[1,2]{1,0:T(1,128)S(1)}, s32[1,2]{1,0:T(1,128)}, u32[]{:S(2)}) copy-start(s32[1,2]{1,0:T(1,128)} %requests_ref.1) | copy-start | bytes 28
  28.4 12.9 %copy-start.5 = (s32[1,4]{1,0:T(1,128)S(1)}, s32[1,4]{1,0:T(1,128)}, u32[]{:S(2)}) copy-start(s32[1,4]{1,0:T(1,128)} %owners_ref.1) | copy-start | bytes 52
  28.4 12.9 %collective-permute-start.8 = (bf16[128,2048]{1,0:T(8,128)(2,1)S(1)}, bf16[128,2048]{1,0:T(8,128)(2,1)S(1)}, u32[]{:S(2)}, u32[]{:S(2)}) collective-permute-start(bf16[128,2048]{1,0:T(8,128)(2,1)S(1)} %copy-done.2), channel_id=1, source_target_pairs={{0,3},{1,2},{2,1},{3,0},{4,7},{5,6},{6,5},{7,4},{8,11},{9,10},{10,... | collective-permute-start | bytes 1572872 | tf_op jit(solution)/shard_map/ppermute | solution.py:321
  30.0 15.2 %collective-permute-start.9 = (bf16[1,2,1040,128]{3,2,1,0:T(8,128)(2,1)S(1)}, bf16[1,2,1040,128]{3,2,1,0:T(8,128)(2,1)S(1)}, u32[]{:S(2)}, u32[]{:S(2)}) collective-permute-start(bf16[1,2,1040,128]{3,2,1,0:T(8,128)(2,1)S(1)} %join_even.1), channel_id=1, source_target_pairs={{0,8},{4,12},{8,0},{12,4},{16,24},{20,28},{24,16},{28,20},{1,9},{5... | collective-permute-start | bytes 1597448 | tf_op jit(solution)/shard_map/ppermute | solution.py:364
  32.3 13.1 %collective-permute-start.11 = (bf16[1,2,1040,128]{3,2,1,0:T(8,128)(2,1)S(1)}, bf16[1,2,1040,128]{3,2,1,0:T(8,128)(2,1)S(1)}, u32[]{:S(2)}, u32[]{:S(2)}) collective-permute-start(bf16[1,2,1040,128]{3,2,1,0:T(8,128)(2,1)S(1)} %join_odd.1), channel_id=1, source_target_pairs={{8,16},{12,20},{16,8},{20,12},{0,4},{4,0},{24,28},{28,24},{9,17},{... | collective-permute-start | bytes 1597448 | tf_op jit(solution)/shard_map/ppermute | solution.py:365

commit v3 on v2

--- a/solution.py
+++ b/solution.py
@@ -185,14 +185,14 @@
         lane = lax.broadcasted_iota(jnp.int32, (half_rows, LANES), 1)
         counts = jnp.sum(jnp.where(row == lane, counts_row, 0.0), axis=1, keepdims=True)
         seen = counts > 0
-        divisor = jnp.maximum(counts, 1.0)
+        share = (1.0 - momentum_keep) / jnp.maximum(counts, 1.0)
         squares = jnp.zeros((half_rows, LANES), jnp.float32)
         for s in range(slabs):
             old = memory_ref[pl.ds(h * half_rows, half_rows), pl.ds(s * LANES, LANES)].astype(
                 jnp.float32
             )
-            averaged = total(s * half_rows, half_rows) / divisor
-            mixed = jnp.where(seen, momentum_keep * old + (1.0 - momentum_keep) * averaged, old)
+            added = total(s * half_rows, half_rows) * share
+            mixed = jnp.where(seen, momentum_keep * old + added, old)
             mixed_ref[:, pl.ds(s * LANES, LANES)] = mixed
             squares = squares + mixed * mixed
         mean = jnp.sum(squares, axis=1, keepdims=True) * (1.0 / feat_width)
@@ -299,6 +299,7 @@
         (later_labels, features),
         block_flops * (layers - 1),
     )
+    came_first, away_rest = after((came_first, away_rest))
     first = call(
         part(chip_first_kernel, layers, block_rows),
         "chip_first",
@@ -306,7 +307,7 @@
         (labels, features, came_first),
         block_flops,
     )
-    first, away_rest, sent_memory = after((first, away_rest, memory))
+    first, sent_memory = after((first, memory))
     second, rest = call(
         part(chip_rest_kernel, layers, block_rows),
         "chip_rest",
@@ -317,8 +318,8 @@
 
     blocks = {0: memory}
 
-    def fetch(k, block):
-        blocks[k] = lax.ppermute(block, "group", [(g, g ^ k) for g in range(group_count)])
+    def fetch(k, step, block):
+        blocks[k] = lax.ppermute(block, "group", [(g, g ^ step) for g in range(group_count)])
 
     even = [(r, ((r // CORES) ^ 1) * CORES + r % CORES) for r in range(region_count)]
     odd = []
@@ -340,7 +341,7 @@
     even_came = [lax.ppermute(x, "region", even) for x in first]
     for k in range(1, group_count):
         if k & (k - 1) == 0:
-            fetch(k, sent_memory)
+            fetch(k, k, sent_memory)
     odd_came = []
     for h in range(HALVES):
         leaves = call(
@@ -351,15 +352,15 @@
             pay_rows * LANES,
         )
         odd_came.append(lax.ppermute(leaves, "region", odd))
+    near, odd_came[0] = after((dict(blocks), odd_came[0]))
+    blocks.update(near)
+    for k in range(1, group_count):
+        if k & (k - 1):
+            bit = 1 << (k.bit_length() - 1)
+            fetch(k, bit, blocks[k ^ bit])
     even_came = [lax.ppermute(second, "region", even)]
     for hop in range(2, layers - 1):
         even_next = joined(hop, False, odd_came)
-        if hop == 2:
-            even_next, sent_memory, near = after((even_next, sent_memory, dict(blocks)))
-            blocks.update(near)
-            for k in range(1, group_count):
-                if k & (k - 1):
-                    fetch(k, sent_memory)
         odd_next = joined(hop, True, even_came)
         even_came = [lax.ppermute(even_next, "region", even)]
         odd_came = [lax.ppermute(odd_next, "region", odd)]

time: 47.1 us -> 47 us (level)
    ppermute x3, waiting for transfers between devices: 7.32 us -> 1.18 us  [fetch(): lax.ppermute(block, 'group', [(g, g ^ step) for g in range(group_count)])]
    ppermute x1, waiting for transfers between devices: 0.01 us -> 4.01 us  [on_device(): even_came = [lax.ppermute(even_next, 'region', even)]]
    ppermute x1, waiting for transfers between devices: 0.19 us -> 2.34 us  [on_device(): odd_came = [lax.ppermute(odd_next, 'region', odd)]]
    ppermute x2, waiting for transfers between devices: 5.7 us -> 4.13 us  [on_device(): odd_came.append(lax.ppermute(leaves, 'region', odd))]
    ppermute x1, waiting for transfers between devices: 2.18 us -> 3.69 us  [on_device(): even_came = [lax.ppermute(second, 'region', even)]]
  transfers between devices with their start and end apart: 12 -> 12, of which waited for: 7 -> 8; matrix products, arithmetic and copies ran while one was open for 0% -> 0% of each run, Pallas kernels for 15% -> 16%
where the time goes in v3:
time: 47 us; the launch traced here: 46.8 us
  waiting for transfers between devices  23.1 us (49%)
  starting transfers between devices  11.5 us (24%)
  Pallas kernels  9.37 us (20%)
  local copies, waits for them, and re-layouts  2.11 us (4%)
  between operations  0.75 us (2%)
    pallas_call x10, Pallas kernels, call(): pl.pallas_call(kernel, out_shape=out_shape, in_specs=specs, out_specs=[VM...  9.37 us
    ppermute x2, waiting for transfers between devices, on_device(): even_came = [lax.ppermute(x, 'region', even) for x in first]  7.19 us
    ppermute x2, waiting for transfers between devices, on_device(): odd_came.append(lax.ppermute(leaves, 'region', odd))  4.13 us
    ppermute x1, waiting for transfers between devices, on_device(): even_came = [lax.ppermute(even_next, 'region', even)]  4.01 us
    ppermute x1, waiting for transfers between devices, on_device(): even_came = [lax.ppermute(second, 'region', even)]  3.69 us
    ppermute x3, starting transfers between devices, fetch(): lax.ppermute(block, 'group', [(g, g ^ step) for g in range(group_count)])  3.63 us
    ppermute x2, starting transfers between devices, on_device(): odd_came.append(lax.ppermute(leaves, 'region', odd))  3.31 us
    ppermute x1, waiting for transfers between devices, on_device(): odd_came = [lax.ppermute(odd_next, 'region', odd)]  2.34 us
  transfers between devices with their start and end apart: 12, of which 8 were waited for; matrix products, arithmetic and copies ran while one was open for 0% of the time, Pallas kernels for 16%

profile of v3, /device:TPU:10, one launch (start us, length us, event | category | flops | bytes accessed | tf_op | source)
XLA Modules:
  0.0 46.8 jit_solution(9585506694015695240)
XLA Ops:
  0.6 0.0 copy-start
  0.6 1.4 %copy-done = bf16[384,2048]{1,0:T(8,128)(2,1)S(1)} copy-done((bf16[384,2048]{1,0:T(8,128)(2,1)S(1)}, bf16[384,2048]{1,0:T(8,128)(2,1)}, u32[]{:S(2)}) %copy-start) | copy-done | bytes 1572888
  2.0 0.0 copy-start.3
  2.0 0.7 %copy-done.3 = s32[1,384]{1,0:T(1,128)S(1)} copy-done((s32[1,384]{1,0:T(1,128)S(1)}, s32[1,384]{1,0:T(1,128)}, u32[]{:S(2)}) %copy-start.3) | copy-done | bytes 1560
  2.7 0.4 away_first.1
  3.2 0.1 collective-permute-start
  3.3 1.4 %away_rest.1 = bf16[3,2,1040,128]{3,2,1,0:T(8,128)(2,1)S(1)} custom-call(s32[1,384]{1,0:T(1,128)S(1)} %copy-done.3, bf16[384,2048]{1,0:T(8,128)(2,1)S(1)} %copy-done), custom_call_target="tpu_custom_call" | custom-call | flops 603979776 | bytes 3171072 | tf_op jit(solution)/shard_map/away_rest/pallas_call | solution.py:264
  4.6 0.0 copy-start.2
  4.6 0.5 %collective-permute-done.came_ref = bf16[1,2,1040,128]{3,2,1,0:T(8,128)(2,1)S(1)} collective-permute-done((bf16[1,2,1040,128]{3,2,1,0:T(8,128)(2,1)S(1)}, bf16[1,2,1040,128]{3,2,1,0:T(8,128)(2,1)S(1)}, u32[]{:S(2)}, u32[]{:S(2)}) %collective-permute-start) | collective-permute-done | bytes 532512 | tf_op jit(solution)/shard_map/ppermute | solution.py:293
  5.2 0.1 collective-permute-start.6
  5.3 0.4 chip_first.1
  5.7 0.5 %collective-permute-start.3 = (bf16[1040,128]{1,0:T(8,128)(2,1)S(1)}, bf16[1040,128]{1,0:T(8,128)(2,1)S(1)}, u32[]{:S(2)}, u32[]{:S(2)}) collective-permute-start(bf16[1040,128]{1,0:T(8,128)(2,1)S(1)} %get-tuple-element.21.mine_ref.refs_0_), channel_id=1, source_target_pairs={{0,8},{4,12},{8,0},{12,4},{16,24},{20,28},{24,16},{28,20},{1,9},{5... | collective-permute-start | bytes 798728 | tf_op jit(solution)/shard_map/ppermute | solution.py:341
  6.3 0.0 copy-done.2
  6.3 0.2 collective-permute-start.1
  6.5 1.9 %collective-permute-start.2 = (bf16[128,2048]{1,0:T(8,128)(2,1)S(1)}, bf16[128,2048]{1,0:T(8,128)(2,1)S(1)}, u32[]{:S(2)}, u32[]{:S(2)}) collective-permute-start(bf16[128,2048]{1,0:T(8,128)(2,1)S(1)} %copy-done.2), channel_id=1, source_target_pairs={{0,2},{1,3},{2,0},{3,1},{4,6},{5,7},{6,4},{7,5},{8,10},{9,11},{10,... | collective-permute-start | bytes 1572872 | tf_op jit(solution)/shard_map/ppermute | solution.py:322
  8.3 1.6 %collective-permute-start.7 = (bf16[1040,128]{1,0:T(8,128)(2,1)S(1)}, bf16[1040,128]{1,0:T(8,128)(2,1)S(1)}, u32[]{:S(2)}, u32[]{:S(2)}) collective-permute-start(bf16[1040,128]{1,0:T(8,128)(2,1)S(1)} %get-tuple-element.27.mine_ref.refs_1_), channel_id=1, source_target_pairs={{0,8},{4,12},{8,0},{12,4},{16,24},{20,28},{24,16},{28,20},{1,9},{5... | collective-permute-start | bytes 798728 | tf_op jit(solution)/shard_map/ppermute | solution.py:341
  9.9 0.0 collective-permute-done.6.came_ref
  9.9 1.4 %chip_rest.1 = (bf16[1,2,1040,128]{3,2,1,0:T(8,128)(2,1)S(1)}, bf16[3,2,1040,128]{3,2,1,0:T(8,128)(2,1)S(1)}) custom-call(s32[1,384]{1,0:T(1,128)S(1)} %copy-done.3, bf16[384,2048]{1,0:T(8,128)(2,1)S(1)} %copy-done, bf16[3,2,1040,128]{3,2,1,0:T(8,128)(2,1)S(1)} %collective-permute-done.6.came_ref), custom_call_target="tpu_custom_call" | custom-call | flops 603979776 | bytes 5300992 | tf_op jit(solution)/shard_map/chip_rest/pallas_call | solution.py:264
  11.3 0.5 %collective-permute-start.10 = (bf16[1,2,1040,128]{3,2,1,0:T(8,128)(2,1)S(1)}, bf16[1,2,1040,128]{3,2,1,0:T(8,128)(2,1)S(1)}, u32[]{:S(2)}, u32[]{:S(2)}) collective-permute-start(bf16[1,2,1040,128]{3,2,1,0:T(8,128)(2,1)S(1)} %get-tuple-element.29), channel_id=1, source_target_pairs={{0,8},{4,12},{8,0},{12,4},{16,24},{20,28},{24,16},{28,20},{1,9},{5... | collective-permute-start | bytes 1597448 | tf_op jit(solution)/shard_map/ppermute | solution.py:361
  11.8 3.2 %collective-permute-done.3.came_ref = bf16[1040,128]{1,0:T(8,128)(2,1)S(1)} collective-permute-done((bf16[1040,128]{1,0:T(8,128)(2,1)S(1)}, bf16[1040,128]{1,0:T(8,128)(2,1)S(1)}, u32[]{:S(2)}, u32[]{:S(2)}) %collective-permute-start.3) | collective-permute-done | bytes 266272 | tf_op jit(solution)/shard_map/ppermute | solution.py:341
  15.0 0.1 join_half.2
  15.1 1.7 %collective-permute-start.4 = (bf16[1040,128]{1,0:T(8,128)(2,1)S(1)}, bf16[1040,128]{1,0:T(8,128)(2,1)S(1)}, u32[]{:S(2)}, u32[]{:S(2)}) collective-permute-start(bf16[1040,128]{1,0:T(8,128)(2,1)S(1)} %join_half.2), channel_id=1, source_target_pairs={{8,16},{12,20},{16,8},{20,12},{0,4},{4,0},{24,28},{28,24},{9,17},{... | collective-permute-start | bytes 798728 | tf_op jit(solution)/shard_map/ppermute | solution.py:354
  16.8 4.0 %collective-permute-done.7.came_ref = bf16[1040,128]{1,0:T(8,128)(2,1)S(1)} collective-permute-done((bf16[1040,128]{1,0:T(8,128)(2,1)S(1)}, bf16[1040,128]{1,0:T(8,128)(2,1)S(1)}, u32[]{:S(2)}, u32[]{:S(2)}) %collective-permute-start.7) | collective-permute-done | bytes 266272 | tf_op jit(solution)/shard_map/ppermute | solution.py:341
  20.7 0.1 join_half.3
  20.8 1.7 %collective-permute-start.8 = (bf16[1040,128]{1,0:T(8,128)(2,1)S(1)}, bf16[1040,128]{1,0:T(8,128)(2,1)S(1)}, u32[]{:S(2)}, u32[]{:S(2)}) collective-permute-start(bf16[1040,128]{1,0:T(8,128)(2,1)S(1)} %join_half.3), channel_id=1, source_target_pairs={{8,16},{12,20},{16,8},{20,12},{0,4},{4,0},{24,28},{28,24},{9,17},{... | collective-permute-start | bytes 798728 | tf_op jit(solution)/shard_map/ppermute | solution.py:354
  22.5 0.0 collective-permute-done.1.rest_1_
  22.5 0.0 collective-permute-done.2.rest_2_
  22.5 0.0 collective-permute-done.4.refs_3_
  22.5 1.6 %collective-permute-start.5 = (bf16[128,2048]{1,0:T(8,128)(2,1)S(1)}, bf16[128,2048]{1,0:T(8,128)(2,1)S(1)}, u32[]{:S(2)}, u32[]{:S(2)}) collective-permute-start(bf16[128,2048]{1,0:T(8,128)(2,1)S(1)} %collective-permute-done.1.rest_1_), channel_id=1, source_target_pairs={{0,2},{1,3},{2,0},{3,1},{4,6},{5,7},{6,4},{7,5},{8,10},{9,11},{10,... | collective-permute-start | bytes 1572872 | tf_op jit(solution)/shard_map/ppermute | solution.py:322
  24.1 4.1 %collective-permute-done.8.refs_4_ = bf16[1040,128]{1,0:T(8,128)(2,1)S(1)} collective-permute-done((bf16[1040,128]{1,0:T(8,128)(2,1)S(1)}, bf16[1040,128]{1,0:T(8,128)(2,1)S(1)}, u32[]{:S(2)}, u32[]{:S(2)}) %collective-permute-start.8) | collective-permute-done | bytes 266272 | tf_op jit(solution)/shard_map/ppermute | solution.py:354
  28.2 0.2 join_even.1
  28.3 0.0 copy-start.1
  28.4 0.0 copy-start.4
  28.4 0.0 copy-start.5
  28.4 0.1 collective-permute-start.9
  28.5 3.7 %collective-permute-done.10.refs_3_ = bf16[1,2,1040,128]{3,2,1,0:T(8,128)(2,1)S(1)} collective-permute-done((bf16[1,2,1040,128]{3,2,1,0:T(8,128)(2,1)S(1)}, bf16[1,2,1040,128]{3,2,1,0:T(8,128)(2,1)S(1)}, u32[]{:S(2)}, u32[]{:S(2)}) %collective-permute-start.10) | collective-permute-done | bytes 532512 | tf_op jit(solution)/shard_map/ppermute | solution.py:361
  32.2 0.1 join_odd.1
  32.3 1.7 %collective-permute-start.11 = (bf16[1,2,1040,128]{3,2,1,0:T(8,128)(2,1)S(1)}, bf16[1,2,1040,128]{3,2,1,0:T(8,128)(2,1)S(1)}, u32[]{:S(2)}, u32[]{:S(2)}) collective-permute-start(bf16[1,2,1040,128]{3,2,1,0:T(8,128)(2,1)S(1)} %join_odd.1), channel_id=1, source_target_pairs={{8,16},{12,20},{16,8},{20,12},{0,4},{4,0},{24,28},{28,24},{9,17},{... | collective-permute-start | bytes 1597448 | tf_op jit(solution)/shard_map/ppermute | solution.py:366
  33.9 1.2 %collective-permute-done.5.rest_3_ = bf16[128,2048]{1,0:T(8,128)(2,1)S(1)} collective-permute-done((bf16[128,2048]{1,0:T(8,128)(2,1)S(1)}, bf16[128,2048]{1,0:T(8,128)(2,1)S(1)}, u32[]{:S(2)}, u32[]{:S(2)}) %collective-permute-start.5) | collective-permute-done | bytes 524320 | tf_op jit(solution)/shard_map/ppermute | solution.py:322
  35.1 0.0 copy-done.1
  35.1 0.0 copy-done.4
  35.1 0.0 copy-done.5
  35.1 3.9 %feat_grad.1 = bf16[384,2048]{1,0:T(8,128)(2,1)} custom-call(s32[1,2]{1,0:T(1,128)S(1)} %copy-done.4, s32[1,4]{1,0:T(1,128)S(1)} %copy-done.5, bf16[384,2048]{1,0:T(8,128)(2,1)S(1)} %copy-done.1, bf16[128,2048]{1,0:T(8,128)(2,1)S(1)} %copy-done.2, bf16[128,2048]{1,0:T(8,128)(2,1)S(1)} %collective-permute-done.1.rest_1_, ...), custom_call_target="tpu_custom_call" | custom-call | flops 805306368 | bytes 5242892 | tf_op jit(solution)/shard_map/feat_grad/pallas_call | solution.py:264
  39.0 4.0 %collective-permute-done.9.rest_0_ = bf16[1,2,1040,128]{3,2,1,0:T(8,128)(2,1)S(1)} collective-permute-done((bf16[1,2,1040,128]{3,2,1,0:T(8,128)(2,1)S(1)}, bf16[1,2,1040,128]{3,2,1,0:T(8,128)(2,1)S(1)}, u32[]{:S(2)}, u32[]{:S(2)}) %collective-permute-start.9) | collective-permute-done | bytes 532512 | tf_op jit(solution)/shard_map/ppermute | solution.py:365
  43.0 2.3 %collective-permute-done.11.rest_1_ = bf16[1,2,1040,128]{3,2,1,0:T(8,128)(2,1)S(1)} collective-permute-done((bf16[1,2,1040,128]{3,2,1,0:T(8,128)(2,1)S(1)}, bf16[1,2,1040,128]{3,2,1,0:T(8,128)(2,1)S(1)}, u32[]{:S(2)}, u32[]{:S(2)}) %collective-permute-start.11) | collective-permute-done | bytes 532512 | tf_op jit(solution)/shard_map/ppermute | solution.py:366
  45.4 1.4 %update.1 = bf16[128,2048]{1,0:T(8,128)(2,1)} custom-call(bf16[128,2048]{1,0:T(8,128)(2,1)S(1)} %copy-done.2, bf16[3,2,1040,128]{3,2,1,0:T(8,128)(2,1)S(1)} %get-tuple-element.26.refs_2_.rest_ref, bf16[1,2,1040,128]{3,2,1,0:T(8,128)(2,1)S(1)} %collective-permute-done.9.rest_0_, bf16[1,2,1040,128]{3,2,1,0:T(8,128)(2,1)S(1)} %collective-permute-done.11.rest_1_), custom_call_target="tpu_custom_call" | custom-call | flops 2621440 | bytes 3710976 | tf_op jit(solution)/shard_map/update/pallas_call | solution.py:264
Async XLA Ops:
  0.6 1.4 %copy-start = (bf16[384,2048]{1,0:T(8,128)(2,1)S(1)}, bf16[384,2048]{1,0:T(8,128)(2,1)}, u32[]{:S(2)}) copy-start(bf16[384,2048]{1,0:T(8,128)(2,1)} %features_ref.9) | copy-start | bytes 4718596
  2.0 0.7 %copy-start.3 = (s32[1,384]{1,0:T(1,128)S(1)}, s32[1,384]{1,0:T(1,128)}, u32[]{:S(2)}) copy-start(s32[1,384]{1,0:T(1,128)} %labels_ref.6) | copy-start | bytes 4612
  3.2 2.0 %collective-permute-start = (bf16[1,2,1040,128]{3,2,1,0:T(8,128)(2,1)S(1)}, bf16[1,2,1040,128]{3,2,1,0:T(8,128)(2,1)S(1)}, u32[]{:S(2)}, u32[]{:S(2)}) collective-permute-start(bf16[1,2,1040,128]{3,2,1,0:T(8,128)(2,1)S(1)} %away_first.1), channel_id=1, source_target_pairs={{0,4},{4,0},{8,12},{12,8},{16,20},{20,16},{24,28},{28,24},{1,5},{5... | collective-permute-start | bytes 1597448 | tf_op jit(solution)/shard_map/ppermute | solution.py:293
  4.6 1.7 %copy-start.2 = (bf16[128,2048]{1,0:T(8,128)(2,1)S(1)}, bf16[128,2048]{1,0:T(8,128)(2,1)}, u32[]{:S(2)}) copy-start(bf16[128,2048]{1,0:T(8,128)(2,1)} %memory_ref.1) | copy-start | bytes 1572868
  5.2 4.8 %collective-permute-start.6 = (bf16[3,2,1040,128]{3,2,1,0:T(8,128)(2,1)S(1)}, bf16[3,2,1040,128]{3,2,1,0:T(8,128)(2,1)S(1)}, u32[]{:S(2)}, u32[]{:S(2)}) collective-permute-start(bf16[3,2,1040,128]{3,2,1,0:T(8,128)(2,1)S(1)} %away_rest.1), channel_id=1, source_target_pairs={{0,4},{4,0},{8,12},{12,8},{16,20},{20,16},{24,28},{28,24},{1,5},{5... | collective-permute-start | bytes 4792328 | tf_op jit(solution)/shard_map/ppermute | solution.py:315
  5.7 9.3 %collective-permute-start.3 = (bf16[1040,128]{1,0:T(8,128)(2,1)S(1)}, bf16[1040,128]{1,0:T(8,128)(2,1)S(1)}, u32[]{:S(2)}, u32[]{:S(2)}) collective-permute-start(bf16[1040,128]{1,0:T(8,128)(2,1)S(1)} %get-tuple-element.21.mine_ref.refs_0_), channel_id=1, source_target_pairs={{0,8},{4,12},{8,0},{12,4},{16,24},{20,28},{24,16},{28,20},{1,9},{5... | collective-permute-start | bytes 798728 | tf_op jit(solution)/shard_map/ppermute | solution.py:341
  6.3 16.2 %collective-permute-start.1 = (bf16[128,2048]{1,0:T(8,128)(2,1)S(1)}, bf16[128,2048]{1,0:T(8,128)(2,1)S(1)}, u32[]{:S(2)}, u32[]{:S(2)}) collective-permute-start(bf16[128,2048]{1,0:T(8,128)(2,1)S(1)} %copy-done.2), channel_id=1, source_target_pairs={{0,1},{1,0},{2,3},{3,2},{4,5},{5,4},{6,7},{7,6},{8,9},{9,8},{10,11... | collective-permute-start | bytes 1572872 | tf_op jit(solution)/shard_map/ppermute | solution.py:322
  6.5 16.0 %collective-permute-start.2 = (bf16[128,2048]{1,0:T(8,128)(2,1)S(1)}, bf16[128,2048]{1,0:T(8,128)(2,1)S(1)}, u32[]{:S(2)}, u32[]{:S(2)}) collective-permute-start(bf16[128,2048]{1,0:T(8,128)(2,1)S(1)} %copy-done.2), channel_id=1, source_target_pairs={{0,2},{1,3},{2,0},{3,1},{4,6},{5,7},{6,4},{7,5},{8,10},{9,11},{10,... | collective-permute-start | bytes 1572872 | tf_op jit(solution)/shard_map/ppermute | solution.py:322
  8.3 12.4 %collective-permute-start.7 = (bf16[1040,128]{1,0:T(8,128)(2,1)S(1)}, bf16[1040,128]{1,0:T(8,128)(2,1)S(1)}, u32[]{:S(2)}, u32[]{:S(2)}) collective-permute-start(bf16[1040,128]{1,0:T(8,128)(2,1)S(1)} %get-tuple-element.27.mine_ref.refs_1_), channel_id=1, source_target_pairs={{0,8},{4,12},{8,0},{12,4},{16,24},{20,28},{24,16},{28,20},{1,9},{5... | collective-permute-start | bytes 798728 | tf_op jit(solution)/shard_map/ppermute | solution.py:341
  11.3 20.8 %collective-permute-start.10 = (bf16[1,2,1040,128]{3,2,1,0:T(8,128)(2,1)S(1)}, bf16[1,2,1040,128]{3,2,1,0:T(8,128)(2,1)S(1)}, u32[]{:S(2)}, u32[]{:S(2)}) collective-permute-start(bf16[1,2,1040,128]{3,2,1,0:T(8,128)(2,1)S(1)} %get-tuple-element.29), channel_id=1, source_target_pairs={{0,8},{4,12},{8,0},{12,4},{16,24},{20,28},{24,16},{28,20},{1,9},{5... | collective-permute-start | bytes 1597448 | tf_op jit(solution)/shard_map/ppermute | solution.py:361
  15.1 7.4 %collective-permute-start.4 = (bf16[1040,128]{1,0:T(8,128)(2,1)S(1)}, bf16[1040,128]{1,0:T(8,128)(2,1)S(1)}, u32[]{:S(2)}, u32[]{:S(2)}) collective-permute-start(bf16[1040,128]{1,0:T(8,128)(2,1)S(1)} %join_half.2), channel_id=1, source_target_pairs={{8,16},{12,20},{16,8},{20,12},{0,4},{4,0},{24,28},{28,24},{9,17},{... | collective-permute-start | bytes 798728 | tf_op jit(solution)/shard_map/ppermute | solution.py:354
  20.8 7.4 %collective-permute-start.8 = (bf16[1040,128]{1,0:T(8,128)(2,1)S(1)}, bf16[1040,128]{1,0:T(8,128)(2,1)S(1)}, u32[]{:S(2)}, u32[]{:S(2)}) collective-permute-start(bf16[1040,128]{1,0:T(8,128)(2,1)S(1)} %join_half.3), channel_id=1, source_target_pairs={{8,16},{12,20},{16,8},{20,12},{0,4},{4,0},{24,28},{28,24},{9,17},{... | collective-permute-start | bytes 798728 | tf_op jit(solution)/shard_map/ppermute | solution.py:354
  22.5 12.6 %collective-permute-start.5 = (bf16[128,2048]{1,0:T(8,128)(2,1)S(1)}, bf16[128,2048]{1,0:T(8,128)(2,1)S(1)}, u32[]{:S(2)}, u32[]{:S(2)}) collective-permute-start(bf16[128,2048]{1,0:T(8,128)(2,1)S(1)} %collective-permute-done.1.rest_1_), channel_id=1, source_target_pairs={{0,2},{1,3},{2,0},{3,1},{4,6},{5,7},{6,4},{7,5},{8,10},{9,11},{10,... | collective-permute-start | bytes 1572872 | tf_op jit(solution)/shard_map/ppermute | solution.py:322
  28.3 6.8 %copy-start.1 = (bf16[384,2048]{1,0:T(8,128)(2,1)S(1)}, bf16[384,2048]{1,0:T(8,128)(2,1)}, u32[]{:S(2)}) copy-start(bf16[384,2048]{1,0:T(8,128)(2,1)} %features_ref.9) | copy-start | bytes 4718596
  28.4 6.8 %copy-start.4 = (s32[1,2]{1,0:T(1,128)S(1)}, s32[1,2]{1,0:T(1,128)}, u32[]{:S(2)}) copy-start(s32[1,2]{1,0:T(1,128)} %requests_ref.1) | copy-start | bytes 28
  28.4 6.7 %copy-start.5 = (s32[1,4]{1,0:T(1,128)S(1)}, s32[1,4]{1,0:T(1,128)}, u32[]{:S(2)}) copy-start(s32[1,4]{1,0:T(1,128)} %owners_ref.1) | copy-start | bytes 52
  28.4 14.6 %collective-permute-start.9 = (bf16[1,2,1040,128]{3,2,1,0:T(8,128)(2,1)S(1)}, bf16[1,2,1040,128]{3,2,1,0:T(8,128)(2,1)S(1)}, u32[]{:S(2)}, u32[]{:S(2)}) collective-permute-start(bf16[1,2,1040,128]{3,2,1,0:T(8,128)(2,1)S(1)} %join_even.1), channel_id=1, source_target_pairs={{0,8},{4,12},{8,0},{12,4},{16,24},{20,28},{24,16},{28,20},{1,9},{5... | collective-permute-start | bytes 1597448 | tf_op jit(solution)/shard_map/ppermute | solution.py:365
  32.3 13.1 %collective-permute-start.11 = (bf16[1,2,1040,128]{3,2,1,0:T(8,128)(2,1)S(1)}, bf16[1,2,1040,128]{3,2,1,0:T(8,128)(2,1)S(1)}, u32[]{:S(2)}, u32[]{:S(2)}) collective-permute-start(bf16[1,2,1040,128]{3,2,1,0:T(8,128)(2,1)S(1)} %join_odd.1), channel_id=1, source_target_pairs={{8,16},{12,20},{16,8},{20,12},{0,4},{4,0},{24,28},{28,24},{9,17},{... | collective-permute-start | bytes 1597448 | tf_op jit(solution)/shard_map/ppermute | solution.py:366

commit v4 on v3

--- a/solution.py
+++ b/solution.py
@@ -82,7 +82,7 @@
     return lambda h, first, rows: ref[(*at, h, pl.ds(first, rows), slice(None))]
 
 
-def away_first_kernel(layers, block_rows, labels_ref, features_ref, out_ref):
+def away_first_kernel(layers, block_rows, labels_ref, features_ref, early_ref, out_ref):
     core = 1 - lax.axis_index("region") % CORES
     base = base_at(0, layers, core, block_rows)
     write_sums(base, labels_ref, features_ref, block_rows, None, block_of(out_ref, 0))
@@ -276,6 +276,16 @@
             name=name,
         )(*flat)
 
+    even = [(r, ((r // CORES) ^ 1) * CORES + r % CORES) for r in range(region_count)]
+    odd = []
+    for z in range(1, layers - 1):
+        other = z + 1 if z % 2 else z - 1
+        odd += [(z * CORES + c, other * CORES + c) for c in range(CORES)]
+    for z in (0, layers - 1):
+        odd += [(z * CORES + c, z * CORES + (c ^ 1)) for c in range(CORES)]
+
+    early = lax.ppermute(requests, "region", even)
+
     swap = [(r, r ^ 1) for r in range(region_count)]
     block_flops = 2 * block_rows * crop_count * feat_width
     part = functools.partial
@@ -287,7 +297,7 @@
         part(away_first_kernel, layers, block_rows),
         "away_first",
         payloads(1),
-        (labels, features),
+        (labels, features, early),
         block_flops,
     )
     came_first = lax.ppermute(away_first, "region", swap)
@@ -320,14 +330,6 @@
 
     def fetch(k, step, block):
         blocks[k] = lax.ppermute(block, "group", [(g, g ^ step) for g in range(group_count)])
-
-    even = [(r, ((r // CORES) ^ 1) * CORES + r % CORES) for r in range(region_count)]
-    odd = []
-    for z in range(1, layers - 1):
-        other = z + 1 if z % 2 else z - 1
-        odd += [(z * CORES + c, other * CORES + c) for c in range(CORES)]
-    for z in (0, layers - 1):
-        odd += [(z * CORES + c, z * CORES + (c ^ 1)) for c in range(CORES)]
 
     def joined(hop, is_odd, came):
         return call(

time: 47 us -> 50.7 us (1.079)
  waiting for transfers between devices: 23.1 us -> 26.3 us
    ppermute x0 -> x1, waiting for transfers between devices: none -> 3.22 us  [on_device(): early = lax.ppermute(requests, 'region', even)]
    ppermute x0 -> x1, starting transfers between devices: none -> 0.51 us  [on_device(): early = lax.ppermute(requests, 'region', even)]
  transfers between devices with their start and end apart: 12 -> 13, of which waited for: 8 -> 9; matrix products, arithmetic and copies ran while one was open for 0% -> 0% of each run, Pallas kernels for 16% -> 15%
where the time goes in v4:
time: 50.7 us; the launch traced here: 50.5 us
  waiting for transfers between devices  26.3 us (52%)
  starting transfers between devices  12 us (24%)
  Pallas kernels  9.39 us (19%)
  local copies, waits for them, and re-layouts  2.11 us (4%)
  between operations  0.74 us (1%)
    pallas_call x10, Pallas kernels, call(): pl.pallas_call(kernel, out_shape=out_shape, in_specs=specs, out_specs=[VM...  9.39 us
    ppermute x2, waiting for transfers between devices, on_device(): even_came = [lax.ppermute(x, 'region', even) for x in first]  7.18 us
    ppermute x2, waiting for transfers between devices, on_device(): odd_came.append(lax.ppermute(leaves, 'region', odd))  4.16 us
    ppermute x1, waiting for transfers between devices, on_device(): even_came = [lax.ppermute(even_next, 'region', even)]  4.02 us
    ppermute x1, waiting for transfers between devices, on_device(): even_came = [lax.ppermute(second, 'region', even)]  3.68 us
    ppermute x3, starting transfers between devices, fetch(): lax.ppermute(block, 'group', [(g, g ^ step) for g in range(group_count)])  3.64 us
    ppermute x2, starting transfers between devices, on_device(): odd_came.append(lax.ppermute(leaves, 'region', odd))  3.29 us
    ppermute x1, waiting for transfers between devices, on_device(): early = lax.ppermute(requests, 'region', even)  3.22 us
  transfers between devices with their start and end apart: 13, of which 9 were waited for; matrix products, arithmetic and copies ran while one was open for 0% of the time, Pallas kernels for 15%

profile of v4, /device:TPU:10, one launch (start us, length us, event | category | flops | bytes accessed | tf_op | source)
XLA Modules:
  0.0 50.5 jit_solution(15912714679578627145)
XLA Ops:
  0.6 0.5 %collective-permute-start = (s32[1,2]{1,0:T(1,128)}, s32[1,2]{1,0:T(1,128)S(1)}, u32[]{:S(2)}, u32[]{:S(2)}) collective-permute-start(s32[1,2]{1,0:T(1,128)} %requests_ref.1), channel_id=1, source_target_pairs={{0,8},{4,12},{8,0},{12,4},{16,24},{20,28},{24,16},{28,20},{1,9},{5... | collective-permute-start | bytes 32 | tf_op jit(solution)/shard_map/ppermute | solution.py:287
  1.1 3.2 %collective-permute-done.early_ref = s32[1,2]{1,0:T(1,128)S(1)} collective-permute-done((s32[1,2]{1,0:T(1,128)}, s32[1,2]{1,0:T(1,128)S(1)}, u32[]{:S(2)}, u32[]{:S(2)}) %collective-permute-start) | collective-permute-done | bytes 40 | tf_op jit(solution)/shard_map/ppermute | solution.py:287
  4.4 0.0 copy-start
  4.4 1.4 %copy-done = bf16[384,2048]{1,0:T(8,128)(2,1)S(1)} copy-done((bf16[384,2048]{1,0:T(8,128)(2,1)S(1)}, bf16[384,2048]{1,0:T(8,128)(2,1)}, u32[]{:S(2)}) %copy-start) | copy-done | bytes 1572888
  5.8 0.0 copy-start.3
  5.8 0.7 %copy-done.3 = s32[1,384]{1,0:T(1,128)S(1)} copy-done((s32[1,384]{1,0:T(1,128)S(1)}, s32[1,384]{1,0:T(1,128)}, u32[]{:S(2)}) %copy-start.3) | copy-done | bytes 1560
  6.5 0.4 away_first.1
  6.9 0.1 collective-permute-start.1
  7.0 1.4 %away_rest.1 = bf16[3,2,1040,128]{3,2,1,0:T(8,128)(2,1)S(1)} custom-call(s32[1,384]{1,0:T(1,128)S(1)} %copy-done.3, bf16[384,2048]{1,0:T(8,128)(2,1)S(1)} %copy-done), custom_call_target="tpu_custom_call" | custom-call | flops 603979776 | bytes 3171072 | tf_op jit(solution)/shard_map/away_rest/pallas_call | solution.py:264
  8.4 0.0 copy-start.2
  8.4 0.5 %collective-permute-done.1.came_ref = bf16[1,2,1040,128]{3,2,1,0:T(8,128)(2,1)S(1)} collective-permute-done((bf16[1,2,1040,128]{3,2,1,0:T(8,128)(2,1)S(1)}, bf16[1,2,1040,128]{3,2,1,0:T(8,128)(2,1)S(1)}, u32[]{:S(2)}, u32[]{:S(2)}) %collective-permute-start.1) | collective-permute-done | bytes 532512 | tf_op jit(solution)/shard_map/ppermute | solution.py:303
  8.9 0.1 collective-permute-start.7
  9.0 0.4 chip_first.1
  9.5 0.5 %collective-permute-start.4 = (bf16[1040,128]{1,0:T(8,128)(2,1)S(1)}, bf16[1040,128]{1,0:T(8,128)(2,1)S(1)}, u32[]{:S(2)}, u32[]{:S(2)}) collective-permute-start(bf16[1040,128]{1,0:T(8,128)(2,1)S(1)} %get-tuple-element.21.mine_ref.refs_0_), channel_id=1, source_target_pairs={{0,8},{4,12},{8,0},{12,4},{16,24},{20,28},{24,16},{28,20},{1,9},{5... | collective-permute-start | bytes 798728 | tf_op jit(solution)/shard_map/ppermute | solution.py:343
  10.0 0.0 copy-done.2
  10.0 0.2 collective-permute-start.2
  10.2 1.9 %collective-permute-start.3 = (bf16[128,2048]{1,0:T(8,128)(2,1)S(1)}, bf16[128,2048]{1,0:T(8,128)(2,1)S(1)}, u32[]{:S(2)}, u32[]{:S(2)}) collective-permute-start(bf16[128,2048]{1,0:T(8,128)(2,1)S(1)} %copy-done.2), channel_id=1, source_target_pairs={{0,2},{1,3},{2,0},{3,1},{4,6},{5,7},{6,4},{7,5},{8,10},{9,11},{10,... | collective-permute-start | bytes 1572872 | tf_op jit(solution)/shard_map/ppermute | solution.py:332
  12.1 1.6 %collective-permute-start.8 = (bf16[1040,128]{1,0:T(8,128)(2,1)S(1)}, bf16[1040,128]{1,0:T(8,128)(2,1)S(1)}, u32[]{:S(2)}, u32[]{:S(2)}) collective-permute-start(bf16[1040,128]{1,0:T(8,128)(2,1)S(1)} %get-tuple-element.27.mine_ref.refs_1_), channel_id=1, source_target_pairs={{0,8},{4,12},{8,0},{12,4},{16,24},{20,28},{24,16},{28,20},{1,9},{5... | collective-permute-start | bytes 798728 | tf_op jit(solution)/shard_map/ppermute | solution.py:343
  13.7 0.0 collective-permute-done.7.came_ref
  13.7 1.4 %chip_rest.1 = (bf16[1,2,1040,128]{3,2,1,0:T(8,128)(2,1)S(1)}, bf16[3,2,1040,128]{3,2,1,0:T(8,128)(2,1)S(1)}) custom-call(s32[1,384]{1,0:T(1,128)S(1)} %copy-done.3, bf16[384,2048]{1,0:T(8,128)(2,1)S(1)} %copy-done, bf16[3,2,1040,128]{3,2,1,0:T(8,128)(2,1)S(1)} %collective-permute-done.7.came_ref), custom_call_target="tpu_custom_call" | custom-call | flops 603979776 | bytes 5300992 | tf_op jit(solution)/shard_map/chip_rest/pallas_call | solution.py:264
  15.1 0.5 %collective-permute-start.11 = (bf16[1,2,1040,128]{3,2,1,0:T(8,128)(2,1)S(1)}, bf16[1,2,1040,128]{3,2,1,0:T(8,128)(2,1)S(1)}, u32[]{:S(2)}, u32[]{:S(2)}) collective-permute-start(bf16[1,2,1040,128]{3,2,1,0:T(8,128)(2,1)S(1)} %get-tuple-element.29), channel_id=1, source_target_pairs={{0,8},{4,12},{8,0},{12,4},{16,24},{20,28},{24,16},{28,20},{1,9},{5... | collective-permute-start | bytes 1597448 | tf_op jit(solution)/shard_map/ppermute | solution.py:363
  15.6 3.2 %collective-permute-done.4.came_ref = bf16[1040,128]{1,0:T(8,128)(2,1)S(1)} collective-permute-done((bf16[1040,128]{1,0:T(8,128)(2,1)S(1)}, bf16[1040,128]{1,0:T(8,128)(2,1)S(1)}, u32[]{:S(2)}, u32[]{:S(2)}) %collective-permute-start.4) | collective-permute-done | bytes 266272 | tf_op jit(solution)/shard_map/ppermute | solution.py:343
  18.8 0.1 join_half.2
  18.9 1.6 %collective-permute-start.5 = (bf16[1040,128]{1,0:T(8,128)(2,1)S(1)}, bf16[1040,128]{1,0:T(8,128)(2,1)S(1)}, u32[]{:S(2)}, u32[]{:S(2)}) collective-permute-start(bf16[1040,128]{1,0:T(8,128)(2,1)S(1)} %join_half.2), channel_id=1, source_target_pairs={{8,16},{12,20},{16,8},{20,12},{0,4},{4,0},{24,28},{28,24},{9,17},{... | collective-permute-start | bytes 798728 | tf_op jit(solution)/shard_map/ppermute | solution.py:356
  20.5 4.0 %collective-permute-done.8.came_ref = bf16[1040,128]{1,0:T(8,128)(2,1)S(1)} collective-permute-done((bf16[1040,128]{1,0:T(8,128)(2,1)S(1)}, bf16[1040,128]{1,0:T(8,128)(2,1)S(1)}, u32[]{:S(2)}, u32[]{:S(2)}) %collective-permute-start.8) | collective-permute-done | bytes 266272 | tf_op jit(solution)/shard_map/ppermute | solution.py:343
  24.5 0.1 join_half.3
  24.6 1.6 %collective-permute-start.9 = (bf16[1040,128]{1,0:T(8,128)(2,1)S(1)}, bf16[1040,128]{1,0:T(8,128)(2,1)S(1)}, u32[]{:S(2)}, u32[]{:S(2)}) collective-permute-start(bf16[1040,128]{1,0:T(8,128)(2,1)S(1)} %join_half.3), channel_id=1, source_target_pairs={{8,16},{12,20},{16,8},{20,12},{0,4},{4,0},{24,28},{28,24},{9,17},{... | collective-permute-start | bytes 798728 | tf_op jit(solution)/shard_map/ppermute | solution.py:356
  26.2 0.0 collective-permute-done.2.rest_1_
  26.2 0.0 collective-permute-done.3.rest_2_
  26.2 0.0 collective-permute-done.5.refs_3_
  26.2 1.6 %collective-permute-start.6 = (bf16[128,2048]{1,0:T(8,128)(2,1)S(1)}, bf16[128,2048]{1,0:T(8,128)(2,1)S(1)}, u32[]{:S(2)}, u32[]{:S(2)}) collective-permute-start(bf16[128,2048]{1,0:T(8,128)(2,1)S(1)} %collective-permute-done.2.rest_1_), channel_id=1, source_target_pairs={{0,2},{1,3},{2,0},{3,1},{4,6},{5,7},{6,4},{7,5},{8,10},{9,11},{10,... | collective-permute-start | bytes 1572872 | tf_op jit(solution)/shard_map/ppermute | solution.py:332
  27.8 4.1 %collective-permute-done.9.refs_4_ = bf16[1040,128]{1,0:T(8,128)(2,1)S(1)} collective-permute-done((bf16[1040,128]{1,0:T(8,128)(2,1)S(1)}, bf16[1040,128]{1,0:T(8,128)(2,1)S(1)}, u32[]{:S(2)}, u32[]{:S(2)}) %collective-permute-start.9) | collective-permute-done | bytes 266272 | tf_op jit(solution)/shard_map/ppermute | solution.py:356
  31.9 0.2 join_even.1
  32.1 0.0 copy-start.1
  32.1 0.0 copy-start.4
  32.1 0.0 copy-start.5
  32.1 0.1 collective-permute-start.10
  32.2 3.7 %collective-permute-done.11.refs_3_ = bf16[1,2,1040,128]{3,2,1,0:T(8,128)(2,1)S(1)} collective-permute-done((bf16[1,2,1040,128]{3,2,1,0:T(8,128)(2,1)S(1)}, bf16[1,2,1040,128]{3,2,1,0:T(8,128)(2,1)S(1)}, u32[]{:S(2)}, u32[]{:S(2)}) %collective-permute-start.11) | collective-permute-done | bytes 532512 | tf_op jit(solution)/shard_map/ppermute | solution.py:363
  35.9 0.1 join_odd.1
  36.0 1.6 %collective-permute-start.12 = (bf16[1,2,1040,128]{3,2,1,0:T(8,128)(2,1)S(1)}, bf16[1,2,1040,128]{3,2,1,0:T(8,128)(2,1)S(1)}, u32[]{:S(2)}, u32[]{:S(2)}) collective-permute-start(bf16[1,2,1040,128]{3,2,1,0:T(8,128)(2,1)S(1)} %join_odd.1), channel_id=1, source_target_pairs={{8,16},{12,20},{16,8},{20,12},{0,4},{4,0},{24,28},{28,24},{9,17},{... | collective-permute-start | bytes 1597448 | tf_op jit(solution)/shard_map/ppermute | solution.py:368
  37.7 1.2 %collective-permute-done.6.rest_3_ = bf16[128,2048]{1,0:T(8,128)(2,1)S(1)} collective-permute-done((bf16[128,2048]{1,0:T(8,128)(2,1)S(1)}, bf16[128,2048]{1,0:T(8,128)(2,1)S(1)}, u32[]{:S(2)}, u32[]{:S(2)}) %collective-permute-start.6) | collective-permute-done | bytes 524320 | tf_op jit(solution)/shard_map/ppermute | solution.py:332
  38.9 0.0 copy-done.1
  38.9 0.0 copy-done.4
  38.9 0.0 copy-done.5
  38.9 3.9 %feat_grad.1 = bf16[384,2048]{1,0:T(8,128)(2,1)} custom-call(s32[1,2]{1,0:T(1,128)S(1)} %copy-done.4, s32[1,4]{1,0:T(1,128)S(1)} %copy-done.5, bf16[384,2048]{1,0:T(8,128)(2,1)S(1)} %copy-done.1, bf16[128,2048]{1,0:T(8,128)(2,1)S(1)} %copy-done.2, bf16[128,2048]{1,0:T(8,128)(2,1)S(1)} %collective-permute-done.2.rest_1_, ...), custom_call_target="tpu_custom_call" | custom-call | flops 805306368 | bytes 5242892 | tf_op jit(solution)/shard_map/feat_grad/pallas_call | solution.py:264
  42.7 4.0 %collective-permute-done.10.rest_0_ = bf16[1,2,1040,128]{3,2,1,0:T(8,128)(2,1)S(1)} collective-permute-done((bf16[1,2,1040,128]{3,2,1,0:T(8,128)(2,1)S(1)}, bf16[1,2,1040,128]{3,2,1,0:T(8,128)(2,1)S(1)}, u32[]{:S(2)}, u32[]{:S(2)}) %collective-permute-start.10) | collective-permute-done | bytes 532512 | tf_op jit(solution)/shard_map/ppermute | solution.py:367
  46.8 2.3 %collective-permute-done.12.rest_1_ = bf16[1,2,1040,128]{3,2,1,0:T(8,128)(2,1)S(1)} collective-permute-done((bf16[1,2,1040,128]{3,2,1,0:T(8,128)(2,1)S(1)}, bf16[1,2,1040,128]{3,2,1,0:T(8,128)(2,1)S(1)}, u32[]{:S(2)}, u32[]{:S(2)}) %collective-permute-start.12) | collective-permute-done | bytes 532512 | tf_op jit(solution)/shard_map/ppermute | solution.py:368
  49.1 1.4 %update.1 = bf16[128,2048]{1,0:T(8,128)(2,1)} custom-call(bf16[128,2048]{1,0:T(8,128)(2,1)S(1)} %copy-done.2, bf16[3,2,1040,128]{3,2,1,0:T(8,128)(2,1)S(1)} %get-tuple-element.26.refs_2_.rest_ref, bf16[1,2,1040,128]{3,2,1,0:T(8,128)(2,1)S(1)} %collective-permute-done.10.rest_0_, bf16[1,2,1040,128]{3,2,1,0:T(8,128)(2,1)S(1)} %collective-permute-done.12.rest_1_), custom_call_target="tpu_custom_call" | custom-call | flops 2621440 | bytes 3710976 | tf_op jit(solution)/shard_map/update/pallas_call | solution.py:264
Async XLA Ops:
  0.6 3.7 %collective-permute-start = (s32[1,2]{1,0:T(1,128)}, s32[1,2]{1,0:T(1,128)S(1)}, u32[]{:S(2)}, u32[]{:S(2)}) collective-permute-start(s32[1,2]{1,0:T(1,128)} %requests_ref.1), channel_id=1, source_target_pairs={{0,8},{4,12},{8,0},{12,4},{16,24},{20,28},{24,16},{28,20},{1,9},{5... | collective-permute-start | bytes 32 | tf_op jit(solution)/shard_map/ppermute | solution.py:287
  4.4 1.4 %copy-start = (bf16[384,2048]{1,0:T(8,128)(2,1)S(1)}, bf16[384,2048]{1,0:T(8,128)(2,1)}, u32[]{:S(2)}) copy-start(bf16[384,2048]{1,0:T(8,128)(2,1)} %features_ref.9) | copy-start | bytes 4718596
  5.8 0.7 %copy-start.3 = (s32[1,384]{1,0:T(1,128)S(1)}, s32[1,384]{1,0:T(1,128)}, u32[]{:S(2)}) copy-start(s32[1,384]{1,0:T(1,128)} %labels_ref.6) | copy-start | bytes 4612
  6.9 2.0 %collective-permute-start.1 = (bf16[1,2,1040,128]{3,2,1,0:T(8,128)(2,1)S(1)}, bf16[1,2,1040,128]{3,2,1,0:T(8,128)(2,1)S(1)}, u32[]{:S(2)}, u32[]{:S(2)}) collective-permute-start(bf16[1,2,1040,128]{3,2,1,0:T(8,128)(2,1)S(1)} %away_first.1), channel_id=1, source_target_pairs={{0,4},{4,0},{8,12},{12,8},{16,20},{20,16},{24,28},{28,24},{1,5},{5... | collective-permute-start | bytes 1597448 | tf_op jit(solution)/shard_map/ppermute | solution.py:303
  8.4 1.6 %copy-start.2 = (bf16[128,2048]{1,0:T(8,128)(2,1)S(1)}, bf16[128,2048]{1,0:T(8,128)(2,1)}, u32[]{:S(2)}) copy-start(bf16[128,2048]{1,0:T(8,128)(2,1)} %memory_ref.1) | copy-start | bytes 1572868
  8.9 4.8 %collective-permute-start.7 = (bf16[3,2,1040,128]{3,2,1,0:T(8,128)(2,1)S(1)}, bf16[3,2,1040,128]{3,2,1,0:T(8,128)(2,1)S(1)}, u32[]{:S(2)}, u32[]{:S(2)}) collective-permute-start(bf16[3,2,1040,128]{3,2,1,0:T(8,128)(2,1)S(1)} %away_rest.1), channel_id=1, source_target_pairs={{0,4},{4,0},{8,12},{12,8},{16,20},{20,16},{24,28},{28,24},{1,5},{5... | collective-permute-start | bytes 4792328 | tf_op jit(solution)/shard_map/ppermute | solution.py:325
  9.5 9.3 %collective-permute-start.4 = (bf16[1040,128]{1,0:T(8,128)(2,1)S(1)}, bf16[1040,128]{1,0:T(8,128)(2,1)S(1)}, u32[]{:S(2)}, u32[]{:S(2)}) collective-permute-start(bf16[1040,128]{1,0:T(8,128)(2,1)S(1)} %get-tuple-element.21.mine_ref.refs_0_), channel_id=1, source_target_pairs={{0,8},{4,12},{8,0},{12,4},{16,24},{20,28},{24,16},{28,20},{1,9},{5... | collective-permute-start | bytes 798728 | tf_op jit(solution)/shard_map/ppermute | solution.py:343
  10.0 16.2 %collective-permute-start.2 = (bf16[128,2048]{1,0:T(8,128)(2,1)S(1)}, bf16[128,2048]{1,0:T(8,128)(2,1)S(1)}, u32[]{:S(2)}, u32[]{:S(2)}) collective-permute-start(bf16[128,2048]{1,0:T(8,128)(2,1)S(1)} %copy-done.2), channel_id=1, source_target_pairs={{0,1},{1,0},{2,3},{3,2},{4,5},{5,4},{6,7},{7,6},{8,9},{9,8},{10,11... | collective-permute-start | bytes 1572872 | tf_op jit(solution)/shard_map/ppermute | solution.py:332
  10.2 16.0 %collective-permute-start.3 = (bf16[128,2048]{1,0:T(8,128)(2,1)S(1)}, bf16[128,2048]{1,0:T(8,128)(2,1)S(1)}, u32[]{:S(2)}, u32[]{:S(2)}) collective-permute-start(bf16[128,2048]{1,0:T(8,128)(2,1)S(1)} %copy-done.2), channel_id=1, source_target_pairs={{0,2},{1,3},{2,0},{3,1},{4,6},{5,7},{6,4},{7,5},{8,10},{9,11},{10,... | collective-permute-start | bytes 1572872 | tf_op jit(solution)/shard_map/ppermute | solution.py:332
  12.1 12.4 %collective-permute-start.8 = (bf16[1040,128]{1,0:T(8,128)(2,1)S(1)}, bf16[1040,128]{1,0:T(8,128)(2,1)S(1)}, u32[]{:S(2)}, u32[]{:S(2)}) collective-permute-start(bf16[1040,128]{1,0:T(8,128)(2,1)S(1)} %get-tuple-element.27.mine_ref.refs_1_), channel_id=1, source_target_pairs={{0,8},{4,12},{8,0},{12,4},{16,24},{20,28},{24,16},{28,20},{1,9},{5... | collective-permute-start | bytes 798728 | tf_op jit(solution)/shard_map/ppermute | solution.py:343
  15.1 20.8 %collective-permute-start.11 = (bf16[1,2,1040,128]{3,2,1,0:T(8,128)(2,1)S(1)}, bf16[1,2,1040,128]{3,2,1,0:T(8,128)(2,1)S(1)}, u32[]{:S(2)}, u32[]{:S(2)}) collective-permute-start(bf16[1,2,1040,128]{3,2,1,0:T(8,128)(2,1)S(1)} %get-tuple-element.29), channel_id=1, source_target_pairs={{0,8},{4,12},{8,0},{12,4},{16,24},{20,28},{24,16},{28,20},{1,9},{5... | collective-permute-start | bytes 1597448 | tf_op jit(solution)/shard_map/ppermute | solution.py:363
  18.9 7.4 %collective-permute-start.5 = (bf16[1040,128]{1,0:T(8,128)(2,1)S(1)}, bf16[1040,128]{1,0:T(8,128)(2,1)S(1)}, u32[]{:S(2)}, u32[]{:S(2)}) collective-permute-start(bf16[1040,128]{1,0:T(8,128)(2,1)S(1)} %join_half.2), channel_id=1, source_target_pairs={{8,16},{12,20},{16,8},{20,12},{0,4},{4,0},{24,28},{28,24},{9,17},{... | collective-permute-start | bytes 798728 | tf_op jit(solution)/shard_map/ppermute | solution.py:356
  24.6 7.4 %collective-permute-start.9 = (bf16[1040,128]{1,0:T(8,128)(2,1)S(1)}, bf16[1040,128]{1,0:T(8,128)(2,1)S(1)}, u32[]{:S(2)}, u32[]{:S(2)}) collective-permute-start(bf16[1040,128]{1,0:T(8,128)(2,1)S(1)} %join_half.3), channel_id=1, source_target_pairs={{8,16},{12,20},{16,8},{20,12},{0,4},{4,0},{24,28},{28,24},{9,17},{... | collective-permute-start | bytes 798728 | tf_op jit(solution)/shard_map/ppermute | solution.py:356
  26.2 12.6 %collective-permute-start.6 = (bf16[128,2048]{1,0:T(8,128)(2,1)S(1)}, bf16[128,2048]{1,0:T(8,128)(2,1)S(1)}, u32[]{:S(2)}, u32[]{:S(2)}) collective-permute-start(bf16[128,2048]{1,0:T(8,128)(2,1)S(1)} %collective-permute-done.2.rest_1_), channel_id=1, source_target_pairs={{0,2},{1,3},{2,0},{3,1},{4,6},{5,7},{6,4},{7,5},{8,10},{9,11},{10,... | collective-permute-start | bytes 1572872 | tf_op jit(solution)/shard_map/ppermute | solution.py:332
  32.1 6.7 %copy-start.1 = (bf16[384,2048]{1,0:T(8,128)(2,1)S(1)}, bf16[384,2048]{1,0:T(8,128)(2,1)}, u32[]{:S(2)}) copy-start(bf16[384,2048]{1,0:T(8,128)(2,1)} %features_ref.9) | copy-start | bytes 4718596
  32.1 6.7 %copy-start.4 = (s32[1,2]{1,0:T(1,128)S(1)}, s32[1,2]{1,0:T(1,128)}, u32[]{:S(2)}) copy-start(s32[1,2]{1,0:T(1,128)} %requests_ref.1) | copy-start | bytes 28
  32.1 6.7 %copy-start.5 = (s32[1,4]{1,0:T(1,128)S(1)}, s32[1,4]{1,0:T(1,128)}, u32[]{:S(2)}) copy-start(s32[1,4]{1,0:T(1,128)} %owners_ref.1) | copy-start | bytes 52
  32.1 14.6 %collective-permute-start.10 = (bf16[1,2,1040,128]{3,2,1,0:T(8,128)(2,1)S(1)}, bf16[1,2,1040,128]{3,2,1,0:T(8,128)(2,1)S(1)}, u32[]{:S(2)}, u32[]{:S(2)}) collective-permute-start(bf16[1,2,1040,128]{3,2,1,0:T(8,128)(2,1)S(1)} %join_even.1), channel_id=1, source_target_pairs={{0,8},{4,12},{8,0},{12,4},{16,24},{20,28},{24,16},{28,20},{1,9},{5... | collective-permute-start | bytes 1597448 | tf_op jit(solution)/shard_map/ppermute | solution.py:367
  36.0 13.1 %collective-permute-start.12 = (bf16[1,2,1040,128]{3,2,1,0:T(8,128)(2,1)S(1)}, bf16[1,2,1040,128]{3,2,1,0:T(8,128)(2,1)S(1)}, u32[]{:S(2)}, u32[]{:S(2)}) collective-permute-start(bf16[1,2,1040,128]{3,2,1,0:T(8,128)(2,1)S(1)} %join_odd.1), channel_id=1, source_target_pairs={{8,16},{12,20},{16,8},{20,12},{0,4},{4,0},{24,28},{28,24},{9,17},{... | collective-permute-start | bytes 1597448 | tf_op jit(solution)/shard_map/ppermute | solution.py:368

commit v5 on v3

--- a/solution.py
+++ b/solution.py
@@ -24,12 +24,16 @@
 PARAMS = pltpu.CompilerParams(vmem_limit_bytes=16 * 2**20)
 
 
+def match_of(base, labels_ref, block_rows):
+    value = base + lax.broadcasted_iota(jnp.int32, (block_rows, labels_ref.shape[1]), 0)
+    return jnp.where(labels_ref[...] == value, 1.0, 0.0).astype(jnp.bfloat16)
+
+
 def write_sums(base, labels_ref, features_ref, block_rows, came, store):
     crop_count, feat_width = features_ref.shape
     half_rows = block_rows // HALVES
     slabs = feat_width // LANES
-    value = base + lax.broadcasted_iota(jnp.int32, (block_rows, crop_count), 0)
-    match = jnp.where(labels_ref[...] == value, 1.0, 0.0).astype(jnp.bfloat16)
+    match = labels_ref[...] if base is None else match_of(base, labels_ref, block_rows)
 
     def put(h, first, part):
         if came is not None:
@@ -82,10 +86,13 @@
     return lambda h, first, rows: ref[(*at, h, pl.ds(first, rows), slice(None))]
 
 
-def away_first_kernel(layers, block_rows, labels_ref, features_ref, out_ref):
+def match_kernel(layers, block_rows, labels_ref, out_ref):
     core = 1 - lax.axis_index("region") % CORES
-    base = base_at(0, layers, core, block_rows)
-    write_sums(base, labels_ref, features_ref, block_rows, None, block_of(out_ref, 0))
+    out_ref[...] = match_of(base_at(0, layers, core, block_rows), labels_ref, block_rows)
+
+
+def away_first_kernel(block_rows, match_ref, features_ref, out_ref):
+    write_sums(None, match_ref, features_ref, block_rows, None, block_of(out_ref, 0))
 
 
 def away_rest_kernel(layers, block_rows, labels_ref, features_ref, out_ref):
@@ -166,7 +173,8 @@
 def update_kernel(layers, memory_ref, rest_ref, *rest):
     layer = lax.axis_index("region") // CORES
     place = jnp.where(layer < layers // 2, layers - 1 - layer, layer) - 1
-    came_refs, out_ref, mixed_ref = rest[:-2], rest[-2], rest[-1]
+    came_refs, (out_hbm, mixed_ref, out_ref, sems) = rest[:-4], rest[-4:]
+    copies = []
     linked = has_odd(layers)
     block_rows, feat_width = memory_ref.shape
     half_rows = block_rows // HALVES
@@ -197,7 +205,14 @@
             squares = squares + mixed * mixed
         mean = jnp.sum(squares, axis=1, keepdims=True) * (1.0 / feat_width)
         scale = lax.rsqrt(mean + 1e-06) * D ** (-0.5)
-        out_ref[pl.ds(h * half_rows, half_rows), :] = (mixed_ref[...] * scale).astype(jnp.bfloat16)
+        rows = pl.ds(h * half_rows, half_rows)
+        out_ref[rows, :] = (mixed_ref[...] * scale).astype(jnp.bfloat16)
+        copies.append(
+            pltpu.make_async_copy(out_ref.at[rows, :], out_hbm.at[rows, :], sems.at[h])
+        )
+        copies[h].start()
+    for copy in copies:
+        copy.wait()
 
 
 def grad_kernel(requests_ref, owners_ref, features_ref, *rest):
@@ -255,17 +270,18 @@
     bf16 = jnp.bfloat16
     after = lax.optimization_barrier
 
-    def call(kernel, name, out_shape, operands, flops, scratch=(), smem=0, any_from=None):
+    def call(kernel, name, out_shape, operands, flops, scratch=(), smem=0, any_from=None, out_from_vmem=True):
         outs = out_shape if isinstance(out_shape, list) else [out_shape]
         flat, tree = jax.tree.flatten(operands)
         specs = [SMEM if i < smem else VMEM for i in range(len(flat))]
         if any_from is not None:
             specs[any_from:] = [pl.BlockSpec(memory_space=pl.ANY)] * (len(flat) - any_from)
+        out_spec = VMEM if out_from_vmem else pl.BlockSpec(memory_space=pl.ANY)
         return pl.pallas_call(
             kernel,
             out_shape=out_shape,
             in_specs=specs,
-            out_specs=[VMEM] * len(outs) if isinstance(out_shape, list) else VMEM,
+            out_specs=[out_spec] * len(outs) if isinstance(out_shape, list) else out_spec,
             scratch_shapes=list(scratch),
             compiler_params=PARAMS,
             cost_estimate=pl.CostEstimate(
@@ -283,11 +299,18 @@
     def payloads(count):
         return jax.ShapeDtypeStruct((count, HALVES, pay_rows, LANES), bf16)
 
+    match_first = call(
+        part(match_kernel, layers, block_rows),
+        "match_first",
+        jax.ShapeDtypeStruct((block_rows, crop_count), bf16),
+        (labels,),
+        10**9,
+    )
     away_first = call(
-        part(away_first_kernel, layers, block_rows),
+        part(away_first_kernel, block_rows),
         "away_first",
         payloads(1),
-        (labels, features),
+        (match_first, features),
         block_flops,
     )
     came_first = lax.ppermute(away_first, "region", swap)
@@ -386,7 +409,12 @@
         jax.ShapeDtypeStruct(memory.shape, bf16),
         (memory, rest, *even_came, *odd_came),
         10 * block_rows * feat_width,
-        scratch=(pltpu.VMEM((half_rows, feat_width), jnp.float32),),
+        scratch=(
+            pltpu.VMEM((half_rows, feat_width), jnp.float32),
+            pltpu.VMEM(memory.shape, bf16),
+            pltpu.SemaphoreType.DMA((HALVES,)),
+        ),
+        out_from_vmem=False,
     )
     return (feat_grad, new_memory)
 

time: 47 us -> 46.3 us (0.985)
  local copies, waits for them, and re-layouts: 2.11 us -> 1.52 us
    unnamed x12, local copies, waits for them, and re-layouts: 2.11 us -> 1.52 us
    pallas_call x10 -> x11, Pallas kernels: 9.37 us -> 9.36 us  [call(): pl.pallas_call(kernel, out_shape=out_shape, in_specs=specs, out_specs=[ou...]
where the time goes in v5:
time: 46.3 us; the launch traced here: 46.1 us
  waiting for transfers between devices  23.1 us (50%)
  starting transfers between devices  11.4 us (25%)
  Pallas kernels  9.36 us (20%)
  local copies, waits for them, and re-layouts  1.52 us (3%)
  between operations  0.75 us (2%)
    pallas_call x11, Pallas kernels, call(): pl.pallas_call(kernel, out_shape=out_shape, in_specs=specs, out_specs=[ou...  9.36 us
    ppermute x2, waiting for transfers between devices, on_device(): even_came = [lax.ppermute(x, 'region', even) for x in first]  7.2 us
    ppermute x2, waiting for transfers between devices, on_device(): odd_came.append(lax.ppermute(leaves, 'region', odd))  4.19 us
    ppermute x1, waiting for transfers between devices, on_device(): even_came = [lax.ppermute(even_next, 'region', even)]  4.07 us
    ppermute x1, waiting for transfers between devices, on_device(): even_came = [lax.ppermute(second, 'region', even)]  3.69 us
    ppermute x3, starting transfers between devices, fetch(): lax.ppermute(block, 'group', [(g, g ^ step) for g in range(group_count)])  3.62 us
    ppermute x2, starting transfers between devices, on_device(): odd_came.append(lax.ppermute(leaves, 'region', odd))  3.23 us
    ppermute x1, waiting for transfers between devices, on_device(): odd_came = [lax.ppermute(odd_next, 'region', odd)]  2.35 us
  transfers between devices with their start and end apart: 12, of which 8 were waited for; matrix products, arithmetic and copies ran while one was open for 0% of the time, Pallas kernels for 16%

profile of v5, /device:TPU:10, one launch (start us, length us, event | category | flops | bytes accessed | tf_op | source)
XLA Modules:
  0.0 46.1 jit_solution(9734675319016819445)
XLA Ops:
  0.6 0.0 copy-start
  0.6 0.0 copy-start.2
  0.7 0.8 %copy-done.2 = s32[1,384]{1,0:T(1,128)S(1)} copy-done((s32[1,384]{1,0:T(1,128)S(1)}, s32[1,384]{1,0:T(1,128)}, u32[]{:S(2)}) %copy-start.2) | copy-done | bytes 1560
  1.5 0.6 %copy-done = bf16[384,2048]{1,0:T(8,128)(2,1)S(1)} copy-done((bf16[384,2048]{1,0:T(8,128)(2,1)S(1)}, bf16[384,2048]{1,0:T(8,128)(2,1)}, u32[]{:S(2)}) %copy-start) | copy-done | bytes 1572888
  2.1 0.0 copy-start.3
  2.1 0.5 %away_first.1 = bf16[1,2,1040,128]{3,2,1,0:T(8,128)(2,1)S(1)} custom-call(bf16[128,384]{1,0:T(8,128)(2,1)S(1)} %match_first.1.match_ref, bf16[384,2048]{1,0:T(8,128)(2,1)S(1)} %copy-done), custom_call_target="tpu_custom_call" | custom-call | flops 201326592 | bytes 2203648 | tf_op jit(solution)/shard_map/away_first/pallas_call | solution.py:280
  2.5 0.1 collective-permute-start
  2.6 0.1 copy-done.3
  2.7 1.3 %away_rest.1 = bf16[3,2,1040,128]{3,2,1,0:T(8,128)(2,1)S(1)} custom-call(s32[1,384]{1,0:T(1,128)S(1)} %copy-done.3, bf16[384,2048]{1,0:T(8,128)(2,1)S(1)} %copy-done), custom_call_target="tpu_custom_call" | custom-call | flops 603979776 | bytes 3171072 | tf_op jit(solution)/shard_map/away_rest/pallas_call | solution.py:280
  4.1 0.0 copy-start.1
  4.1 0.4 collective-permute-done.came_ref
  4.5 0.1 collective-permute-start.6
  4.7 0.4 chip_first.1
  5.1 0.5 %collective-permute-start.3 = (bf16[1040,128]{1,0:T(8,128)(2,1)S(1)}, bf16[1040,128]{1,0:T(8,128)(2,1)S(1)}, u32[]{:S(2)}, u32[]{:S(2)}) collective-permute-start(bf16[1040,128]{1,0:T(8,128)(2,1)S(1)} %get-tuple-element.21.mine_ref.refs_0_), channel_id=1, source_target_pairs={{0,8},{4,12},{8,0},{12,4},{16,24},{20,28},{24,16},{28,20},{1,9},{5... | collective-permute-start | bytes 798728 | tf_op jit(solution)/shard_map/ppermute | solution.py:364
  5.7 0.0 copy-done.1
  5.7 0.1 collective-permute-start.1
  5.8 1.9 %collective-permute-start.2 = (bf16[128,2048]{1,0:T(8,128)(2,1)S(1)}, bf16[128,2048]{1,0:T(8,128)(2,1)S(1)}, u32[]{:S(2)}, u32[]{:S(2)}) collective-permute-start(bf16[128,2048]{1,0:T(8,128)(2,1)S(1)} %copy-done.1), channel_id=1, source_target_pairs={{0,2},{1,3},{2,0},{3,1},{4,6},{5,7},{6,4},{7,5},{8,10},{9,11},{10,... | collective-permute-start | bytes 1572872 | tf_op jit(solution)/shard_map/ppermute | solution.py:345
  7.7 1.5 %collective-permute-start.7 = (bf16[1040,128]{1,0:T(8,128)(2,1)S(1)}, bf16[1040,128]{1,0:T(8,128)(2,1)S(1)}, u32[]{:S(2)}, u32[]{:S(2)}) collective-permute-start(bf16[1040,128]{1,0:T(8,128)(2,1)S(1)} %get-tuple-element.27.mine_ref.refs_1_), channel_id=1, source_target_pairs={{0,8},{4,12},{8,0},{12,4},{16,24},{20,28},{24,16},{28,20},{1,9},{5... | collective-permute-start | bytes 798728 | tf_op jit(solution)/shard_map/ppermute | solution.py:364
  9.3 0.0 collective-permute-done.6.came_ref
  9.3 1.4 %chip_rest.1 = (bf16[1,2,1040,128]{3,2,1,0:T(8,128)(2,1)S(1)}, bf16[3,2,1040,128]{3,2,1,0:T(8,128)(2,1)S(1)}) custom-call(s32[1,384]{1,0:T(1,128)S(1)} %copy-done.3, bf16[384,2048]{1,0:T(8,128)(2,1)S(1)} %copy-done, bf16[3,2,1040,128]{3,2,1,0:T(8,128)(2,1)S(1)} %collective-permute-done.6.came_ref), custom_call_target="tpu_custom_call" | custom-call | flops 603979776 | bytes 5300992 | tf_op jit(solution)/shard_map/chip_rest/pallas_call | solution.py:280
  10.7 0.6 %collective-permute-start.10 = (bf16[1,2,1040,128]{3,2,1,0:T(8,128)(2,1)S(1)}, bf16[1,2,1040,128]{3,2,1,0:T(8,128)(2,1)S(1)}, u32[]{:S(2)}, u32[]{:S(2)}) collective-permute-start(bf16[1,2,1040,128]{3,2,1,0:T(8,128)(2,1)S(1)} %get-tuple-element.29), channel_id=1, source_target_pairs={{0,8},{4,12},{8,0},{12,4},{16,24},{20,28},{24,16},{28,20},{1,9},{5... | collective-permute-start | bytes 1597448 | tf_op jit(solution)/shard_map/ppermute | solution.py:384
  11.2 3.2 %collective-permute-done.3.came_ref = bf16[1040,128]{1,0:T(8,128)(2,1)S(1)} collective-permute-done((bf16[1040,128]{1,0:T(8,128)(2,1)S(1)}, bf16[1040,128]{1,0:T(8,128)(2,1)S(1)}, u32[]{:S(2)}, u32[]{:S(2)}) %collective-permute-start.3) | collective-permute-done | bytes 266272 | tf_op jit(solution)/shard_map/ppermute | solution.py:364
  14.4 0.1 join_half.2
  14.5 1.6 %collective-permute-start.4 = (bf16[1040,128]{1,0:T(8,128)(2,1)S(1)}, bf16[1040,128]{1,0:T(8,128)(2,1)S(1)}, u32[]{:S(2)}, u32[]{:S(2)}) collective-permute-start(bf16[1040,128]{1,0:T(8,128)(2,1)S(1)} %join_half.2), channel_id=1, source_target_pairs={{8,16},{12,20},{16,8},{20,12},{0,4},{4,0},{24,28},{28,24},{9,17},{... | collective-permute-start | bytes 798728 | tf_op jit(solution)/shard_map/ppermute | solution.py:377
  16.1 4.0 %collective-permute-done.7.came_ref = bf16[1040,128]{1,0:T(8,128)(2,1)S(1)} collective-permute-done((bf16[1040,128]{1,0:T(8,128)(2,1)S(1)}, bf16[1040,128]{1,0:T(8,128)(2,1)S(1)}, u32[]{:S(2)}, u32[]{:S(2)}) %collective-permute-start.7) | collective-permute-done | bytes 266272 | tf_op jit(solution)/shard_map/ppermute | solution.py:364
  20.1 0.1 join_half.3
  20.2 1.6 %collective-permute-start.8 = (bf16[1040,128]{1,0:T(8,128)(2,1)S(1)}, bf16[1040,128]{1,0:T(8,128)(2,1)S(1)}, u32[]{:S(2)}, u32[]{:S(2)}) collective-permute-start(bf16[1040,128]{1,0:T(8,128)(2,1)S(1)} %join_half.3), channel_id=1, source_target_pairs={{8,16},{12,20},{16,8},{20,12},{0,4},{4,0},{24,28},{28,24},{9,17},{... | collective-permute-start | bytes 798728 | tf_op jit(solution)/shard_map/ppermute | solution.py:377
  21.8 0.0 collective-permute-done.1.rest_1_
  21.8 0.0 collective-permute-done.2.rest_2_
  21.8 0.0 collective-permute-done.4.refs_3_
  21.9 1.6 %collective-permute-start.5 = (bf16[128,2048]{1,0:T(8,128)(2,1)S(1)}, bf16[128,2048]{1,0:T(8,128)(2,1)S(1)}, u32[]{:S(2)}, u32[]{:S(2)}) collective-permute-start(bf16[128,2048]{1,0:T(8,128)(2,1)S(1)} %collective-permute-done.1.rest_1_), channel_id=1, source_target_pairs={{0,2},{1,3},{2,0},{3,1},{4,6},{5,7},{6,4},{7,5},{8,10},{9,11},{10,... | collective-permute-start | bytes 1572872 | tf_op jit(solution)/shard_map/ppermute | solution.py:345
  23.4 4.1 %collective-permute-done.8.refs_4_ = bf16[1040,128]{1,0:T(8,128)(2,1)S(1)} collective-permute-done((bf16[1040,128]{1,0:T(8,128)(2,1)S(1)}, bf16[1040,128]{1,0:T(8,128)(2,1)S(1)}, u32[]{:S(2)}, u32[]{:S(2)}) %collective-permute-start.8) | collective-permute-done | bytes 266272 | tf_op jit(solution)/shard_map/ppermute | solution.py:377
  27.6 0.2 join_even.1
  27.7 0.0 copy-start.4
  27.8 0.0 copy-start.5
  27.8 0.1 collective-permute-start.9
  27.8 3.7 %collective-permute-done.10.refs_3_ = bf16[1,2,1040,128]{3,2,1,0:T(8,128)(2,1)S(1)} collective-permute-done((bf16[1,2,1040,128]{3,2,1,0:T(8,128)(2,1)S(1)}, bf16[1,2,1040,128]{3,2,1,0:T(8,128)(2,1)S(1)}, u32[]{:S(2)}, u32[]{:S(2)}) %collective-permute-start.10) | collective-permute-done | bytes 532512 | tf_op jit(solution)/shard_map/ppermute | solution.py:384
  31.5 0.1 join_odd.1
  31.7 1.6 %collective-permute-start.11 = (bf16[1,2,1040,128]{3,2,1,0:T(8,128)(2,1)S(1)}, bf16[1,2,1040,128]{3,2,1,0:T(8,128)(2,1)S(1)}, u32[]{:S(2)}, u32[]{:S(2)}) collective-permute-start(bf16[1,2,1040,128]{3,2,1,0:T(8,128)(2,1)S(1)} %join_odd.1), channel_id=1, source_target_pairs={{8,16},{12,20},{16,8},{20,12},{0,4},{4,0},{24,28},{28,24},{9,17},{... | collective-permute-start | bytes 1597448 | tf_op jit(solution)/shard_map/ppermute | solution.py:389
  33.3 1.2 %collective-permute-done.5.rest_3_ = bf16[128,2048]{1,0:T(8,128)(2,1)S(1)} collective-permute-done((bf16[128,2048]{1,0:T(8,128)(2,1)S(1)}, bf16[128,2048]{1,0:T(8,128)(2,1)S(1)}, u32[]{:S(2)}, u32[]{:S(2)}) %collective-permute-start.5) | collective-permute-done | bytes 524320 | tf_op jit(solution)/shard_map/ppermute | solution.py:345
  34.4 0.0 copy-done.4
  34.4 0.0 copy-done.5
  34.4 3.9 %feat_grad.1 = bf16[384,2048]{1,0:T(8,128)(2,1)} custom-call(s32[1,2]{1,0:T(1,128)S(1)} %copy-done.4, s32[1,4]{1,0:T(1,128)S(1)} %copy-done.5, bf16[384,2048]{1,0:T(8,128)(2,1)S(1)} %copy-done, bf16[128,2048]{1,0:T(8,128)(2,1)S(1)} %copy-done.1, bf16[128,2048]{1,0:T(8,128)(2,1)S(1)} %collective-permute-done.1.rest_1_, ...), custom_call_target="tpu_custom_call" | custom-call | flops 805306368 | bytes 5242892 | tf_op jit(solution)/shard_map/feat_grad/pallas_call | solution.py:280
  38.3 4.1 %collective-permute-done.9.rest_0_ = bf16[1,2,1040,128]{3,2,1,0:T(8,128)(2,1)S(1)} collective-permute-done((bf16[1,2,1040,128]{3,2,1,0:T(8,128)(2,1)S(1)}, bf16[1,2,1040,128]{3,2,1,0:T(8,128)(2,1)S(1)}, u32[]{:S(2)}, u32[]{:S(2)}) %collective-permute-start.9) | collective-permute-done | bytes 532512 | tf_op jit(solution)/shard_map/ppermute | solution.py:388
  42.4 2.3 %collective-permute-done.11.rest_1_ = bf16[1,2,1040,128]{3,2,1,0:T(8,128)(2,1)S(1)} collective-permute-done((bf16[1,2,1040,128]{3,2,1,0:T(8,128)(2,1)S(1)}, bf16[1,2,1040,128]{3,2,1,0:T(8,128)(2,1)S(1)}, u32[]{:S(2)}, u32[]{:S(2)}) %collective-permute-start.11) | collective-permute-done | bytes 532512 | tf_op jit(solution)/shard_map/ppermute | solution.py:389
  44.7 1.4 %update.1 = bf16[128,2048]{1,0:T(8,128)(2,1)} custom-call(bf16[128,2048]{1,0:T(8,128)(2,1)S(1)} %copy-done.1, bf16[3,2,1040,128]{3,2,1,0:T(8,128)(2,1)S(1)} %get-tuple-element.26.refs_2_.rest_ref, bf16[1,2,1040,128]{3,2,1,0:T(8,128)(2,1)S(1)} %collective-permute-done.9.rest_0_, bf16[1,2,1040,128]{3,2,1,0:T(8,128)(2,1)S(1)} %collective-permute-done.11.rest_1_), custom_call_target="tpu_custom_call" | custom-call | flops 2621440 | bytes 3710976 | tf_op jit(solution)/shard_map/update/pallas_call | solution.py:280
  (1 shorter events, 0.0 us)
Async XLA Ops:
  0.6 1.4 %copy-start = (bf16[384,2048]{1,0:T(8,128)(2,1)S(1)}, bf16[384,2048]{1,0:T(8,128)(2,1)}, u32[]{:S(2)}) copy-start(bf16[384,2048]{1,0:T(8,128)(2,1)} %features_ref.9) | copy-start | bytes 4718596
  0.6 0.8 %copy-start.2 = (s32[1,384]{1,0:T(1,128)S(1)}, s32[1,384]{1,0:T(1,128)}, u32[]{:S(2)}) copy-start(s32[1,384]{1,0:T(1,128)} %labels_ref.6) | copy-start | bytes 4612
  2.1 0.7 %copy-start.3 = (s32[1,384]{1,0:T(1,128)S(1)}, s32[1,384]{1,0:T(1,128)}, u32[]{:S(2)}) copy-start(s32[1,384]{1,0:T(1,128)} %labels_ref.6) | copy-start | bytes 4612
  2.5 2.0 %collective-permute-start = (bf16[1,2,1040,128]{3,2,1,0:T(8,128)(2,1)S(1)}, bf16[1,2,1040,128]{3,2,1,0:T(8,128)(2,1)S(1)}, u32[]{:S(2)}, u32[]{:S(2)}) collective-permute-start(bf16[1,2,1040,128]{3,2,1,0:T(8,128)(2,1)S(1)} %away_first.1), channel_id=1, source_target_pairs={{0,4},{4,0},{8,12},{12,8},{16,20},{20,16},{24,28},{28,24},{1,5},{5... | collective-permute-start | bytes 1597448 | tf_op jit(solution)/shard_map/ppermute | solution.py:316
  4.1 1.6 %copy-start.1 = (bf16[128,2048]{1,0:T(8,128)(2,1)S(1)}, bf16[128,2048]{1,0:T(8,128)(2,1)}, u32[]{:S(2)}) copy-start(bf16[128,2048]{1,0:T(8,128)(2,1)} %memory_ref.1) | copy-start | bytes 1572868
  4.5 4.7 %collective-permute-start.6 = (bf16[3,2,1040,128]{3,2,1,0:T(8,128)(2,1)S(1)}, bf16[3,2,1040,128]{3,2,1,0:T(8,128)(2,1)S(1)}, u32[]{:S(2)}, u32[]{:S(2)}) collective-permute-start(bf16[3,2,1040,128]{3,2,1,0:T(8,128)(2,1)S(1)} %away_rest.1), channel_id=1, source_target_pairs={{0,4},{4,0},{8,12},{12,8},{16,20},{20,16},{24,28},{28,24},{1,5},{5... | collective-permute-start | bytes 4792328 | tf_op jit(solution)/shard_map/ppermute | solution.py:338
  5.1 9.3 %collective-permute-start.3 = (bf16[1040,128]{1,0:T(8,128)(2,1)S(1)}, bf16[1040,128]{1,0:T(8,128)(2,1)S(1)}, u32[]{:S(2)}, u32[]{:S(2)}) collective-permute-start(bf16[1040,128]{1,0:T(8,128)(2,1)S(1)} %get-tuple-element.21.mine_ref.refs_0_), channel_id=1, source_target_pairs={{0,8},{4,12},{8,0},{12,4},{16,24},{20,28},{24,16},{28,20},{1,9},{5... | collective-permute-start | bytes 798728 | tf_op jit(solution)/shard_map/ppermute | solution.py:364
  5.7 16.2 %collective-permute-start.1 = (bf16[128,2048]{1,0:T(8,128)(2,1)S(1)}, bf16[128,2048]{1,0:T(8,128)(2,1)S(1)}, u32[]{:S(2)}, u32[]{:S(2)}) collective-permute-start(bf16[128,2048]{1,0:T(8,128)(2,1)S(1)} %copy-done.1), channel_id=1, source_target_pairs={{0,1},{1,0},{2,3},{3,2},{4,5},{5,4},{6,7},{7,6},{8,9},{9,8},{10,11... | collective-permute-start | bytes 1572872 | tf_op jit(solution)/shard_map/ppermute | solution.py:345
  5.8 16.0 %collective-permute-start.2 = (bf16[128,2048]{1,0:T(8,128)(2,1)S(1)}, bf16[128,2048]{1,0:T(8,128)(2,1)S(1)}, u32[]{:S(2)}, u32[]{:S(2)}) collective-permute-start(bf16[128,2048]{1,0:T(8,128)(2,1)S(1)} %copy-done.1), channel_id=1, source_target_pairs={{0,2},{1,3},{2,0},{3,1},{4,6},{5,7},{6,4},{7,5},{8,10},{9,11},{10,... | collective-permute-start | bytes 1572872 | tf_op jit(solution)/shard_map/ppermute | solution.py:345
  7.7 12.4 %collective-permute-start.7 = (bf16[1040,128]{1,0:T(8,128)(2,1)S(1)}, bf16[1040,128]{1,0:T(8,128)(2,1)S(1)}, u32[]{:S(2)}, u32[]{:S(2)}) collective-permute-start(bf16[1040,128]{1,0:T(8,128)(2,1)S(1)} %get-tuple-element.27.mine_ref.refs_1_), channel_id=1, source_target_pairs={{0,8},{4,12},{8,0},{12,4},{16,24},{20,28},{24,16},{28,20},{1,9},{5... | collective-permute-start | bytes 798728 | tf_op jit(solution)/shard_map/ppermute | solution.py:364
  10.7 20.9 %collective-permute-start.10 = (bf16[1,2,1040,128]{3,2,1,0:T(8,128)(2,1)S(1)}, bf16[1,2,1040,128]{3,2,1,0:T(8,128)(2,1)S(1)}, u32[]{:S(2)}, u32[]{:S(2)}) collective-permute-start(bf16[1,2,1040,128]{3,2,1,0:T(8,128)(2,1)S(1)} %get-tuple-element.29), channel_id=1, source_target_pairs={{0,8},{4,12},{8,0},{12,4},{16,24},{20,28},{24,16},{28,20},{1,9},{5... | collective-permute-start | bytes 1597448 | tf_op jit(solution)/shard_map/ppermute | solution.py:384
  14.5 7.4 %collective-permute-start.4 = (bf16[1040,128]{1,0:T(8,128)(2,1)S(1)}, bf16[1040,128]{1,0:T(8,128)(2,1)S(1)}, u32[]{:S(2)}, u32[]{:S(2)}) collective-permute-start(bf16[1040,128]{1,0:T(8,128)(2,1)S(1)} %join_half.2), channel_id=1, source_target_pairs={{8,16},{12,20},{16,8},{20,12},{0,4},{4,0},{24,28},{28,24},{9,17},{... | collective-permute-start | bytes 798728 | tf_op jit(solution)/shard_map/ppermute | solution.py:377
  20.2 7.4 %collective-permute-start.8 = (bf16[1040,128]{1,0:T(8,128)(2,1)S(1)}, bf16[1040,128]{1,0:T(8,128)(2,1)S(1)}, u32[]{:S(2)}, u32[]{:S(2)}) collective-permute-start(bf16[1040,128]{1,0:T(8,128)(2,1)S(1)} %join_half.3), channel_id=1, source_target_pairs={{8,16},{12,20},{16,8},{20,12},{0,4},{4,0},{24,28},{28,24},{9,17},{... | collective-permute-start | bytes 798728 | tf_op jit(solution)/shard_map/ppermute | solution.py:377
  21.9 12.6 %collective-permute-start.5 = (bf16[128,2048]{1,0:T(8,128)(2,1)S(1)}, bf16[128,2048]{1,0:T(8,128)(2,1)S(1)}, u32[]{:S(2)}, u32[]{:S(2)}) collective-permute-start(bf16[128,2048]{1,0:T(8,128)(2,1)S(1)} %collective-permute-done.1.rest_1_), channel_id=1, source_target_pairs={{0,2},{1,3},{2,0},{3,1},{4,6},{5,7},{6,4},{7,5},{8,10},{9,11},{10,... | collective-permute-start | bytes 1572872 | tf_op jit(solution)/shard_map/ppermute | solution.py:345
  27.7 6.7 %copy-start.4 = (s32[1,2]{1,0:T(1,128)S(1)}, s32[1,2]{1,0:T(1,128)}, u32[]{:S(2)}) copy-start(s32[1,2]{1,0:T(1,128)} %requests_ref.1) | copy-start | bytes 28
  27.8 6.7 %copy-start.5 = (s32[1,4]{1,0:T(1,128)S(1)}, s32[1,4]{1,0:T(1,128)}, u32[]{:S(2)}) copy-start(s32[1,4]{1,0:T(1,128)} %owners_ref.1) | copy-start | bytes 52
  27.8 14.6 %collective-permute-start.9 = (bf16[1,2,1040,128]{3,2,1,0:T(8,128)(2,1)S(1)}, bf16[1,2,1040,128]{3,2,1,0:T(8,128)(2,1)S(1)}, u32[]{:S(2)}, u32[]{:S(2)}) collective-permute-start(bf16[1,2,1040,128]{3,2,1,0:T(8,128)(2,1)S(1)} %join_even.1), channel_id=1, source_target_pairs={{0,8},{4,12},{8,0},{12,4},{16,24},{20,28},{24,16},{28,20},{1,9},{5... | collective-permute-start | bytes 1597448 | tf_op jit(solution)/shard_map/ppermute | solution.py:388
  31.7 13.1 %collective-permute-start.11 = (bf16[1,2,1040,128]{3,2,1,0:T(8,128)(2,1)S(1)}, bf16[1,2,1040,128]{3,2,1,0:T(8,128)(2,1)S(1)}, u32[]{:S(2)}, u32[]{:S(2)}) collective-permute-start(bf16[1,2,1040,128]{3,2,1,0:T(8,128)(2,1)S(1)} %join_odd.1), channel_id=1, source_target_pairs={{8,16},{12,20},{16,8},{20,12},{0,4},{4,0},{24,28},{28,24},{9,17},{... | collective-permute-start | bytes 1597448 | tf_op jit(solution)/shard_map/ppermute | solution.py:389

commit v6 on v5

--- a/solution.py
+++ b/solution.py
@@ -29,10 +29,11 @@
     return jnp.where(labels_ref[...] == value, 1.0, 0.0).astype(jnp.bfloat16)
 
 
-def write_sums(base, labels_ref, features_ref, block_rows, came, store):
+def write_sums(base, labels_ref, features_ref, block_rows, came, store, only=None):
     crop_count, feat_width = features_ref.shape
     half_rows = block_rows // HALVES
     slabs = feat_width // LANES
+    halves = range(HALVES) if only is None else (only,)
     match = labels_ref[...] if base is None else match_of(base, labels_ref, block_rows)
 
     def put(h, first, part):
@@ -41,17 +42,19 @@
         store(h, first, part.astype(jnp.bfloat16))
 
     for s in range(0, slabs, WIDE):
+        rows = match if only is None else match[only * half_rows : (only + 1) * half_rows]
         part = jnp.dot(
-            match,
+            rows,
             features_ref[:, s * LANES : (s + WIDE) * LANES],
             preferred_element_type=jnp.float32,
         )
-        for h in range(HALVES):
+        for h in halves:
+            at = (h - halves[0]) * half_rows
             for i in range(WIDE):
                 put(
                     h,
                     (s + i) * half_rows,
-                    part[h * half_rows : (h + 1) * half_rows, i * LANES : (i + 1) * LANES],
+                    part[at : at + half_rows, i * LANES : (i + 1) * LANES],
                 )
     counts = lax.dot_general(
         jnp.ones((EXTRA, crop_count), jnp.bfloat16),
@@ -62,7 +65,7 @@
     high = jnp.floor(counts * (1.0 / BASE))
     digit = lax.broadcasted_iota(jnp.int32, counts.shape, 0)
     digits = jnp.where(digit == 0, counts - BASE * high, jnp.where(digit == 1, high, 0.0))
-    for h in range(HALVES):
+    for h in halves:
         put(h, slabs * half_rows, digits)
 
 
@@ -112,7 +115,13 @@
     def store(h, first, part):
         outs[h][pl.ds(first, part.shape[0]), :] = part
 
-    write_sums(base, labels_ref, features_ref, block_rows, came_at(came_ref, 0), store)
+    def write():
+        write_sums(base, labels_ref, features_ref, block_rows, came_at(came_ref, 0), store)
+
+    if layers == 4:
+        pl.when(jnp.logical_not(has_odd(layers)))(write)
+    else:
+        write()
 
 
 def chip_rest_kernel(layers, block_rows, labels_ref, features_ref, came_ref, second_ref, out_ref):
@@ -138,6 +147,21 @@
     out_ref[...] = (
         mine_ref[...].astype(jnp.float32) + came_ref[...].astype(jnp.float32)
     ).astype(jnp.bfloat16)
+
+
+def join_first_kernel(layers, block_rows, h, labels_ref, features_ref, sibling_ref, came_ref, out_ref):
+    base = base_at(0, layers, lax.axis_index("region") % CORES, block_rows)
+
+    def came(_, first, rows):
+        part = pl.ds(first, rows)
+        return sibling_ref[0, h, part, :].astype(jnp.float32) + came_ref[part, :].astype(jnp.float32)
+
+    def store(_, first, part):
+        out_ref[pl.ds(first, part.shape[0]), :] = part
+
+    @pl.when(has_odd(layers))
+    def _():
+        write_sums(base, labels_ref, features_ref, block_rows, came, store, only=h)
 
 
 def join_kernel(layers, hop, odd, *refs):
@@ -367,11 +391,16 @@
             fetch(k, k, sent_memory)
     odd_came = []
     for h in range(HALVES):
+        if layers == 4:
+            kernel = part(join_first_kernel, layers, block_rows, h)
+            operands = (labels, features, came_first, even_came[h])
+        else:
+            kernel, operands = join_half_kernel, (first[h], even_came[h])
         leaves = call(
-            join_half_kernel,
+            kernel,
             "join_half",
             jax.ShapeDtypeStruct((pay_rows, LANES), bf16),
-            (first[h], even_came[h]),
+            operands,
             pay_rows * LANES,
         )
         odd_came.append(lax.ppermute(leaves, "region", odd))

time: 46.3 us -> 46.4 us (level)
  waiting for transfers between devices: 23.1 us -> 21.9 us
  starting transfers between devices: 11.4 us -> 12.1 us
    ppermute x2, waiting for transfers between devices: 7.2 us -> 6.21 us  [on_device(): even_came = [lax.ppermute(x, 'region', even) for x in first]]
    ppermute x1, waiting for transfers between devices: 4.07 us -> 3.11 us  [on_device(): even_came = [lax.ppermute(even_next, 'region', even)]]
    ppermute x3, waiting for transfers between devices: 1.17 us -> 2 us  [fetch(): lax.ppermute(block, 'group', [(g, g ^ step) for g in range(group_count)])]
    ppermute x1, waiting for transfers between devices: 3.69 us -> 2.94 us  [on_device(): even_came = [lax.ppermute(second, 'region', even)]]
    ppermute x1, starting transfers between devices: 0.56 us -> 1.05 us  [on_device(): even_came = [lax.ppermute(second, 'region', even)]]
  transfers between devices with their start and end apart: 12 -> 12, of which waited for: 8 -> 9; matrix products, arithmetic and copies ran while one was open for 0% -> 0% of each run, Pallas kernels for 16% -> 17%
where the time goes in v6:
time: 46.4 us; the launch traced here: 46 us
  waiting for transfers between devices  21.9 us (47%)
  starting transfers between devices  12.1 us (26%)
  Pallas kernels  9.67 us (21%)
  local copies, waits for them, and re-layouts  1.52 us (3%)
  between operations  0.74 us (2%)
    pallas_call x11, Pallas kernels, call(): pl.pallas_call(kernel, out_shape=out_shape, in_specs=specs, out_specs=[ou...  9.67 us
    ppermute x2, waiting for transfers between devices, on_device(): even_came = [lax.ppermute(x, 'region', even) for x in first]  6.21 us
    ppermute x2, waiting for transfers between devices, on_device(): odd_came.append(lax.ppermute(leaves, 'region', odd))  4.51 us
    ppermute x3, starting transfers between devices, fetch(): lax.ppermute(block, 'group', [(g, g ^ step) for g in range(group_count)])  3.57 us
    ppermute x2, starting transfers between devices, on_device(): odd_came.append(lax.ppermute(leaves, 'region', odd))  3.44 us
    ppermute x1, waiting for transfers between devices, on_device(): even_came = [lax.ppermute(even_next, 'region', even)]  3.11 us
    ppermute x1, waiting for transfers between devices, on_device(): even_came = [lax.ppermute(second, 'region', even)]  2.94 us
    ppermute x1, waiting for transfers between devices, on_device(): odd_came = [lax.ppermute(odd_next, 'region', odd)]  2.76 us
  transfers between devices with their start and end apart: 12, of which 9 were waited for; matrix products, arithmetic and copies ran while one was open for 0% of the time, Pallas kernels for 17%

profile of v6, /device:TPU:10, one launch (start us, length us, event | category | flops | bytes accessed | tf_op | source)
XLA Modules:
  0.0 46.0 jit_solution(116308743359387430)
XLA Ops:
  0.6 0.0 copy-start
  0.6 0.0 copy-start.2
  0.7 0.8 %copy-done.2 = s32[1,384]{1,0:T(1,128)S(1)} copy-done((s32[1,384]{1,0:T(1,128)S(1)}, s32[1,384]{1,0:T(1,128)}, u32[]{:S(2)}) %copy-start.2) | copy-done | bytes 1560
  1.5 0.6 %copy-done = bf16[384,2048]{1,0:T(8,128)(2,1)S(1)} copy-done((bf16[384,2048]{1,0:T(8,128)(2,1)S(1)}, bf16[384,2048]{1,0:T(8,128)(2,1)}, u32[]{:S(2)}) %copy-start) | copy-done | bytes 1572888
  2.1 0.0 copy-start.3
  2.1 0.5 %away_first.1 = bf16[1,2,1040,128]{3,2,1,0:T(8,128)(2,1)S(1)} custom-call(bf16[128,384]{1,0:T(8,128)(2,1)S(1)} %match_first.1.match_ref, bf16[384,2048]{1,0:T(8,128)(2,1)S(1)} %copy-done), custom_call_target="tpu_custom_call" | custom-call | flops 201326592 | bytes 2203648 | tf_op jit(solution)/shard_map/away_first/pallas_call | solution.py:304
  2.5 0.1 collective-permute-start
  2.6 0.1 copy-done.3
  2.7 1.3 %away_rest.1 = bf16[3,2,1040,128]{3,2,1,0:T(8,128)(2,1)S(1)} custom-call(s32[1,384]{1,0:T(1,128)S(1)} %copy-done.3, bf16[384,2048]{1,0:T(8,128)(2,1)S(1)} %copy-done), custom_call_target="tpu_custom_call" | custom-call | flops 603979776 | bytes 3171072 | tf_op jit(solution)/shard_map/away_rest/pallas_call | solution.py:304
  4.1 0.0 copy-start.1
  4.1 0.4 collective-permute-done.came_ref.sibling_ref
  4.5 0.1 collective-permute-start.6
  4.7 1.0 %collective-permute-start.3 = (bf16[1040,128]{1,0:T(8,128)(2,1)S(1)}, bf16[1040,128]{1,0:T(8,128)(2,1)S(1)}, u32[]{:S(2)}, u32[]{:S(2)}) collective-permute-start(bf16[1040,128]{1,0:T(8,128)(2,1)S(1)} %get-tuple-element.21.refs_0_), channel_id=1, source_target_pairs={{0,8},{4,12},{8,0},{12,4},{16,24},{20,28},{24,16},{28,20},{1,9},{5... | collective-permute-start | bytes 798728 | tf_op jit(solution)/shard_map/ppermute | solution.py:388
  5.7 0.0 copy-done.1
  5.7 0.0 collective-permute-start.1
  5.7 2.0 %collective-permute-start.2 = (bf16[128,2048]{1,0:T(8,128)(2,1)S(1)}, bf16[128,2048]{1,0:T(8,128)(2,1)S(1)}, u32[]{:S(2)}, u32[]{:S(2)}) collective-permute-start(bf16[128,2048]{1,0:T(8,128)(2,1)S(1)} %copy-done.1), channel_id=1, source_target_pairs={{0,2},{1,3},{2,0},{3,1},{4,6},{5,7},{6,4},{7,5},{8,10},{9,11},{10,... | collective-permute-start | bytes 1572872 | tf_op jit(solution)/shard_map/ppermute | solution.py:369
  7.7 1.0 %collective-permute-start.7 = (bf16[1040,128]{1,0:T(8,128)(2,1)S(1)}, bf16[1040,128]{1,0:T(8,128)(2,1)S(1)}, u32[]{:S(2)}, u32[]{:S(2)}) collective-permute-start(bf16[1040,128]{1,0:T(8,128)(2,1)S(1)} %get-tuple-element.27.refs_1_), channel_id=1, source_target_pairs={{0,8},{4,12},{8,0},{12,4},{16,24},{20,28},{24,16},{28,20},{1,9},{5... | collective-permute-start | bytes 798728 | tf_op jit(solution)/shard_map/ppermute | solution.py:388
  8.7 0.0 collective-permute-done.6.came_ref
  8.7 1.4 %chip_rest.1 = (bf16[1,2,1040,128]{3,2,1,0:T(8,128)(2,1)S(1)}, bf16[3,2,1040,128]{3,2,1,0:T(8,128)(2,1)S(1)}) custom-call(s32[1,384]{1,0:T(1,128)S(1)} %copy-done.3, bf16[384,2048]{1,0:T(8,128)(2,1)S(1)} %copy-done, bf16[3,2,1040,128]{3,2,1,0:T(8,128)(2,1)S(1)} %collective-permute-done.6.came_ref), custom_call_target="tpu_custom_call" | custom-call | flops 603979776 | bytes 5300992 | tf_op jit(solution)/shard_map/chip_rest/pallas_call | solution.py:304
  10.2 1.1 %collective-permute-start.10 = (bf16[1,2,1040,128]{3,2,1,0:T(8,128)(2,1)S(1)}, bf16[1,2,1040,128]{3,2,1,0:T(8,128)(2,1)S(1)}, u32[]{:S(2)}, u32[]{:S(2)}) collective-permute-start(bf16[1,2,1040,128]{3,2,1,0:T(8,128)(2,1)S(1)} %get-tuple-element.29), channel_id=1, source_target_pairs={{0,8},{4,12},{8,0},{12,4},{16,24},{20,28},{24,16},{28,20},{1,9},{5... | collective-permute-start | bytes 1597448 | tf_op jit(solution)/shard_map/ppermute | solution.py:413
  11.2 2.7 %collective-permute-done.3.came_ref = bf16[1040,128]{1,0:T(8,128)(2,1)S(1)} collective-permute-done((bf16[1040,128]{1,0:T(8,128)(2,1)S(1)}, bf16[1040,128]{1,0:T(8,128)(2,1)S(1)}, u32[]{:S(2)}, u32[]{:S(2)}) %collective-permute-start.3) | collective-permute-done | bytes 266272 | tf_op jit(solution)/shard_map/ppermute | solution.py:388
  13.9 0.4 join_half.2
  14.3 1.7 %collective-permute-start.4 = (bf16[1040,128]{1,0:T(8,128)(2,1)S(1)}, bf16[1040,128]{1,0:T(8,128)(2,1)S(1)}, u32[]{:S(2)}, u32[]{:S(2)}) collective-permute-start(bf16[1040,128]{1,0:T(8,128)(2,1)S(1)} %join_half.2), channel_id=1, source_target_pairs={{8,16},{12,20},{16,8},{20,12},{0,4},{4,0},{24,28},{28,24},{9,17},{... | collective-permute-start | bytes 798728 | tf_op jit(solution)/shard_map/ppermute | solution.py:406
  16.0 3.5 %collective-permute-done.7.came_ref = bf16[1040,128]{1,0:T(8,128)(2,1)S(1)} collective-permute-done((bf16[1040,128]{1,0:T(8,128)(2,1)S(1)}, bf16[1040,128]{1,0:T(8,128)(2,1)S(1)}, u32[]{:S(2)}, u32[]{:S(2)}) %collective-permute-start.7) | collective-permute-done | bytes 266272 | tf_op jit(solution)/shard_map/ppermute | solution.py:388
  19.6 0.4 join_half.3
  20.0 1.7 %collective-permute-start.8 = (bf16[1040,128]{1,0:T(8,128)(2,1)S(1)}, bf16[1040,128]{1,0:T(8,128)(2,1)S(1)}, u32[]{:S(2)}, u32[]{:S(2)}) collective-permute-start(bf16[1040,128]{1,0:T(8,128)(2,1)S(1)} %join_half.3), channel_id=1, source_target_pairs={{8,16},{12,20},{16,8},{20,12},{0,4},{4,0},{24,28},{28,24},{9,17},{... | collective-permute-start | bytes 798728 | tf_op jit(solution)/shard_map/ppermute | solution.py:406
  21.8 0.0 collective-permute-done.1.rest_1_
  21.8 0.0 collective-permute-done.2.rest_2_
  21.8 0.3 collective-permute-done.4.refs_3_
  22.1 1.5 %collective-permute-start.5 = (bf16[128,2048]{1,0:T(8,128)(2,1)S(1)}, bf16[128,2048]{1,0:T(8,128)(2,1)S(1)}, u32[]{:S(2)}, u32[]{:S(2)}) collective-permute-start(bf16[128,2048]{1,0:T(8,128)(2,1)S(1)} %collective-permute-done.1.rest_1_), channel_id=1, source_target_pairs={{0,2},{1,3},{2,0},{3,1},{4,6},{5,7},{6,4},{7,5},{8,10},{9,11},{10,... | collective-permute-start | bytes 1572872 | tf_op jit(solution)/shard_map/ppermute | solution.py:369
  23.6 4.2 %collective-permute-done.8.refs_4_ = bf16[1040,128]{1,0:T(8,128)(2,1)S(1)} collective-permute-done((bf16[1040,128]{1,0:T(8,128)(2,1)S(1)}, bf16[1040,128]{1,0:T(8,128)(2,1)S(1)}, u32[]{:S(2)}, u32[]{:S(2)}) %collective-permute-start.8) | collective-permute-done | bytes 266272 | tf_op jit(solution)/shard_map/ppermute | solution.py:406
  27.8 0.2 join_even.1
  28.0 0.0 copy-start.4
  28.0 0.0 copy-start.5
  28.0 0.1 collective-permute-start.9
  28.1 2.9 %collective-permute-done.10.refs_3_ = bf16[1,2,1040,128]{3,2,1,0:T(8,128)(2,1)S(1)} collective-permute-done((bf16[1,2,1040,128]{3,2,1,0:T(8,128)(2,1)S(1)}, bf16[1,2,1040,128]{3,2,1,0:T(8,128)(2,1)S(1)}, u32[]{:S(2)}, u32[]{:S(2)}) %collective-permute-start.10) | collective-permute-done | bytes 532512 | tf_op jit(solution)/shard_map/ppermute | solution.py:413
  31.0 0.1 join_odd.1
  31.1 1.7 %collective-permute-start.11 = (bf16[1,2,1040,128]{3,2,1,0:T(8,128)(2,1)S(1)}, bf16[1,2,1040,128]{3,2,1,0:T(8,128)(2,1)S(1)}, u32[]{:S(2)}, u32[]{:S(2)}) collective-permute-start(bf16[1,2,1040,128]{3,2,1,0:T(8,128)(2,1)S(1)} %join_odd.1), channel_id=1, source_target_pairs={{8,16},{12,20},{16,8},{20,12},{0,4},{4,0},{24,28},{28,24},{9,17},{... | collective-permute-start | bytes 1597448 | tf_op jit(solution)/shard_map/ppermute | solution.py:418
  32.9 2.0 %collective-permute-done.5.rest_3_ = bf16[128,2048]{1,0:T(8,128)(2,1)S(1)} collective-permute-done((bf16[128,2048]{1,0:T(8,128)(2,1)S(1)}, bf16[128,2048]{1,0:T(8,128)(2,1)S(1)}, u32[]{:S(2)}, u32[]{:S(2)}) %collective-permute-start.5) | collective-permute-done | bytes 524320 | tf_op jit(solution)/shard_map/ppermute | solution.py:369
  34.9 0.0 copy-done.4
  34.9 0.0 copy-done.5
  34.9 3.9 %feat_grad.1 = bf16[384,2048]{1,0:T(8,128)(2,1)} custom-call(s32[1,2]{1,0:T(1,128)S(1)} %copy-done.4, s32[1,4]{1,0:T(1,128)S(1)} %copy-done.5, bf16[384,2048]{1,0:T(8,128)(2,1)S(1)} %copy-done, bf16[128,2048]{1,0:T(8,128)(2,1)S(1)} %copy-done.1, bf16[128,2048]{1,0:T(8,128)(2,1)S(1)} %collective-permute-done.1.rest_1_, ...), custom_call_target="tpu_custom_call" | custom-call | flops 805306368 | bytes 5242892 | tf_op jit(solution)/shard_map/feat_grad/pallas_call | solution.py:304
  38.7 3.1 %collective-permute-done.9.rest_0_ = bf16[1,2,1040,128]{3,2,1,0:T(8,128)(2,1)S(1)} collective-permute-done((bf16[1,2,1040,128]{3,2,1,0:T(8,128)(2,1)S(1)}, bf16[1,2,1040,128]{3,2,1,0:T(8,128)(2,1)S(1)}, u32[]{:S(2)}, u32[]{:S(2)}) %collective-permute-start.9) | collective-permute-done | bytes 532512 | tf_op jit(solution)/shard_map/ppermute | solution.py:417
  41.9 2.8 %collective-permute-done.11.rest_1_ = bf16[1,2,1040,128]{3,2,1,0:T(8,128)(2,1)S(1)} collective-permute-done((bf16[1,2,1040,128]{3,2,1,0:T(8,128)(2,1)S(1)}, bf16[1,2,1040,128]{3,2,1,0:T(8,128)(2,1)S(1)}, u32[]{:S(2)}, u32[]{:S(2)}) %collective-permute-start.11) | collective-permute-done | bytes 532512 | tf_op jit(solution)/shard_map/ppermute | solution.py:418
  44.6 1.4 %update.1 = bf16[128,2048]{1,0:T(8,128)(2,1)} custom-call(bf16[128,2048]{1,0:T(8,128)(2,1)S(1)} %copy-done.1, bf16[3,2,1040,128]{3,2,1,0:T(8,128)(2,1)S(1)} %get-tuple-element.26.refs_2_.rest_ref, bf16[1,2,1040,128]{3,2,1,0:T(8,128)(2,1)S(1)} %collective-permute-done.9.rest_0_, bf16[1,2,1040,128]{3,2,1,0:T(8,128)(2,1)S(1)} %collective-permute-done.11.rest_1_), custom_call_target="tpu_custom_call" | custom-call | flops 2621440 | bytes 3710976 | tf_op jit(solution)/shard_map/update/pallas_call | solution.py:304
  (2 shorter events, 0.0 us)
Async XLA Ops:
  0.6 1.4 %copy-start = (bf16[384,2048]{1,0:T(8,128)(2,1)S(1)}, bf16[384,2048]{1,0:T(8,128)(2,1)}, u32[]{:S(2)}) copy-start(bf16[384,2048]{1,0:T(8,128)(2,1)} %features_ref.13) | copy-start | bytes 4718596
  0.6 0.8 %copy-start.2 = (s32[1,384]{1,0:T(1,128)S(1)}, s32[1,384]{1,0:T(1,128)}, u32[]{:S(2)}) copy-start(s32[1,384]{1,0:T(1,128)} %labels_ref.10) | copy-start | bytes 4612
  2.1 0.7 %copy-start.3 = (s32[1,384]{1,0:T(1,128)S(1)}, s32[1,384]{1,0:T(1,128)}, u32[]{:S(2)}) copy-start(s32[1,384]{1,0:T(1,128)} %labels_ref.10) | copy-start | bytes 4612
  2.5 2.0 %collective-permute-start = (bf16[1,2,1040,128]{3,2,1,0:T(8,128)(2,1)S(1)}, bf16[1,2,1040,128]{3,2,1,0:T(8,128)(2,1)S(1)}, u32[]{:S(2)}, u32[]{:S(2)}) collective-permute-start(bf16[1,2,1040,128]{3,2,1,0:T(8,128)(2,1)S(1)} %away_first.1), channel_id=1, source_target_pairs={{0,4},{4,0},{8,12},{12,8},{16,20},{20,16},{24,28},{28,24},{1,5},{5... | collective-permute-start | bytes 1597448 | tf_op jit(solution)/shard_map/ppermute | solution.py:340
  4.1 1.6 %copy-start.1 = (bf16[128,2048]{1,0:T(8,128)(2,1)S(1)}, bf16[128,2048]{1,0:T(8,128)(2,1)}, u32[]{:S(2)}) copy-start(bf16[128,2048]{1,0:T(8,128)(2,1)} %memory_ref.1) | copy-start | bytes 1572868
  4.5 4.2 %collective-permute-start.6 = (bf16[3,2,1040,128]{3,2,1,0:T(8,128)(2,1)S(1)}, bf16[3,2,1040,128]{3,2,1,0:T(8,128)(2,1)S(1)}, u32[]{:S(2)}, u32[]{:S(2)}) collective-permute-start(bf16[3,2,1040,128]{3,2,1,0:T(8,128)(2,1)S(1)} %away_rest.1), channel_id=1, source_target_pairs={{0,4},{4,0},{8,12},{12,8},{16,20},{20,16},{24,28},{28,24},{1,5},{5... | collective-permute-start | bytes 4792328 | tf_op jit(solution)/shard_map/ppermute | solution.py:362
  4.7 9.2 %collective-permute-start.3 = (bf16[1040,128]{1,0:T(8,128)(2,1)S(1)}, bf16[1040,128]{1,0:T(8,128)(2,1)S(1)}, u32[]{:S(2)}, u32[]{:S(2)}) collective-permute-start(bf16[1040,128]{1,0:T(8,128)(2,1)S(1)} %get-tuple-element.21.refs_0_), channel_id=1, source_target_pairs={{0,8},{4,12},{8,0},{12,4},{16,24},{20,28},{24,16},{28,20},{1,9},{5... | collective-permute-start | bytes 798728 | tf_op jit(solution)/shard_map/ppermute | solution.py:388
  5.7 16.1 %collective-permute-start.1 = (bf16[128,2048]{1,0:T(8,128)(2,1)S(1)}, bf16[128,2048]{1,0:T(8,128)(2,1)S(1)}, u32[]{:S(2)}, u32[]{:S(2)}) collective-permute-start(bf16[128,2048]{1,0:T(8,128)(2,1)S(1)} %copy-done.1), channel_id=1, source_target_pairs={{0,1},{1,0},{2,3},{3,2},{4,5},{5,4},{6,7},{7,6},{8,9},{9,8},{10,11... | collective-permute-start | bytes 1572872 | tf_op jit(solution)/shard_map/ppermute | solution.py:369
  5.7 16.1 %collective-permute-start.2 = (bf16[128,2048]{1,0:T(8,128)(2,1)S(1)}, bf16[128,2048]{1,0:T(8,128)(2,1)S(1)}, u32[]{:S(2)}, u32[]{:S(2)}) collective-permute-start(bf16[128,2048]{1,0:T(8,128)(2,1)S(1)} %copy-done.1), channel_id=1, source_target_pairs={{0,2},{1,3},{2,0},{3,1},{4,6},{5,7},{6,4},{7,5},{8,10},{9,11},{10,... | collective-permute-start | bytes 1572872 | tf_op jit(solution)/shard_map/ppermute | solution.py:369
  7.7 11.9 %collective-permute-start.7 = (bf16[1040,128]{1,0:T(8,128)(2,1)S(1)}, bf16[1040,128]{1,0:T(8,128)(2,1)S(1)}, u32[]{:S(2)}, u32[]{:S(2)}) collective-permute-start(bf16[1040,128]{1,0:T(8,128)(2,1)S(1)} %get-tuple-element.27.refs_1_), channel_id=1, source_target_pairs={{0,8},{4,12},{8,0},{12,4},{16,24},{20,28},{24,16},{28,20},{1,9},{5... | collective-permute-start | bytes 798728 | tf_op jit(solution)/shard_map/ppermute | solution.py:388
  10.2 20.8 %collective-permute-start.10 = (bf16[1,2,1040,128]{3,2,1,0:T(8,128)(2,1)S(1)}, bf16[1,2,1040,128]{3,2,1,0:T(8,128)(2,1)S(1)}, u32[]{:S(2)}, u32[]{:S(2)}) collective-permute-start(bf16[1,2,1040,128]{3,2,1,0:T(8,128)(2,1)S(1)} %get-tuple-element.29), channel_id=1, source_target_pairs={{0,8},{4,12},{8,0},{12,4},{16,24},{20,28},{24,16},{28,20},{1,9},{5... | collective-permute-start | bytes 1597448 | tf_op jit(solution)/shard_map/ppermute | solution.py:413
  14.3 7.8 %collective-permute-start.4 = (bf16[1040,128]{1,0:T(8,128)(2,1)S(1)}, bf16[1040,128]{1,0:T(8,128)(2,1)S(1)}, u32[]{:S(2)}, u32[]{:S(2)}) collective-permute-start(bf16[1040,128]{1,0:T(8,128)(2,1)S(1)} %join_half.2), channel_id=1, source_target_pairs={{8,16},{12,20},{16,8},{20,12},{0,4},{4,0},{24,28},{28,24},{9,17},{... | collective-permute-start | bytes 798728 | tf_op jit(solution)/shard_map/ppermute | solution.py:406
  20.0 7.8 %collective-permute-start.8 = (bf16[1040,128]{1,0:T(8,128)(2,1)S(1)}, bf16[1040,128]{1,0:T(8,128)(2,1)S(1)}, u32[]{:S(2)}, u32[]{:S(2)}) collective-permute-start(bf16[1040,128]{1,0:T(8,128)(2,1)S(1)} %join_half.3), channel_id=1, source_target_pairs={{8,16},{12,20},{16,8},{20,12},{0,4},{4,0},{24,28},{28,24},{9,17},{... | collective-permute-start | bytes 798728 | tf_op jit(solution)/shard_map/ppermute | solution.py:406
  22.1 12.8 %collective-permute-start.5 = (bf16[128,2048]{1,0:T(8,128)(2,1)S(1)}, bf16[128,2048]{1,0:T(8,128)(2,1)S(1)}, u32[]{:S(2)}, u32[]{:S(2)}) collective-permute-start(bf16[128,2048]{1,0:T(8,128)(2,1)S(1)} %collective-permute-done.1.rest_1_), channel_id=1, source_target_pairs={{0,2},{1,3},{2,0},{3,1},{4,6},{5,7},{6,4},{7,5},{8,10},{9,11},{10,... | collective-permute-start | bytes 1572872 | tf_op jit(solution)/shard_map/ppermute | solution.py:369
  28.0 6.9 %copy-start.4 = (s32[1,2]{1,0:T(1,128)S(1)}, s32[1,2]{1,0:T(1,128)}, u32[]{:S(2)}) copy-start(s32[1,2]{1,0:T(1,128)} %requests_ref.1) | copy-start | bytes 28
  28.0 6.9 %copy-start.5 = (s32[1,4]{1,0:T(1,128)S(1)}, s32[1,4]{1,0:T(1,128)}, u32[]{:S(2)}) copy-start(s32[1,4]{1,0:T(1,128)} %owners_ref.1) | copy-start | bytes 52
  28.0 13.9 %collective-permute-start.9 = (bf16[1,2,1040,128]{3,2,1,0:T(8,128)(2,1)S(1)}, bf16[1,2,1040,128]{3,2,1,0:T(8,128)(2,1)S(1)}, u32[]{:S(2)}, u32[]{:S(2)}) collective-permute-start(bf16[1,2,1040,128]{3,2,1,0:T(8,128)(2,1)S(1)} %join_even.1), channel_id=1, source_target_pairs={{0,8},{4,12},{8,0},{12,4},{16,24},{20,28},{24,16},{28,20},{1,9},{5... | collective-permute-start | bytes 1597448 | tf_op jit(solution)/shard_map/ppermute | solution.py:417
  31.1 13.5 %collective-permute-start.11 = (bf16[1,2,1040,128]{3,2,1,0:T(8,128)(2,1)S(1)}, bf16[1,2,1040,128]{3,2,1,0:T(8,128)(2,1)S(1)}, u32[]{:S(2)}, u32[]{:S(2)}) collective-permute-start(bf16[1,2,1040,128]{3,2,1,0:T(8,128)(2,1)S(1)} %join_odd.1), channel_id=1, source_target_pairs={{8,16},{12,20},{16,8},{20,12},{0,4},{4,0},{24,28},{28,24},{9,17},{... | collective-permute-start | bytes 1597448 | tf_op jit(solution)/shard_map/ppermute | solution.py:418

commit v7 on v6

--- a/solution.py
+++ b/solution.py
@@ -217,20 +217,24 @@
         lane = lax.broadcasted_iota(jnp.int32, (half_rows, LANES), 1)
         counts = jnp.sum(jnp.where(row == lane, counts_row, 0.0), axis=1, keepdims=True)
         seen = counts > 0
-        share = (1.0 - momentum_keep) / jnp.maximum(counts, 1.0)
+        share = jnp.where(seen, (1.0 - momentum_keep) / jnp.maximum(counts, 1.0), 0.0)
+        share = jnp.broadcast_to(share, (half_rows, LANES))
+        keep = jnp.broadcast_to(jnp.where(seen, momentum_keep, 1.0), (half_rows, LANES))
         squares = jnp.zeros((half_rows, LANES), jnp.float32)
         for s in range(slabs):
             old = memory_ref[pl.ds(h * half_rows, half_rows), pl.ds(s * LANES, LANES)].astype(
                 jnp.float32
             )
-            added = total(s * half_rows, half_rows) * share
-            mixed = jnp.where(seen, momentum_keep * old + added, old)
+            mixed = keep * old + share * total(s * half_rows, half_rows)
             mixed_ref[:, pl.ds(s * LANES, LANES)] = mixed
             squares = squares + mixed * mixed
         mean = jnp.sum(squares, axis=1, keepdims=True) * (1.0 / feat_width)
         scale = lax.rsqrt(mean + 1e-06) * D ** (-0.5)
         rows = pl.ds(h * half_rows, half_rows)
-        out_ref[rows, :] = (mixed_ref[...] * scale).astype(jnp.bfloat16)
+        scale = jnp.broadcast_to(scale, (half_rows, LANES))
+        for s in range(slabs):
+            columns = pl.ds(s * LANES, LANES)
+            out_ref[rows, columns] = (mixed_ref[:, columns] * scale).astype(jnp.bfloat16)
         copies.append(
             pltpu.make_async_copy(out_ref.at[rows, :], out_hbm.at[rows, :], sems.at[h])
         )

time: 46.4 us -> 46.3 us (level)
  no operation moved by 1% of the time
where the time goes in v7:
time: 46.3 us; the launch traced here: 45.9 us
  waiting for transfers between devices  21.9 us (47%)
  starting transfers between devices  12.1 us (26%)
  Pallas kernels  9.61 us (21%)
  local copies, waits for them, and re-layouts  1.52 us (3%)
  between operations  0.74 us (2%)
    pallas_call x11, Pallas kernels, call(): pl.pallas_call(kernel, out_shape=out_shape, in_specs=specs, out_specs=[ou...  9.61 us
    ppermute x2, waiting for transfers between devices, on_device(): even_came = [lax.ppermute(x, 'region', even) for x in first]  6.21 us
    ppermute x2, waiting for transfers between devices, on_device(): odd_came.append(lax.ppermute(leaves, 'region', odd))  4.51 us
    ppermute x3, starting transfers between devices, fetch(): lax.ppermute(block, 'group', [(g, g ^ step) for g in range(group_count)])  3.57 us
    ppermute x2, starting transfers between devices, on_device(): odd_came.append(lax.ppermute(leaves, 'region', odd))  3.44 us
    ppermute x1, waiting for transfers between devices, on_device(): even_came = [lax.ppermute(even_next, 'region', even)]  3.11 us
    ppermute x1, waiting for transfers between devices, on_device(): even_came = [lax.ppermute(second, 'region', even)]  2.94 us
    ppermute x1, waiting for transfers between devices, on_device(): odd_came = [lax.ppermute(odd_next, 'region', odd)]  2.76 us
  transfers between devices with their start and end apart: 12, of which 9 were waited for; matrix products, arithmetic and copies ran while one was open for 0% of the time, Pallas kernels for 17%

profile of v7, /device:TPU:10, one launch (start us, length us, event | category | flops | bytes accessed | tf_op | source)
XLA Modules:
  0.0 45.9 jit_solution(8133328573178785355)
XLA Ops:
  0.6 0.0 copy-start
  0.6 0.0 copy-start.2
  0.7 0.8 %copy-done.2 = s32[1,384]{1,0:T(1,128)S(1)} copy-done((s32[1,384]{1,0:T(1,128)S(1)}, s32[1,384]{1,0:T(1,128)}, u32[]{:S(2)}) %copy-start.2) | copy-done | bytes 1560
  1.5 0.6 %copy-done = bf16[384,2048]{1,0:T(8,128)(2,1)S(1)} copy-done((bf16[384,2048]{1,0:T(8,128)(2,1)S(1)}, bf16[384,2048]{1,0:T(8,128)(2,1)}, u32[]{:S(2)}) %copy-start) | copy-done | bytes 1572888
  2.1 0.0 copy-start.3
  2.1 0.5 %away_first.1 = bf16[1,2,1040,128]{3,2,1,0:T(8,128)(2,1)S(1)} custom-call(bf16[128,384]{1,0:T(8,128)(2,1)S(1)} %match_first.1.match_ref, bf16[384,2048]{1,0:T(8,128)(2,1)S(1)} %copy-done), custom_call_target="tpu_custom_call" | custom-call | flops 201326592 | bytes 2203648 | tf_op jit(solution)/shard_map/away_first/pallas_call | solution.py:308
  2.5 0.1 collective-permute-start
  2.6 0.1 copy-done.3
  2.7 1.3 %away_rest.1 = bf16[3,2,1040,128]{3,2,1,0:T(8,128)(2,1)S(1)} custom-call(s32[1,384]{1,0:T(1,128)S(1)} %copy-done.3, bf16[384,2048]{1,0:T(8,128)(2,1)S(1)} %copy-done), custom_call_target="tpu_custom_call" | custom-call | flops 603979776 | bytes 3171072 | tf_op jit(solution)/shard_map/away_rest/pallas_call | solution.py:308
  4.1 0.0 copy-start.1
  4.1 0.4 collective-permute-done.came_ref.sibling_ref
  4.5 0.1 collective-permute-start.6
  4.7 1.0 %collective-permute-start.3 = (bf16[1040,128]{1,0:T(8,128)(2,1)S(1)}, bf16[1040,128]{1,0:T(8,128)(2,1)S(1)}, u32[]{:S(2)}, u32[]{:S(2)}) collective-permute-start(bf16[1040,128]{1,0:T(8,128)(2,1)S(1)} %get-tuple-element.21.refs_0_), channel_id=1, source_target_pairs={{0,8},{4,12},{8,0},{12,4},{16,24},{20,28},{24,16},{28,20},{1,9},{5... | collective-permute-start | bytes 798728 | tf_op jit(solution)/shard_map/ppermute | solution.py:392
  5.7 0.0 copy-done.1
  5.7 0.0 collective-permute-start.1
  5.7 2.0 %collective-permute-start.2 = (bf16[128,2048]{1,0:T(8,128)(2,1)S(1)}, bf16[128,2048]{1,0:T(8,128)(2,1)S(1)}, u32[]{:S(2)}, u32[]{:S(2)}) collective-permute-start(bf16[128,2048]{1,0:T(8,128)(2,1)S(1)} %copy-done.1), channel_id=1, source_target_pairs={{0,2},{1,3},{2,0},{3,1},{4,6},{5,7},{6,4},{7,5},{8,10},{9,11},{10,... | collective-permute-start | bytes 1572872 | tf_op jit(solution)/shard_map/ppermute | solution.py:373
  7.7 1.0 %collective-permute-start.7 = (bf16[1040,128]{1,0:T(8,128)(2,1)S(1)}, bf16[1040,128]{1,0:T(8,128)(2,1)S(1)}, u32[]{:S(2)}, u32[]{:S(2)}) collective-permute-start(bf16[1040,128]{1,0:T(8,128)(2,1)S(1)} %get-tuple-element.27.refs_1_), channel_id=1, source_target_pairs={{0,8},{4,12},{8,0},{12,4},{16,24},{20,28},{24,16},{28,20},{1,9},{5... | collective-permute-start | bytes 798728 | tf_op jit(solution)/shard_map/ppermute | solution.py:392
  8.7 0.0 collective-permute-done.6.came_ref
  8.7 1.4 %chip_rest.1 = (bf16[1,2,1040,128]{3,2,1,0:T(8,128)(2,1)S(1)}, bf16[3,2,1040,128]{3,2,1,0:T(8,128)(2,1)S(1)}) custom-call(s32[1,384]{1,0:T(1,128)S(1)} %copy-done.3, bf16[384,2048]{1,0:T(8,128)(2,1)S(1)} %copy-done, bf16[3,2,1040,128]{3,2,1,0:T(8,128)(2,1)S(1)} %collective-permute-done.6.came_ref), custom_call_target="tpu_custom_call" | custom-call | flops 603979776 | bytes 5300992 | tf_op jit(solution)/shard_map/chip_rest/pallas_call | solution.py:308
  10.2 1.1 %collective-permute-start.10 = (bf16[1,2,1040,128]{3,2,1,0:T(8,128)(2,1)S(1)}, bf16[1,2,1040,128]{3,2,1,0:T(8,128)(2,1)S(1)}, u32[]{:S(2)}, u32[]{:S(2)}) collective-permute-start(bf16[1,2,1040,128]{3,2,1,0:T(8,128)(2,1)S(1)} %get-tuple-element.29), channel_id=1, source_target_pairs={{0,8},{4,12},{8,0},{12,4},{16,24},{20,28},{24,16},{28,20},{1,9},{5... | collective-permute-start | bytes 1597448 | tf_op jit(solution)/shard_map/ppermute | solution.py:417
  11.2 2.7 %collective-permute-done.3.came_ref = bf16[1040,128]{1,0:T(8,128)(2,1)S(1)} collective-permute-done((bf16[1040,128]{1,0:T(8,128)(2,1)S(1)}, bf16[1040,128]{1,0:T(8,128)(2,1)S(1)}, u32[]{:S(2)}, u32[]{:S(2)}) %collective-permute-start.3) | collective-permute-done | bytes 266272 | tf_op jit(solution)/shard_map/ppermute | solution.py:392
  13.9 0.4 join_half.2
  14.3 1.7 %collective-permute-start.4 = (bf16[1040,128]{1,0:T(8,128)(2,1)S(1)}, bf16[1040,128]{1,0:T(8,128)(2,1)S(1)}, u32[]{:S(2)}, u32[]{:S(2)}) collective-permute-start(bf16[1040,128]{1,0:T(8,128)(2,1)S(1)} %join_half.2), channel_id=1, source_target_pairs={{8,16},{12,20},{16,8},{20,12},{0,4},{4,0},{24,28},{28,24},{9,17},{... | collective-permute-start | bytes 798728 | tf_op jit(solution)/shard_map/ppermute | solution.py:410
  16.0 3.5 %collective-permute-done.7.came_ref = bf16[1040,128]{1,0:T(8,128)(2,1)S(1)} collective-permute-done((bf16[1040,128]{1,0:T(8,128)(2,1)S(1)}, bf16[1040,128]{1,0:T(8,128)(2,1)S(1)}, u32[]{:S(2)}, u32[]{:S(2)}) %collective-permute-start.7) | collective-permute-done | bytes 266272 | tf_op jit(solution)/shard_map/ppermute | solution.py:392
  19.6 0.4 join_half.3
  20.0 1.7 %collective-permute-start.8 = (bf16[1040,128]{1,0:T(8,128)(2,1)S(1)}, bf16[1040,128]{1,0:T(8,128)(2,1)S(1)}, u32[]{:S(2)}, u32[]{:S(2)}) collective-permute-start(bf16[1040,128]{1,0:T(8,128)(2,1)S(1)} %join_half.3), channel_id=1, source_target_pairs={{8,16},{12,20},{16,8},{20,12},{0,4},{4,0},{24,28},{28,24},{9,17},{... | collective-permute-start | bytes 798728 | tf_op jit(solution)/shard_map/ppermute | solution.py:410
  21.8 0.0 collective-permute-done.1.rest_1_
  21.8 0.0 collective-permute-done.2.rest_2_
  21.8 0.3 collective-permute-done.4.refs_3_
  22.1 1.5 %collective-permute-start.5 = (bf16[128,2048]{1,0:T(8,128)(2,1)S(1)}, bf16[128,2048]{1,0:T(8,128)(2,1)S(1)}, u32[]{:S(2)}, u32[]{:S(2)}) collective-permute-start(bf16[128,2048]{1,0:T(8,128)(2,1)S(1)} %collective-permute-done.1.rest_1_), channel_id=1, source_target_pairs={{0,2},{1,3},{2,0},{3,1},{4,6},{5,7},{6,4},{7,5},{8,10},{9,11},{10,... | collective-permute-start | bytes 1572872 | tf_op jit(solution)/shard_map/ppermute | solution.py:373
  23.6 4.2 %collective-permute-done.8.refs_4_ = bf16[1040,128]{1,0:T(8,128)(2,1)S(1)} collective-permute-done((bf16[1040,128]{1,0:T(8,128)(2,1)S(1)}, bf16[1040,128]{1,0:T(8,128)(2,1)S(1)}, u32[]{:S(2)}, u32[]{:S(2)}) %collective-permute-start.8) | collective-permute-done | bytes 266272 | tf_op jit(solution)/shard_map/ppermute | solution.py:410
  27.8 0.2 join_even.1
  28.0 0.0 copy-start.4
  28.0 0.0 copy-start.5
  28.0 0.1 collective-permute-start.9
  28.1 2.9 %collective-permute-done.10.refs_3_ = bf16[1,2,1040,128]{3,2,1,0:T(8,128)(2,1)S(1)} collective-permute-done((bf16[1,2,1040,128]{3,2,1,0:T(8,128)(2,1)S(1)}, bf16[1,2,1040,128]{3,2,1,0:T(8,128)(2,1)S(1)}, u32[]{:S(2)}, u32[]{:S(2)}) %collective-permute-start.10) | collective-permute-done | bytes 532512 | tf_op jit(solution)/shard_map/ppermute | solution.py:417
  31.0 0.1 join_odd.1
  31.1 1.7 %collective-permute-start.11 = (bf16[1,2,1040,128]{3,2,1,0:T(8,128)(2,1)S(1)}, bf16[1,2,1040,128]{3,2,1,0:T(8,128)(2,1)S(1)}, u32[]{:S(2)}, u32[]{:S(2)}) collective-permute-start(bf16[1,2,1040,128]{3,2,1,0:T(8,128)(2,1)S(1)} %join_odd.1), channel_id=1, source_target_pairs={{8,16},{12,20},{16,8},{20,12},{0,4},{4,0},{24,28},{28,24},{9,17},{... | collective-permute-start | bytes 1597448 | tf_op jit(solution)/shard_map/ppermute | solution.py:422
  32.9 2.0 %collective-permute-done.5.rest_3_ = bf16[128,2048]{1,0:T(8,128)(2,1)S(1)} collective-permute-done((bf16[128,2048]{1,0:T(8,128)(2,1)S(1)}, bf16[128,2048]{1,0:T(8,128)(2,1)S(1)}, u32[]{:S(2)}, u32[]{:S(2)}) %collective-permute-start.5) | collective-permute-done | bytes 524320 | tf_op jit(solution)/shard_map/ppermute | solution.py:373
  34.9 0.0 copy-done.4
  34.9 0.0 copy-done.5
  34.9 3.9 %feat_grad.1 = bf16[384,2048]{1,0:T(8,128)(2,1)} custom-call(s32[1,2]{1,0:T(1,128)S(1)} %copy-done.4, s32[1,4]{1,0:T(1,128)S(1)} %copy-done.5, bf16[384,2048]{1,0:T(8,128)(2,1)S(1)} %copy-done, bf16[128,2048]{1,0:T(8,128)(2,1)S(1)} %copy-done.1, bf16[128,2048]{1,0:T(8,128)(2,1)S(1)} %collective-permute-done.1.rest_1_, ...), custom_call_target="tpu_custom_call" | custom-call | flops 805306368 | bytes 5242892 | tf_op jit(solution)/shard_map/feat_grad/pallas_call | solution.py:308
  38.7 3.1 %collective-permute-done.9.rest_0_ = bf16[1,2,1040,128]{3,2,1,0:T(8,128)(2,1)S(1)} collective-permute-done((bf16[1,2,1040,128]{3,2,1,0:T(8,128)(2,1)S(1)}, bf16[1,2,1040,128]{3,2,1,0:T(8,128)(2,1)S(1)}, u32[]{:S(2)}, u32[]{:S(2)}) %collective-permute-start.9) | collective-permute-done | bytes 532512 | tf_op jit(solution)/shard_map/ppermute | solution.py:421
  41.9 2.8 %collective-permute-done.11.rest_1_ = bf16[1,2,1040,128]{3,2,1,0:T(8,128)(2,1)S(1)} collective-permute-done((bf16[1,2,1040,128]{3,2,1,0:T(8,128)(2,1)S(1)}, bf16[1,2,1040,128]{3,2,1,0:T(8,128)(2,1)S(1)}, u32[]{:S(2)}, u32[]{:S(2)}) %collective-permute-start.11) | collective-permute-done | bytes 532512 | tf_op jit(solution)/shard_map/ppermute | solution.py:422
  44.6 1.3 %update.1 = bf16[128,2048]{1,0:T(8,128)(2,1)} custom-call(bf16[128,2048]{1,0:T(8,128)(2,1)S(1)} %copy-done.1, bf16[3,2,1040,128]{3,2,1,0:T(8,128)(2,1)S(1)} %get-tuple-element.26.refs_2_.rest_ref, bf16[1,2,1040,128]{3,2,1,0:T(8,128)(2,1)S(1)} %collective-permute-done.9.rest_0_, bf16[1,2,1040,128]{3,2,1,0:T(8,128)(2,1)S(1)} %collective-permute-done.11.rest_1_), custom_call_target="tpu_custom_call" | custom-call | flops 2621440 | bytes 3710976 | tf_op jit(solution)/shard_map/update/pallas_call | solution.py:308
  (2 shorter events, 0.0 us)
Async XLA Ops:
  0.6 1.4 %copy-start = (bf16[384,2048]{1,0:T(8,128)(2,1)S(1)}, bf16[384,2048]{1,0:T(8,128)(2,1)}, u32[]{:S(2)}) copy-start(bf16[384,2048]{1,0:T(8,128)(2,1)} %features_ref.13) | copy-start | bytes 4718596
  0.6 0.8 %copy-start.2 = (s32[1,384]{1,0:T(1,128)S(1)}, s32[1,384]{1,0:T(1,128)}, u32[]{:S(2)}) copy-start(s32[1,384]{1,0:T(1,128)} %labels_ref.10) | copy-start | bytes 4612
  2.1 0.7 %copy-start.3 = (s32[1,384]{1,0:T(1,128)S(1)}, s32[1,384]{1,0:T(1,128)}, u32[]{:S(2)}) copy-start(s32[1,384]{1,0:T(1,128)} %labels_ref.10) | copy-start | bytes 4612
  2.5 2.0 %collective-permute-start = (bf16[1,2,1040,128]{3,2,1,0:T(8,128)(2,1)S(1)}, bf16[1,2,1040,128]{3,2,1,0:T(8,128)(2,1)S(1)}, u32[]{:S(2)}, u32[]{:S(2)}) collective-permute-start(bf16[1,2,1040,128]{3,2,1,0:T(8,128)(2,1)S(1)} %away_first.1), channel_id=1, source_target_pairs={{0,4},{4,0},{8,12},{12,8},{16,20},{20,16},{24,28},{28,24},{1,5},{5... | collective-permute-start | bytes 1597448 | tf_op jit(solution)/shard_map/ppermute | solution.py:344
  4.1 1.6 %copy-start.1 = (bf16[128,2048]{1,0:T(8,128)(2,1)S(1)}, bf16[128,2048]{1,0:T(8,128)(2,1)}, u32[]{:S(2)}) copy-start(bf16[128,2048]{1,0:T(8,128)(2,1)} %memory_ref.1) | copy-start | bytes 1572868
  4.5 4.2 %collective-permute-start.6 = (bf16[3,2,1040,128]{3,2,1,0:T(8,128)(2,1)S(1)}, bf16[3,2,1040,128]{3,2,1,0:T(8,128)(2,1)S(1)}, u32[]{:S(2)}, u32[]{:S(2)}) collective-permute-start(bf16[3,2,1040,128]{3,2,1,0:T(8,128)(2,1)S(1)} %away_rest.1), channel_id=1, source_target_pairs={{0,4},{4,0},{8,12},{12,8},{16,20},{20,16},{24,28},{28,24},{1,5},{5... | collective-permute-start | bytes 4792328 | tf_op jit(solution)/shard_map/ppermute | solution.py:366
  4.7 9.2 %collective-permute-start.3 = (bf16[1040,128]{1,0:T(8,128)(2,1)S(1)}, bf16[1040,128]{1,0:T(8,128)(2,1)S(1)}, u32[]{:S(2)}, u32[]{:S(2)}) collective-permute-start(bf16[1040,128]{1,0:T(8,128)(2,1)S(1)} %get-tuple-element.21.refs_0_), channel_id=1, source_target_pairs={{0,8},{4,12},{8,0},{12,4},{16,24},{20,28},{24,16},{28,20},{1,9},{5... | collective-permute-start | bytes 798728 | tf_op jit(solution)/shard_map/ppermute | solution.py:392
  5.7 16.1 %collective-permute-start.1 = (bf16[128,2048]{1,0:T(8,128)(2,1)S(1)}, bf16[128,2048]{1,0:T(8,128)(2,1)S(1)}, u32[]{:S(2)}, u32[]{:S(2)}) collective-permute-start(bf16[128,2048]{1,0:T(8,128)(2,1)S(1)} %copy-done.1), channel_id=1, source_target_pairs={{0,1},{1,0},{2,3},{3,2},{4,5},{5,4},{6,7},{7,6},{8,9},{9,8},{10,11... | collective-permute-start | bytes 1572872 | tf_op jit(solution)/shard_map/ppermute | solution.py:373
  5.7 16.1 %collective-permute-start.2 = (bf16[128,2048]{1,0:T(8,128)(2,1)S(1)}, bf16[128,2048]{1,0:T(8,128)(2,1)S(1)}, u32[]{:S(2)}, u32[]{:S(2)}) collective-permute-start(bf16[128,2048]{1,0:T(8,128)(2,1)S(1)} %copy-done.1), channel_id=1, source_target_pairs={{0,2},{1,3},{2,0},{3,1},{4,6},{5,7},{6,4},{7,5},{8,10},{9,11},{10,... | collective-permute-start | bytes 1572872 | tf_op jit(solution)/shard_map/ppermute | solution.py:373
  7.7 11.9 %collective-permute-start.7 = (bf16[1040,128]{1,0:T(8,128)(2,1)S(1)}, bf16[1040,128]{1,0:T(8,128)(2,1)S(1)}, u32[]{:S(2)}, u32[]{:S(2)}) collective-permute-start(bf16[1040,128]{1,0:T(8,128)(2,1)S(1)} %get-tuple-element.27.refs_1_), channel_id=1, source_target_pairs={{0,8},{4,12},{8,0},{12,4},{16,24},{20,28},{24,16},{28,20},{1,9},{5... | collective-permute-start | bytes 798728 | tf_op jit(solution)/shard_map/ppermute | solution.py:392
  10.2 20.8 %collective-permute-start.10 = (bf16[1,2,1040,128]{3,2,1,0:T(8,128)(2,1)S(1)}, bf16[1,2,1040,128]{3,2,1,0:T(8,128)(2,1)S(1)}, u32[]{:S(2)}, u32[]{:S(2)}) collective-permute-start(bf16[1,2,1040,128]{3,2,1,0:T(8,128)(2,1)S(1)} %get-tuple-element.29), channel_id=1, source_target_pairs={{0,8},{4,12},{8,0},{12,4},{16,24},{20,28},{24,16},{28,20},{1,9},{5... | collective-permute-start | bytes 1597448 | tf_op jit(solution)/shard_map/ppermute | solution.py:417
  14.3 7.8 %collective-permute-start.4 = (bf16[1040,128]{1,0:T(8,128)(2,1)S(1)}, bf16[1040,128]{1,0:T(8,128)(2,1)S(1)}, u32[]{:S(2)}, u32[]{:S(2)}) collective-permute-start(bf16[1040,128]{1,0:T(8,128)(2,1)S(1)} %join_half.2), channel_id=1, source_target_pairs={{8,16},{12,20},{16,8},{20,12},{0,4},{4,0},{24,28},{28,24},{9,17},{... | collective-permute-start | bytes 798728 | tf_op jit(solution)/shard_map/ppermute | solution.py:410
  20.0 7.8 %collective-permute-start.8 = (bf16[1040,128]{1,0:T(8,128)(2,1)S(1)}, bf16[1040,128]{1,0:T(8,128)(2,1)S(1)}, u32[]{:S(2)}, u32[]{:S(2)}) collective-permute-start(bf16[1040,128]{1,0:T(8,128)(2,1)S(1)} %join_half.3), channel_id=1, source_target_pairs={{8,16},{12,20},{16,8},{20,12},{0,4},{4,0},{24,28},{28,24},{9,17},{... | collective-permute-start | bytes 798728 | tf_op jit(solution)/shard_map/ppermute | solution.py:410
  22.1 12.8 %collective-permute-start.5 = (bf16[128,2048]{1,0:T(8,128)(2,1)S(1)}, bf16[128,2048]{1,0:T(8,128)(2,1)S(1)}, u32[]{:S(2)}, u32[]{:S(2)}) collective-permute-start(bf16[128,2048]{1,0:T(8,128)(2,1)S(1)} %collective-permute-done.1.rest_1_), channel_id=1, source_target_pairs={{0,2},{1,3},{2,0},{3,1},{4,6},{5,7},{6,4},{7,5},{8,10},{9,11},{10,... | collective-permute-start | bytes 1572872 | tf_op jit(solution)/shard_map/ppermute | solution.py:373
  28.0 6.9 %copy-start.4 = (s32[1,2]{1,0:T(1,128)S(1)}, s32[1,2]{1,0:T(1,128)}, u32[]{:S(2)}) copy-start(s32[1,2]{1,0:T(1,128)} %requests_ref.1) | copy-start | bytes 28
  28.0 6.9 %copy-start.5 = (s32[1,4]{1,0:T(1,128)S(1)}, s32[1,4]{1,0:T(1,128)}, u32[]{:S(2)}) copy-start(s32[1,4]{1,0:T(1,128)} %owners_ref.1) | copy-start | bytes 52
  28.0 13.9 %collective-permute-start.9 = (bf16[1,2,1040,128]{3,2,1,0:T(8,128)(2,1)S(1)}, bf16[1,2,1040,128]{3,2,1,0:T(8,128)(2,1)S(1)}, u32[]{:S(2)}, u32[]{:S(2)}) collective-permute-start(bf16[1,2,1040,128]{3,2,1,0:T(8,128)(2,1)S(1)} %join_even.1), channel_id=1, source_target_pairs={{0,8},{4,12},{8,0},{12,4},{16,24},{20,28},{24,16},{28,20},{1,9},{5... | collective-permute-start | bytes 1597448 | tf_op jit(solution)/shard_map/ppermute | solution.py:421
  31.1 13.5 %collective-permute-start.11 = (bf16[1,2,1040,128]{3,2,1,0:T(8,128)(2,1)S(1)}, bf16[1,2,1040,128]{3,2,1,0:T(8,128)(2,1)S(1)}, u32[]{:S(2)}, u32[]{:S(2)}) collective-permute-start(bf16[1,2,1040,128]{3,2,1,0:T(8,128)(2,1)S(1)} %join_odd.1), channel_id=1, source_target_pairs={{8,16},{12,20},{16,8},{20,12},{0,4},{4,0},{24,28},{28,24},{9,17},{... | collective-permute-start | bytes 1597448 | tf_op jit(solution)/shard_map/ppermute | solution.py:422

commit v8 on v6

--- a/solution.py
+++ b/solution.py
@@ -164,6 +164,12 @@
         write_sums(base, labels_ref, features_ref, block_rows, came, store, only=h)
 
 
+def join_second_kernel(h, mine_ref, came_ref, out_ref):
+    out_ref[...] = (
+        mine_ref[0, h].astype(jnp.float32) + came_ref[0, h].astype(jnp.float32)
+    ).astype(jnp.bfloat16)
+
+
 def join_kernel(layers, hop, odd, *refs):
     first_refs, rest_ref, came_refs, out_ref = (
         refs[:HALVES],
@@ -194,49 +200,47 @@
         add(lambda h: rest_ref[jnp.maximum(place - 1, 0), h])
 
 
-def update_kernel(layers, memory_ref, rest_ref, *rest):
+def update_kernel(layers, h, memory_ref, rest_ref, even_ref, odd_ref, *rest):
+    out_hbm, mixed_ref, out_ref, sem = rest[-4:]
     layer = lax.axis_index("region") // CORES
     place = jnp.where(layer < layers // 2, layers - 1 - layer, layer) - 1
-    came_refs, (out_hbm, mixed_ref, out_ref, sems) = rest[:-4], rest[-4:]
-    copies = []
     linked = has_odd(layers)
     block_rows, feat_width = memory_ref.shape
     half_rows = block_rows // HALVES
     slabs = feat_width // LANES
-    for h in range(HALVES):
-
-        def total(first, rows):
-            t = rest_ref[place, h, pl.ds(first, rows), :].astype(jnp.float32)
-            even, odd = (ref[0, h, pl.ds(first, rows), :].astype(jnp.float32) for ref in came_refs)
-            t = t + even + jnp.where(linked, odd, 0.0)
-            return t
-
-        digits = total(slabs * half_rows, EXTRA)
-        counts_row = digits[0:1, :] + BASE * digits[1:2, :]
-        row = lax.broadcasted_iota(jnp.int32, (half_rows, LANES), 0) + h * half_rows
-        lane = lax.broadcasted_iota(jnp.int32, (half_rows, LANES), 1)
-        counts = jnp.sum(jnp.where(row == lane, counts_row, 0.0), axis=1, keepdims=True)
-        seen = counts > 0
-        share = (1.0 - momentum_keep) / jnp.maximum(counts, 1.0)
-        squares = jnp.zeros((half_rows, LANES), jnp.float32)
-        for s in range(slabs):
-            old = memory_ref[pl.ds(h * half_rows, half_rows), pl.ds(s * LANES, LANES)].astype(
-                jnp.float32
-            )
-            added = total(s * half_rows, half_rows) * share
-            mixed = jnp.where(seen, momentum_keep * old + added, old)
-            mixed_ref[:, pl.ds(s * LANES, LANES)] = mixed
-            squares = squares + mixed * mixed
-        mean = jnp.sum(squares, axis=1, keepdims=True) * (1.0 / feat_width)
-        scale = lax.rsqrt(mean + 1e-06) * D ** (-0.5)
-        rows = pl.ds(h * half_rows, half_rows)
-        out_ref[rows, :] = (mixed_ref[...] * scale).astype(jnp.bfloat16)
-        copies.append(
-            pltpu.make_async_copy(out_ref.at[rows, :], out_hbm.at[rows, :], sems.at[h])
-        )
-        copies[h].start()
-    for copy in copies:
-        copy.wait()
+    half = pl.ds(h * half_rows, half_rows)
+
+    def total(first, rows):
+        part = pl.ds(first, rows)
+        mine = rest_ref[place, h, part, :].astype(jnp.float32)
+        even = even_ref[0, h, part, :].astype(jnp.float32)
+        odd = odd_ref[part, :] if len(odd_ref.shape) == 2 else odd_ref[0, h, part, :]
+        return mine + even + jnp.where(linked, odd.astype(jnp.float32), 0.0)
+
+    digits = total(slabs * half_rows, EXTRA)
+    counts_row = digits[0:1, :] + BASE * digits[1:2, :]
+    row = lax.broadcasted_iota(jnp.int32, (half_rows, LANES), 0) + h * half_rows
+    lane = lax.broadcasted_iota(jnp.int32, (half_rows, LANES), 1)
+    counts = jnp.sum(jnp.where(row == lane, counts_row, 0.0), axis=1, keepdims=True)
+    seen = counts > 0
+    share = jnp.where(seen, (1.0 - momentum_keep) / jnp.maximum(counts, 1.0), 0.0)
+    share = jnp.broadcast_to(share, (half_rows, LANES))
+    keep = jnp.broadcast_to(jnp.where(seen, momentum_keep, 1.0), (half_rows, LANES))
+    squares = jnp.zeros((half_rows, LANES), jnp.float32)
+    for s in range(slabs):
+        old = memory_ref[half, pl.ds(s * LANES, LANES)].astype(jnp.float32)
+        mixed = keep * old + share * total(s * half_rows, half_rows)
+        mixed_ref[:, pl.ds(s * LANES, LANES)] = mixed
+        squares = squares + mixed * mixed
+    mean = jnp.sum(squares, axis=1, keepdims=True) * (1.0 / feat_width)
+    scale = lax.rsqrt(mean + 1e-06) * D ** (-0.5)
+    scale = jnp.broadcast_to(scale, (half_rows, LANES))
+    for s in range(slabs):
+        columns = pl.ds(s * LANES, LANES)
+        out_ref[:, columns] = (mixed_ref[:, columns] * scale).astype(jnp.bfloat16)
+    copy = pltpu.make_async_copy(out_ref, out_hbm.at[half, :], sem)
+    copy.start()
+    copy.wait()
 
 
 def grad_kernel(requests_ref, owners_ref, features_ref, *rest):
@@ -294,7 +298,7 @@
     bf16 = jnp.bfloat16
     after = lax.optimization_barrier
 
-    def call(kernel, name, out_shape, operands, flops, scratch=(), smem=0, any_from=None, out_from_vmem=True):
+    def call(kernel, name, out_shape, operands, flops, scratch=(), smem=0, any_from=None, out_from_vmem=True, aliases={}):
         outs = out_shape if isinstance(out_shape, list) else [out_shape]
         flat, tree = jax.tree.flatten(operands)
         specs = [SMEM if i < smem else VMEM for i in range(len(flat))]
@@ -307,6 +311,7 @@
             in_specs=specs,
             out_specs=[out_spec] * len(outs) if isinstance(out_shape, list) else out_spec,
             scratch_shapes=list(scratch),
+            input_output_aliases=aliases,
             compiler_params=PARAMS,
             cost_estimate=pl.CostEstimate(
                 flops=flops,
@@ -413,9 +418,20 @@
     even_came = [lax.ppermute(second, "region", even)]
     for hop in range(2, layers - 1):
         even_next = joined(hop, False, odd_came)
-        odd_next = joined(hop, True, even_came)
+        if hop == 2:
+            odd_came = []
+            for h in range(HALVES):
+                leaves = call(
+                    part(join_second_kernel, h),
+                    "join_second",
+                    jax.ShapeDtypeStruct((pay_rows, LANES), bf16),
+                    (second, *even_came),
+                    10**9,
+                )
+                odd_came.append(lax.ppermute(leaves, "region", odd))
+        else:
+            odd_came = [lax.ppermute(joined(hop, True, even_came), "region", odd)]
         even_came = [lax.ppermute(even_next, "region", even)]
-        odd_came = [lax.ppermute(odd_next, "region", odd)]
 
     cand_count = requests.shape[1] * block_rows
     feat_grad = call(
@@ -432,19 +448,24 @@
         any_from=3,
     )
 
-    new_memory = call(
-        part(update_kernel, layers),
-        "update",
-        jax.ShapeDtypeStruct(memory.shape, bf16),
-        (memory, rest, *even_came, *odd_came),
-        10 * block_rows * feat_width,
-        scratch=(
-            pltpu.VMEM((half_rows, feat_width), jnp.float32),
-            pltpu.VMEM(memory.shape, bf16),
-            pltpu.SemaphoreType.DMA((HALVES,)),
-        ),
-        out_from_vmem=False,
-    )
+    new_memory = None
+    for h in range(HALVES):
+        before = () if new_memory is None else (new_memory,)
+        new_memory = call(
+            part(update_kernel, layers, h),
+            "update",
+            jax.ShapeDtypeStruct(memory.shape, bf16),
+            (memory, rest, even_came[0], odd_came[h if len(odd_came) > 1 else 0], *before),
+            5 * block_rows * feat_width,
+            scratch=(
+                pltpu.VMEM((half_rows, feat_width), jnp.float32),
+                pltpu.VMEM((half_rows, feat_width), bf16),
+                pltpu.SemaphoreType.DMA,
+            ),
+            any_from=4,
+            out_from_vmem=False,
+            aliases={4: 0} if before else {},
+        )
     return (feat_grad, new_memory)
 
 

time: 46.4 us -> 46 us (level)
  waiting for transfers between devices: 21.9 us -> 20.4 us
  Pallas kernels: 9.67 us -> 10.4 us
    ppermute x1 -> x0, waiting for transfers between devices: 2.76 us -> none  [on_device(): odd_came = [lax.ppermute(odd_next, 'region', odd)]]
    ppermute x2 -> x4, starting transfers between devices: 3.44 us -> 5.61 us  [on_device(): odd_came.append(lax.ppermute(leaves, 'region', odd))]
    ppermute x1 -> x0, starting transfers between devices: 1.74 us -> none  [on_device(): odd_came = [lax.ppermute(odd_next, 'region', odd)]]
    ppermute x2 -> x4, waiting for transfers between devices: 4.51 us -> 6.17 us  [on_device(): odd_came.append(lax.ppermute(leaves, 'region', odd))]
    pallas_call x11 -> x13, Pallas kernels: 9.67 us -> 10.4 us  [call(): pl.pallas_call(kernel, out_shape=out_shape, in_specs=specs, out_specs=[ou...]
  transfers between devices with their start and end apart: 12 -> 13, of which waited for: 9 -> 9; matrix products, arithmetic and copies ran while one was open for 0% -> 0% of each run, Pallas kernels for 17% -> 19%
where the time goes in v8:
time: 46 us; the launch traced here: 45.6 us
  waiting for transfers between devices  20.4 us (44%)
  starting transfers between devices  12.5 us (27%)
  Pallas kernels  10.4 us (23%)
  local copies, waits for them, and re-layouts  1.52 us (3%)
  between operations  0.75 us (2%)
    pallas_call x13, Pallas kernels, call(): pl.pallas_call(kernel, out_shape=out_shape, in_specs=specs, out_specs=[ou...  10.4 us
    ppermute x2, waiting for transfers between devices, on_device(): even_came = [lax.ppermute(x, 'region', even) for x in first]  6.21 us
    ppermute x4, waiting for transfers between devices, on_device(): odd_came.append(lax.ppermute(leaves, 'region', odd))  6.17 us
    ppermute x4, starting transfers between devices, on_device(): odd_came.append(lax.ppermute(leaves, 'region', odd))  5.61 us
    ppermute x3, starting transfers between devices, fetch(): lax.ppermute(block, 'group', [(g, g ^ step) for g in range(group_count)])  3.57 us
    ppermute x1, waiting for transfers between devices, on_device(): even_came = [lax.ppermute(even_next, 'region', even)]  3.11 us
    ppermute x1, waiting for transfers between devices, on_device(): even_came = [lax.ppermute(second, 'region', even)]  2.97 us
    ppermute x2, starting transfers between devices, on_device(): even_came = [lax.ppermute(x, 'region', even) for x in first]  2.02 us
  transfers between devices with their start and end apart: 13, of which 9 were waited for; matrix products, arithmetic and copies ran while one was open for 0% of the time, Pallas kernels for 19%

profile of v8, /device:TPU:10, one launch (start us, length us, event | category | flops | bytes accessed | tf_op | source)
XLA Modules:
  0.0 45.6 jit_solution(17710607393625778265)
XLA Ops:
  0.6 0.0 copy-start
  0.6 0.0 copy-start.2
  0.7 0.8 %copy-done.2 = s32[1,384]{1,0:T(1,128)S(1)} copy-done((s32[1,384]{1,0:T(1,128)S(1)}, s32[1,384]{1,0:T(1,128)}, u32[]{:S(2)}) %copy-start.2) | copy-done | bytes 1560
  1.5 0.6 %copy-done = bf16[384,2048]{1,0:T(8,128)(2,1)S(1)} copy-done((bf16[384,2048]{1,0:T(8,128)(2,1)S(1)}, bf16[384,2048]{1,0:T(8,128)(2,1)}, u32[]{:S(2)}) %copy-start) | copy-done | bytes 1572888
  2.1 0.5 %away_first.1 = bf16[1,2,1040,128]{3,2,1,0:T(8,128)(2,1)S(1)} custom-call(bf16[128,384]{1,0:T(8,128)(2,1)S(1)} %match_first.1.match_ref, bf16[384,2048]{1,0:T(8,128)(2,1)S(1)} %copy-done), custom_call_target="tpu_custom_call" | custom-call | flops 201326592 | bytes 2203648 | tf_op jit(solution)/shard_map/away_first/pallas_call | solution.py:308
  2.5 0.1 collective-permute-start
  2.6 0.1 copy-done.3
  2.7 1.3 %away_rest.1 = bf16[3,2,1040,128]{3,2,1,0:T(8,128)(2,1)S(1)} custom-call(s32[1,384]{1,0:T(1,128)S(1)} %copy-done.3, bf16[384,2048]{1,0:T(8,128)(2,1)S(1)} %copy-done), custom_call_target="tpu_custom_call" | custom-call | flops 603979776 | bytes 3171072 | tf_op jit(solution)/shard_map/away_rest/pallas_call | solution.py:308
  4.1 0.0 copy-start.1
  4.1 0.4 collective-permute-done.came_ref.sibling_ref
  4.5 0.1 collective-permute-start.6
  4.7 1.0 %collective-permute-start.3 = (bf16[1040,128]{1,0:T(8,128)(2,1)S(1)}, bf16[1040,128]{1,0:T(8,128)(2,1)S(1)}, u32[]{:S(2)}, u32[]{:S(2)}) collective-permute-start(bf16[1040,128]{1,0:T(8,128)(2,1)S(1)} %get-tuple-element.21.refs_0_), channel_id=1, source_target_pairs={{0,8},{4,12},{8,0},{12,4},{16,24},{20,28},{24,16},{28,20},{1,9},{5... | collective-permute-start | bytes 798728 | tf_op jit(solution)/shard_map/ppermute | solution.py:393
  5.7 0.0 copy-done.1
  5.7 0.0 collective-permute-start.1
  5.7 2.0 %collective-permute-start.2 = (bf16[128,2048]{1,0:T(8,128)(2,1)S(1)}, bf16[128,2048]{1,0:T(8,128)(2,1)S(1)}, u32[]{:S(2)}, u32[]{:S(2)}) collective-permute-start(bf16[128,2048]{1,0:T(8,128)(2,1)S(1)} %copy-done.1), channel_id=1, source_target_pairs={{0,2},{1,3},{2,0},{3,1},{4,6},{5,7},{6,4},{7,5},{8,10},{9,11},{10,... | collective-permute-start | bytes 1572872 | tf_op jit(solution)/shard_map/ppermute | solution.py:374
  7.7 1.0 %collective-permute-start.7 = (bf16[1040,128]{1,0:T(8,128)(2,1)S(1)}, bf16[1040,128]{1,0:T(8,128)(2,1)S(1)}, u32[]{:S(2)}, u32[]{:S(2)}) collective-permute-start(bf16[1040,128]{1,0:T(8,128)(2,1)S(1)} %get-tuple-element.27.refs_1_), channel_id=1, source_target_pairs={{0,8},{4,12},{8,0},{12,4},{16,24},{20,28},{24,16},{28,20},{1,9},{5... | collective-permute-start | bytes 798728 | tf_op jit(solution)/shard_map/ppermute | solution.py:393
  8.7 0.0 collective-permute-done.6.came_ref
  8.7 1.4 %chip_rest.1 = (bf16[1,2,1040,128]{3,2,1,0:T(8,128)(2,1)S(1)}, bf16[3,2,1040,128]{3,2,1,0:T(8,128)(2,1)S(1)}) custom-call(s32[1,384]{1,0:T(1,128)S(1)} %copy-done.3, bf16[384,2048]{1,0:T(8,128)(2,1)S(1)} %copy-done, bf16[3,2,1040,128]{3,2,1,0:T(8,128)(2,1)S(1)} %collective-permute-done.6.came_ref), custom_call_target="tpu_custom_call" | custom-call | flops 603979776 | bytes 5300992 | tf_op jit(solution)/shard_map/chip_rest/pallas_call | solution.py:308
  10.2 1.1 %collective-permute-start.10 = (bf16[1,2,1040,128]{3,2,1,0:T(8,128)(2,1)S(1)}, bf16[1,2,1040,128]{3,2,1,0:T(8,128)(2,1)S(1)}, u32[]{:S(2)}, u32[]{:S(2)}) collective-permute-start(bf16[1,2,1040,128]{3,2,1,0:T(8,128)(2,1)S(1)} %get-tuple-element.29.mine_ref), channel_id=1, source_target_pairs={{0,8},{4,12},{8,0},{12,4},{16,24},{20,28},{24,16},{28,20},{1,9},{5... | collective-permute-start | bytes 1597448 | tf_op jit(solution)/shard_map/ppermute | solution.py:418
  11.2 2.7 %collective-permute-done.3.came_ref = bf16[1040,128]{1,0:T(8,128)(2,1)S(1)} collective-permute-done((bf16[1040,128]{1,0:T(8,128)(2,1)S(1)}, bf16[1040,128]{1,0:T(8,128)(2,1)S(1)}, u32[]{:S(2)}, u32[]{:S(2)}) %collective-permute-start.3) | collective-permute-done | bytes 266272 | tf_op jit(solution)/shard_map/ppermute | solution.py:393
  13.9 0.4 join_half.2
  14.3 1.7 %collective-permute-start.4 = (bf16[1040,128]{1,0:T(8,128)(2,1)S(1)}, bf16[1040,128]{1,0:T(8,128)(2,1)S(1)}, u32[]{:S(2)}, u32[]{:S(2)}) collective-permute-start(bf16[1040,128]{1,0:T(8,128)(2,1)S(1)} %join_half.2), channel_id=1, source_target_pairs={{8,16},{12,20},{16,8},{20,12},{0,4},{4,0},{24,28},{28,24},{9,17},{... | collective-permute-start | bytes 798728 | tf_op jit(solution)/shard_map/ppermute | solution.py:411
  16.0 3.5 %collective-permute-done.7.came_ref = bf16[1040,128]{1,0:T(8,128)(2,1)S(1)} collective-permute-done((bf16[1040,128]{1,0:T(8,128)(2,1)S(1)}, bf16[1040,128]{1,0:T(8,128)(2,1)S(1)}, u32[]{:S(2)}, u32[]{:S(2)}) %collective-permute-start.7) | collective-permute-done | bytes 266272 | tf_op jit(solution)/shard_map/ppermute | solution.py:393
  19.6 0.4 join_half.3
  20.0 1.7 %collective-permute-start.8 = (bf16[1040,128]{1,0:T(8,128)(2,1)S(1)}, bf16[1040,128]{1,0:T(8,128)(2,1)S(1)}, u32[]{:S(2)}, u32[]{:S(2)}) collective-permute-start(bf16[1040,128]{1,0:T(8,128)(2,1)S(1)} %join_half.3), channel_id=1, source_target_pairs={{8,16},{12,20},{16,8},{20,12},{0,4},{4,0},{24,28},{28,24},{9,17},{... | collective-permute-start | bytes 798728 | tf_op jit(solution)/shard_map/ppermute | solution.py:411
  21.8 0.0 collective-permute-done.1.rest_1_
  21.8 0.0 collective-permute-done.2.rest_2_
  21.8 0.3 collective-permute-done.4.refs_3_
  22.1 1.5 %collective-permute-start.5 = (bf16[128,2048]{1,0:T(8,128)(2,1)S(1)}, bf16[128,2048]{1,0:T(8,128)(2,1)S(1)}, u32[]{:S(2)}, u32[]{:S(2)}) collective-permute-start(bf16[128,2048]{1,0:T(8,128)(2,1)S(1)} %collective-permute-done.1.rest_1_), channel_id=1, source_target_pairs={{0,2},{1,3},{2,0},{3,1},{4,6},{5,7},{6,4},{7,5},{8,10},{9,11},{10,... | collective-permute-start | bytes 1572872 | tf_op jit(solution)/shard_map/ppermute | solution.py:374
  23.6 4.2 %collective-permute-done.8.refs_4_ = bf16[1040,128]{1,0:T(8,128)(2,1)S(1)} collective-permute-done((bf16[1040,128]{1,0:T(8,128)(2,1)S(1)}, bf16[1040,128]{1,0:T(8,128)(2,1)S(1)}, u32[]{:S(2)}, u32[]{:S(2)}) %collective-permute-start.8) | collective-permute-done | bytes 266272 | tf_op jit(solution)/shard_map/ppermute | solution.py:411
  27.8 0.2 join_even.1
  28.0 0.1 collective-permute-start.9
  28.0 3.0 %collective-permute-done.10.came_ref = bf16[1,2,1040,128]{3,2,1,0:T(8,128)(2,1)S(1)} collective-permute-done((bf16[1,2,1040,128]{3,2,1,0:T(8,128)(2,1)S(1)}, bf16[1,2,1040,128]{3,2,1,0:T(8,128)(2,1)S(1)}, u32[]{:S(2)}, u32[]{:S(2)}) %collective-permute-start.10) | collective-permute-done | bytes 532512 | tf_op jit(solution)/shard_map/ppermute | solution.py:418
  31.0 0.1 join_second.3
  31.1 0.0 copy-start.4
  31.1 0.0 copy-start.5
  31.1 1.7 %collective-permute-start.12 = (bf16[1040,128]{1,0:T(8,128)(2,1)S(1)}, bf16[1040,128]{1,0:T(8,128)(2,1)S(1)}, u32[]{:S(2)}, u32[]{:S(2)}) collective-permute-start(bf16[1040,128]{1,0:T(8,128)(2,1)S(1)} %join_second.3), channel_id=1, source_target_pairs={{8,16},{12,20},{16,8},{20,12},{0,4},{4,0},{24,28},{28,24},{9,17},{... | collective-permute-start | bytes 798728 | tf_op jit(solution)/shard_map/ppermute | solution.py:431
  32.8 0.1 join_second.2
  32.9 0.4 collective-permute-start.11
  33.3 1.5 %collective-permute-done.5.rest_3_ = bf16[128,2048]{1,0:T(8,128)(2,1)S(1)} collective-permute-done((bf16[128,2048]{1,0:T(8,128)(2,1)S(1)}, bf16[128,2048]{1,0:T(8,128)(2,1)S(1)}, u32[]{:S(2)}, u32[]{:S(2)}) %collective-permute-start.5) | collective-permute-done | bytes 524320 | tf_op jit(solution)/shard_map/ppermute | solution.py:374
  34.9 0.0 copy-done.4
  34.9 0.0 copy-done.5
  34.9 3.9 %feat_grad.1 = bf16[384,2048]{1,0:T(8,128)(2,1)} custom-call(s32[1,2]{1,0:T(1,128)S(1)} %copy-done.4, s32[1,4]{1,0:T(1,128)S(1)} %copy-done.5, bf16[384,2048]{1,0:T(8,128)(2,1)S(1)} %copy-done, bf16[128,2048]{1,0:T(8,128)(2,1)S(1)} %copy-done.1, bf16[128,2048]{1,0:T(8,128)(2,1)S(1)} %collective-permute-done.1.rest_1_, ...), custom_call_target="tpu_custom_call" | custom-call | flops 805306368 | bytes 5242892 | tf_op jit(solution)/shard_map/feat_grad/pallas_call | solution.py:308
  38.7 3.1 %collective-permute-done.9.even_ref = bf16[1,2,1040,128]{3,2,1,0:T(8,128)(2,1)S(1)} collective-permute-done((bf16[1,2,1040,128]{3,2,1,0:T(8,128)(2,1)S(1)}, bf16[1,2,1040,128]{3,2,1,0:T(8,128)(2,1)S(1)}, u32[]{:S(2)}, u32[]{:S(2)}) %collective-permute-start.9) | collective-permute-done | bytes 532512 | tf_op jit(solution)/shard_map/ppermute | solution.py:434
  41.9 0.0 collective-permute-done.12.odd_ref
  41.9 1.1 %update.2.rest_0_ = bf16[128,2048]{1,0:T(8,128)(2,1)} custom-call(bf16[128,2048]{1,0:T(8,128)(2,1)S(1)} %copy-done.1, bf16[3,2,1040,128]{3,2,1,0:T(8,128)(2,1)S(1)} %get-tuple-element.26.refs_2_.rest_ref, bf16[1,2,1040,128]{3,2,1,0:T(8,128)(2,1)S(1)} %collective-permute-done.9.even_ref, bf16[1040,128]{1,0:T(8,128)(2,1)S(1)} %collective-permute-done.12.odd_ref), custom_call_target="tpu_custom_call" | custom-call | flops 1310720 | bytes 3444736 | tf_op jit(solution)/shard_map/update/pallas_call | solution.py:308
  42.9 1.7 %collective-permute-done.11.odd_ref = bf16[1040,128]{1,0:T(8,128)(2,1)S(1)} collective-permute-done((bf16[1040,128]{1,0:T(8,128)(2,1)S(1)}, bf16[1040,128]{1,0:T(8,128)(2,1)S(1)}, u32[]{:S(2)}, u32[]{:S(2)}) %collective-permute-start.11) | collective-permute-done | bytes 266272 | tf_op jit(solution)/shard_map/ppermute | solution.py:431
  44.6 1.0 %update.3 = bf16[128,2048]{1,0:T(8,128)(2,1)} custom-call(bf16[128,2048]{1,0:T(8,128)(2,1)S(1)} %copy-done.1, bf16[3,2,1040,128]{3,2,1,0:T(8,128)(2,1)S(1)} %get-tuple-element.26.refs_2_.rest_ref, bf16[1,2,1040,128]{3,2,1,0:T(8,128)(2,1)S(1)} %collective-permute-done.9.even_ref, ...), custom_call_target="tpu_custom_call", output_to_operand_aliasing={{}: (4, {})} | custom-call | flops 1310720 | bytes 3969024 | tf_op jit(solution)/shard_map/update/pallas_call | solution.py:308
  (3 shorter events, 0.0 us)
Async XLA Ops:
  0.6 1.4 %copy-start = (bf16[384,2048]{1,0:T(8,128)(2,1)S(1)}, bf16[384,2048]{1,0:T(8,128)(2,1)}, u32[]{:S(2)}) copy-start(bf16[384,2048]{1,0:T(8,128)(2,1)} %features_ref.13) | copy-start | bytes 4718596
  0.6 0.8 %copy-start.2 = (s32[1,384]{1,0:T(1,128)S(1)}, s32[1,384]{1,0:T(1,128)}, u32[]{:S(2)}) copy-start(s32[1,384]{1,0:T(1,128)} %labels_ref.10) | copy-start | bytes 4612
  2.1 0.7 %copy-start.3 = (s32[1,384]{1,0:T(1,128)S(1)}, s32[1,384]{1,0:T(1,128)}, u32[]{:S(2)}) copy-start(s32[1,384]{1,0:T(1,128)} %labels_ref.10) | copy-start | bytes 4612
  2.5 2.0 %collective-permute-start = (bf16[1,2,1040,128]{3,2,1,0:T(8,128)(2,1)S(1)}, bf16[1,2,1040,128]{3,2,1,0:T(8,128)(2,1)S(1)}, u32[]{:S(2)}, u32[]{:S(2)}) collective-permute-start(bf16[1,2,1040,128]{3,2,1,0:T(8,128)(2,1)S(1)} %away_first.1), channel_id=1, source_target_pairs={{0,4},{4,0},{8,12},{12,8},{16,20},{20,16},{24,28},{28,24},{1,5},{5... | collective-permute-start | bytes 1597448 | tf_op jit(solution)/shard_map/ppermute | solution.py:345
  4.1 1.6 %copy-start.1 = (bf16[128,2048]{1,0:T(8,128)(2,1)S(1)}, bf16[128,2048]{1,0:T(8,128)(2,1)}, u32[]{:S(2)}) copy-start(bf16[128,2048]{1,0:T(8,128)(2,1)} %memory_ref.3) | copy-start | bytes 1572868
  4.5 4.2 %collective-permute-start.6 = (bf16[3,2,1040,128]{3,2,1,0:T(8,128)(2,1)S(1)}, bf16[3,2,1040,128]{3,2,1,0:T(8,128)(2,1)S(1)}, u32[]{:S(2)}, u32[]{:S(2)}) collective-permute-start(bf16[3,2,1040,128]{3,2,1,0:T(8,128)(2,1)S(1)} %away_rest.1), channel_id=1, source_target_pairs={{0,4},{4,0},{8,12},{12,8},{16,20},{20,16},{24,28},{28,24},{1,5},{5... | collective-permute-start | bytes 4792328 | tf_op jit(solution)/shard_map/ppermute | solution.py:367
  4.7 9.2 %collective-permute-start.3 = (bf16[1040,128]{1,0:T(8,128)(2,1)S(1)}, bf16[1040,128]{1,0:T(8,128)(2,1)S(1)}, u32[]{:S(2)}, u32[]{:S(2)}) collective-permute-start(bf16[1040,128]{1,0:T(8,128)(2,1)S(1)} %get-tuple-element.21.refs_0_), channel_id=1, source_target_pairs={{0,8},{4,12},{8,0},{12,4},{16,24},{20,28},{24,16},{28,20},{1,9},{5... | collective-permute-start | bytes 798728 | tf_op jit(solution)/shard_map/ppermute | solution.py:393
  5.7 16.1 %collective-permute-start.1 = (bf16[128,2048]{1,0:T(8,128)(2,1)S(1)}, bf16[128,2048]{1,0:T(8,128)(2,1)S(1)}, u32[]{:S(2)}, u32[]{:S(2)}) collective-permute-start(bf16[128,2048]{1,0:T(8,128)(2,1)S(1)} %copy-done.1), channel_id=1, source_target_pairs={{0,1},{1,0},{2,3},{3,2},{4,5},{5,4},{6,7},{7,6},{8,9},{9,8},{10,11... | collective-permute-start | bytes 1572872 | tf_op jit(solution)/shard_map/ppermute | solution.py:374
  5.7 16.1 %collective-permute-start.2 = (bf16[128,2048]{1,0:T(8,128)(2,1)S(1)}, bf16[128,2048]{1,0:T(8,128)(2,1)S(1)}, u32[]{:S(2)}, u32[]{:S(2)}) collective-permute-start(bf16[128,2048]{1,0:T(8,128)(2,1)S(1)} %copy-done.1), channel_id=1, source_target_pairs={{0,2},{1,3},{2,0},{3,1},{4,6},{5,7},{6,4},{7,5},{8,10},{9,11},{10,... | collective-permute-start | bytes 1572872 | tf_op jit(solution)/shard_map/ppermute | solution.py:374
  7.7 11.9 %collective-permute-start.7 = (bf16[1040,128]{1,0:T(8,128)(2,1)S(1)}, bf16[1040,128]{1,0:T(8,128)(2,1)S(1)}, u32[]{:S(2)}, u32[]{:S(2)}) collective-permute-start(bf16[1040,128]{1,0:T(8,128)(2,1)S(1)} %get-tuple-element.27.refs_1_), channel_id=1, source_target_pairs={{0,8},{4,12},{8,0},{12,4},{16,24},{20,28},{24,16},{28,20},{1,9},{5... | collective-permute-start | bytes 798728 | tf_op jit(solution)/shard_map/ppermute | solution.py:393
  10.2 20.8 %collective-permute-start.10 = (bf16[1,2,1040,128]{3,2,1,0:T(8,128)(2,1)S(1)}, bf16[1,2,1040,128]{3,2,1,0:T(8,128)(2,1)S(1)}, u32[]{:S(2)}, u32[]{:S(2)}) collective-permute-start(bf16[1,2,1040,128]{3,2,1,0:T(8,128)(2,1)S(1)} %get-tuple-element.29.mine_ref), channel_id=1, source_target_pairs={{0,8},{4,12},{8,0},{12,4},{16,24},{20,28},{24,16},{28,20},{1,9},{5... | collective-permute-start | bytes 1597448 | tf_op jit(solution)/shard_map/ppermute | solution.py:418
  14.3 7.8 %collective-permute-start.4 = (bf16[1040,128]{1,0:T(8,128)(2,1)S(1)}, bf16[1040,128]{1,0:T(8,128)(2,1)S(1)}, u32[]{:S(2)}, u32[]{:S(2)}) collective-permute-start(bf16[1040,128]{1,0:T(8,128)(2,1)S(1)} %join_half.2), channel_id=1, source_target_pairs={{8,16},{12,20},{16,8},{20,12},{0,4},{4,0},{24,28},{28,24},{9,17},{... | collective-permute-start | bytes 798728 | tf_op jit(solution)/shard_map/ppermute | solution.py:411
  20.0 7.8 %collective-permute-start.8 = (bf16[1040,128]{1,0:T(8,128)(2,1)S(1)}, bf16[1040,128]{1,0:T(8,128)(2,1)S(1)}, u32[]{:S(2)}, u32[]{:S(2)}) collective-permute-start(bf16[1040,128]{1,0:T(8,128)(2,1)S(1)} %join_half.3), channel_id=1, source_target_pairs={{8,16},{12,20},{16,8},{20,12},{0,4},{4,0},{24,28},{28,24},{9,17},{... | collective-permute-start | bytes 798728 | tf_op jit(solution)/shard_map/ppermute | solution.py:411
  22.1 12.8 %collective-permute-start.5 = (bf16[128,2048]{1,0:T(8,128)(2,1)S(1)}, bf16[128,2048]{1,0:T(8,128)(2,1)S(1)}, u32[]{:S(2)}, u32[]{:S(2)}) collective-permute-start(bf16[128,2048]{1,0:T(8,128)(2,1)S(1)} %collective-permute-done.1.rest_1_), channel_id=1, source_target_pairs={{0,2},{1,3},{2,0},{3,1},{4,6},{5,7},{6,4},{7,5},{8,10},{9,11},{10,... | collective-permute-start | bytes 1572872 | tf_op jit(solution)/shard_map/ppermute | solution.py:374
  28.0 13.9 %collective-permute-start.9 = (bf16[1,2,1040,128]{3,2,1,0:T(8,128)(2,1)S(1)}, bf16[1,2,1040,128]{3,2,1,0:T(8,128)(2,1)S(1)}, u32[]{:S(2)}, u32[]{:S(2)}) collective-permute-start(bf16[1,2,1040,128]{3,2,1,0:T(8,128)(2,1)S(1)} %join_even.1), channel_id=1, source_target_pairs={{0,8},{4,12},{8,0},{12,4},{16,24},{20,28},{24,16},{28,20},{1,9},{5... | collective-permute-start | bytes 1597448 | tf_op jit(solution)/shard_map/ppermute | solution.py:434
  31.1 3.8 %copy-start.4 = (s32[1,2]{1,0:T(1,128)S(1)}, s32[1,2]{1,0:T(1,128)}, u32[]{:S(2)}) copy-start(s32[1,2]{1,0:T(1,128)} %requests_ref.1) | copy-start | bytes 28
  31.1 3.8 %copy-start.5 = (s32[1,4]{1,0:T(1,128)S(1)}, s32[1,4]{1,0:T(1,128)}, u32[]{:S(2)}) copy-start(s32[1,4]{1,0:T(1,128)} %owners_ref.1) | copy-start | bytes 52
  31.1 10.8 %collective-permute-start.12 = (bf16[1040,128]{1,0:T(8,128)(2,1)S(1)}, bf16[1040,128]{1,0:T(8,128)(2,1)S(1)}, u32[]{:S(2)}, u32[]{:S(2)}) collective-permute-start(bf16[1040,128]{1,0:T(8,128)(2,1)S(1)} %join_second.3), channel_id=1, source_target_pairs={{8,16},{12,20},{16,8},{20,12},{0,4},{4,0},{24,28},{28,24},{9,17},{... | collective-permute-start | bytes 798728 | tf_op jit(solution)/shard_map/ppermute | solution.py:431
  32.9 11.7 %collective-permute-start.11 = (bf16[1040,128]{1,0:T(8,128)(2,1)S(1)}, bf16[1040,128]{1,0:T(8,128)(2,1)S(1)}, u32[]{:S(2)}, u32[]{:S(2)}) collective-permute-start(bf16[1040,128]{1,0:T(8,128)(2,1)S(1)} %join_second.2), channel_id=1, source_target_pairs={{8,16},{12,20},{16,8},{20,12},{0,4},{4,0},{24,28},{28,24},{9,17},{... | collective-permute-start | bytes 798728 | tf_op jit(solution)/shard_map/ppermute | solution.py:431

commit v9 on v8

--- a/solution.py
+++ b/solution.py
@@ -234,13 +234,23 @@
         squares = squares + mixed * mixed
     mean = jnp.sum(squares, axis=1, keepdims=True) * (1.0 / feat_width)
     scale = lax.rsqrt(mean + 1e-06) * D ** (-0.5)
-    scale = jnp.broadcast_to(scale, (half_rows, LANES))
-    for s in range(slabs):
-        columns = pl.ds(s * LANES, LANES)
-        out_ref[:, columns] = (mixed_ref[:, columns] * scale).astype(jnp.bfloat16)
-    copy = pltpu.make_async_copy(out_ref, out_hbm.at[half, :], sem)
-    copy.start()
-    copy.wait()
+    copies = []
+    for i in range(half_rows // EXTRA):
+        rows = pl.ds(i * EXTRA, EXTRA)
+        rows_scale = jnp.broadcast_to(scale[i * EXTRA : (i + 1) * EXTRA], (EXTRA, LANES))
+        for s in range(slabs):
+            columns = pl.ds(s * LANES, LANES)
+            out_ref[rows, columns] = (mixed_ref[rows, columns] * rows_scale).astype(jnp.bfloat16)
+        copies.append(
+            pltpu.make_async_copy(
+                out_ref.at[rows, :],
+                out_hbm.at[pl.ds(h * half_rows + i * EXTRA, EXTRA), :],
+                sem.at[i],
+            )
+        )
+        copies[i].start()
+    for copy in copies:
+        copy.wait()
 
 
 def grad_kernel(requests_ref, owners_ref, features_ref, *rest):
@@ -460,7 +470,7 @@
             scratch=(
                 pltpu.VMEM((half_rows, feat_width), jnp.float32),
                 pltpu.VMEM((half_rows, feat_width), bf16),
-                pltpu.SemaphoreType.DMA,
+                pltpu.SemaphoreType.DMA((half_rows // EXTRA,)),
             ),
             any_from=4,
             out_from_vmem=False,

time: 46 us -> 46 us (level)
  no operation moved by 1% of the time
where the time goes in v9:
time: 46 us; the launch traced here: 45.6 us
  waiting for transfers between devices  20.5 us (45%)
  starting transfers between devices  12.5 us (27%)
  Pallas kernels  10.3 us (22%)
  local copies, waits for them, and re-layouts  1.52 us (3%)
  between operations  0.75 us (2%)
    pallas_call x13, Pallas kernels, call(): pl.pallas_call(kernel, out_shape=out_shape, in_specs=specs, out_specs=[ou...  10.3 us
    ppermute x4, waiting for transfers between devices, on_device(): odd_came.append(lax.ppermute(leaves, 'region', odd))  6.21 us
    ppermute x2, waiting for transfers between devices, on_device(): even_came = [lax.ppermute(x, 'region', even) for x in first]  6.21 us
    ppermute x4, starting transfers between devices, on_device(): odd_came.append(lax.ppermute(leaves, 'region', odd))  5.61 us
    ppermute x3, starting transfers between devices, fetch(): lax.ppermute(block, 'group', [(g, g ^ step) for g in range(group_count)])  3.57 us
    ppermute x1, waiting for transfers between devices, on_device(): even_came = [lax.ppermute(even_next, 'region', even)]  3.11 us
    ppermute x1, waiting for transfers between devices, on_device(): even_came = [lax.ppermute(second, 'region', even)]  2.97 us
    ppermute x2, starting transfers between devices, on_device(): even_came = [lax.ppermute(x, 'region', even) for x in first]  2.02 us
  transfers between devices with their start and end apart: 13, of which 9 were waited for; matrix products, arithmetic and copies ran while one was open for 0% of the time, Pallas kernels for 19%

profile of v9, /device:TPU:10, one launch (start us, length us, event | category | flops | bytes accessed | tf_op | source)
XLA Modules:
  0.0 45.6 jit_solution(7236535706578379066)
XLA Ops:
  0.6 0.0 copy-start
  0.6 0.0 copy-start.2
  0.7 0.8 %copy-done.2 = s32[1,384]{1,0:T(1,128)S(1)} copy-done((s32[1,384]{1,0:T(1,128)S(1)}, s32[1,384]{1,0:T(1,128)}, u32[]{:S(2)}) %copy-start.2) | copy-done | bytes 1560
  1.5 0.6 %copy-done = bf16[384,2048]{1,0:T(8,128)(2,1)S(1)} copy-done((bf16[384,2048]{1,0:T(8,128)(2,1)S(1)}, bf16[384,2048]{1,0:T(8,128)(2,1)}, u32[]{:S(2)}) %copy-start) | copy-done | bytes 1572888
  2.1 0.5 %away_first.1 = bf16[1,2,1040,128]{3,2,1,0:T(8,128)(2,1)S(1)} custom-call(bf16[128,384]{1,0:T(8,128)(2,1)S(1)} %match_first.1.match_ref, bf16[384,2048]{1,0:T(8,128)(2,1)S(1)} %copy-done), custom_call_target="tpu_custom_call" | custom-call | flops 201326592 | bytes 2203648 | tf_op jit(solution)/shard_map/away_first/pallas_call | solution.py:318
  2.5 0.1 collective-permute-start
  2.6 0.1 copy-done.3
  2.7 1.3 %away_rest.1 = bf16[3,2,1040,128]{3,2,1,0:T(8,128)(2,1)S(1)} custom-call(s32[1,384]{1,0:T(1,128)S(1)} %copy-done.3, bf16[384,2048]{1,0:T(8,128)(2,1)S(1)} %copy-done), custom_call_target="tpu_custom_call" | custom-call | flops 603979776 | bytes 3171072 | tf_op jit(solution)/shard_map/away_rest/pallas_call | solution.py:318
  4.1 0.0 copy-start.1
  4.1 0.4 collective-permute-done.came_ref.sibling_ref
  4.5 0.1 collective-permute-start.6
  4.7 1.0 %collective-permute-start.3 = (bf16[1040,128]{1,0:T(8,128)(2,1)S(1)}, bf16[1040,128]{1,0:T(8,128)(2,1)S(1)}, u32[]{:S(2)}, u32[]{:S(2)}) collective-permute-start(bf16[1040,128]{1,0:T(8,128)(2,1)S(1)} %get-tuple-element.21.refs_0_), channel_id=1, source_target_pairs={{0,8},{4,12},{8,0},{12,4},{16,24},{20,28},{24,16},{28,20},{1,9},{5... | collective-permute-start | bytes 798728 | tf_op jit(solution)/shard_map/ppermute | solution.py:403
  5.7 0.0 copy-done.1
  5.7 0.0 collective-permute-start.1
  5.7 2.0 %collective-permute-start.2 = (bf16[128,2048]{1,0:T(8,128)(2,1)S(1)}, bf16[128,2048]{1,0:T(8,128)(2,1)S(1)}, u32[]{:S(2)}, u32[]{:S(2)}) collective-permute-start(bf16[128,2048]{1,0:T(8,128)(2,1)S(1)} %copy-done.1), channel_id=1, source_target_pairs={{0,2},{1,3},{2,0},{3,1},{4,6},{5,7},{6,4},{7,5},{8,10},{9,11},{10,... | collective-permute-start | bytes 1572872 | tf_op jit(solution)/shard_map/ppermute | solution.py:384
  7.7 1.0 %collective-permute-start.7 = (bf16[1040,128]{1,0:T(8,128)(2,1)S(1)}, bf16[1040,128]{1,0:T(8,128)(2,1)S(1)}, u32[]{:S(2)}, u32[]{:S(2)}) collective-permute-start(bf16[1040,128]{1,0:T(8,128)(2,1)S(1)} %get-tuple-element.27.refs_1_), channel_id=1, source_target_pairs={{0,8},{4,12},{8,0},{12,4},{16,24},{20,28},{24,16},{28,20},{1,9},{5... | collective-permute-start | bytes 798728 | tf_op jit(solution)/shard_map/ppermute | solution.py:403
  8.7 0.0 collective-permute-done.6.came_ref
  8.7 1.4 %chip_rest.1 = (bf16[1,2,1040,128]{3,2,1,0:T(8,128)(2,1)S(1)}, bf16[3,2,1040,128]{3,2,1,0:T(8,128)(2,1)S(1)}) custom-call(s32[1,384]{1,0:T(1,128)S(1)} %copy-done.3, bf16[384,2048]{1,0:T(8,128)(2,1)S(1)} %copy-done, bf16[3,2,1040,128]{3,2,1,0:T(8,128)(2,1)S(1)} %collective-permute-done.6.came_ref), custom_call_target="tpu_custom_call" | custom-call | flops 603979776 | bytes 5300992 | tf_op jit(solution)/shard_map/chip_rest/pallas_call | solution.py:318
  10.2 1.1 %collective-permute-start.10 = (bf16[1,2,1040,128]{3,2,1,0:T(8,128)(2,1)S(1)}, bf16[1,2,1040,128]{3,2,1,0:T(8,128)(2,1)S(1)}, u32[]{:S(2)}, u32[]{:S(2)}) collective-permute-start(bf16[1,2,1040,128]{3,2,1,0:T(8,128)(2,1)S(1)} %get-tuple-element.29.mine_ref), channel_id=1, source_target_pairs={{0,8},{4,12},{8,0},{12,4},{16,24},{20,28},{24,16},{28,20},{1,9},{5... | collective-permute-start | bytes 1597448 | tf_op jit(solution)/shard_map/ppermute | solution.py:428
  11.2 2.7 %collective-permute-done.3.came_ref = bf16[1040,128]{1,0:T(8,128)(2,1)S(1)} collective-permute-done((bf16[1040,128]{1,0:T(8,128)(2,1)S(1)}, bf16[1040,128]{1,0:T(8,128)(2,1)S(1)}, u32[]{:S(2)}, u32[]{:S(2)}) %collective-permute-start.3) | collective-permute-done | bytes 266272 | tf_op jit(solution)/shard_map/ppermute | solution.py:403
  13.9 0.4 join_half.2
  14.3 1.7 %collective-permute-start.4 = (bf16[1040,128]{1,0:T(8,128)(2,1)S(1)}, bf16[1040,128]{1,0:T(8,128)(2,1)S(1)}, u32[]{:S(2)}, u32[]{:S(2)}) collective-permute-start(bf16[1040,128]{1,0:T(8,128)(2,1)S(1)} %join_half.2), channel_id=1, source_target_pairs={{8,16},{12,20},{16,8},{20,12},{0,4},{4,0},{24,28},{28,24},{9,17},{... | collective-permute-start | bytes 798728 | tf_op jit(solution)/shard_map/ppermute | solution.py:421
  16.0 3.5 %collective-permute-done.7.came_ref = bf16[1040,128]{1,0:T(8,128)(2,1)S(1)} collective-permute-done((bf16[1040,128]{1,0:T(8,128)(2,1)S(1)}, bf16[1040,128]{1,0:T(8,128)(2,1)S(1)}, u32[]{:S(2)}, u32[]{:S(2)}) %collective-permute-start.7) | collective-permute-done | bytes 266272 | tf_op jit(solution)/shard_map/ppermute | solution.py:403
  19.6 0.4 join_half.3
  20.0 1.7 %collective-permute-start.8 = (bf16[1040,128]{1,0:T(8,128)(2,1)S(1)}, bf16[1040,128]{1,0:T(8,128)(2,1)S(1)}, u32[]{:S(2)}, u32[]{:S(2)}) collective-permute-start(bf16[1040,128]{1,0:T(8,128)(2,1)S(1)} %join_half.3), channel_id=1, source_target_pairs={{8,16},{12,20},{16,8},{20,12},{0,4},{4,0},{24,28},{28,24},{9,17},{... | collective-permute-start | bytes 798728 | tf_op jit(solution)/shard_map/ppermute | solution.py:421
  21.8 0.0 collective-permute-done.1.rest_1_
  21.8 0.0 collective-permute-done.2.rest_2_
  21.8 0.3 collective-permute-done.4.refs_3_
  22.1 1.5 %collective-permute-start.5 = (bf16[128,2048]{1,0:T(8,128)(2,1)S(1)}, bf16[128,2048]{1,0:T(8,128)(2,1)S(1)}, u32[]{:S(2)}, u32[]{:S(2)}) collective-permute-start(bf16[128,2048]{1,0:T(8,128)(2,1)S(1)} %collective-permute-done.1.rest_1_), channel_id=1, source_target_pairs={{0,2},{1,3},{2,0},{3,1},{4,6},{5,7},{6,4},{7,5},{8,10},{9,11},{10,... | collective-permute-start | bytes 1572872 | tf_op jit(solution)/shard_map/ppermute | solution.py:384
  23.6 4.2 %collective-permute-done.8.refs_4_ = bf16[1040,128]{1,0:T(8,128)(2,1)S(1)} collective-permute-done((bf16[1040,128]{1,0:T(8,128)(2,1)S(1)}, bf16[1040,128]{1,0:T(8,128)(2,1)S(1)}, u32[]{:S(2)}, u32[]{:S(2)}) %collective-permute-start.8) | collective-permute-done | bytes 266272 | tf_op jit(solution)/shard_map/ppermute | solution.py:421
  27.8 0.2 join_even.1
  28.0 0.1 collective-permute-start.9
  28.0 3.0 %collective-permute-done.10.came_ref = bf16[1,2,1040,128]{3,2,1,0:T(8,128)(2,1)S(1)} collective-permute-done((bf16[1,2,1040,128]{3,2,1,0:T(8,128)(2,1)S(1)}, bf16[1,2,1040,128]{3,2,1,0:T(8,128)(2,1)S(1)}, u32[]{:S(2)}, u32[]{:S(2)}) %collective-permute-start.10) | collective-permute-done | bytes 532512 | tf_op jit(solution)/shard_map/ppermute | solution.py:428
  31.0 0.1 join_second.3
  31.1 0.0 copy-start.4
  31.1 0.0 copy-start.5
  31.1 1.7 %collective-permute-start.12 = (bf16[1040,128]{1,0:T(8,128)(2,1)S(1)}, bf16[1040,128]{1,0:T(8,128)(2,1)S(1)}, u32[]{:S(2)}, u32[]{:S(2)}) collective-permute-start(bf16[1040,128]{1,0:T(8,128)(2,1)S(1)} %join_second.3), channel_id=1, source_target_pairs={{8,16},{12,20},{16,8},{20,12},{0,4},{4,0},{24,28},{28,24},{9,17},{... | collective-permute-start | bytes 798728 | tf_op jit(solution)/shard_map/ppermute | solution.py:441
  32.8 0.1 join_second.2
  32.9 0.4 collective-permute-start.11
  33.3 1.5 %collective-permute-done.5.rest_3_ = bf16[128,2048]{1,0:T(8,128)(2,1)S(1)} collective-permute-done((bf16[128,2048]{1,0:T(8,128)(2,1)S(1)}, bf16[128,2048]{1,0:T(8,128)(2,1)S(1)}, u32[]{:S(2)}, u32[]{:S(2)}) %collective-permute-start.5) | collective-permute-done | bytes 524320 | tf_op jit(solution)/shard_map/ppermute | solution.py:384
  34.9 0.0 copy-done.4
  34.9 0.0 copy-done.5
  34.9 3.9 %feat_grad.1 = bf16[384,2048]{1,0:T(8,128)(2,1)} custom-call(s32[1,2]{1,0:T(1,128)S(1)} %copy-done.4, s32[1,4]{1,0:T(1,128)S(1)} %copy-done.5, bf16[384,2048]{1,0:T(8,128)(2,1)S(1)} %copy-done, bf16[128,2048]{1,0:T(8,128)(2,1)S(1)} %copy-done.1, bf16[128,2048]{1,0:T(8,128)(2,1)S(1)} %collective-permute-done.1.rest_1_, ...), custom_call_target="tpu_custom_call" | custom-call | flops 805306368 | bytes 5242892 | tf_op jit(solution)/shard_map/feat_grad/pallas_call | solution.py:318
  38.7 3.1 %collective-permute-done.9.even_ref = bf16[1,2,1040,128]{3,2,1,0:T(8,128)(2,1)S(1)} collective-permute-done((bf16[1,2,1040,128]{3,2,1,0:T(8,128)(2,1)S(1)}, bf16[1,2,1040,128]{3,2,1,0:T(8,128)(2,1)S(1)}, u32[]{:S(2)}, u32[]{:S(2)}) %collective-permute-start.9) | collective-permute-done | bytes 532512 | tf_op jit(solution)/shard_map/ppermute | solution.py:444
  41.9 0.0 collective-permute-done.12.odd_ref
  41.9 1.0 %update.2.rest_0_ = bf16[128,2048]{1,0:T(8,128)(2,1)} custom-call(bf16[128,2048]{1,0:T(8,128)(2,1)S(1)} %copy-done.1, bf16[3,2,1040,128]{3,2,1,0:T(8,128)(2,1)S(1)} %get-tuple-element.26.refs_2_.rest_ref, bf16[1,2,1040,128]{3,2,1,0:T(8,128)(2,1)S(1)} %collective-permute-done.9.even_ref, bf16[1040,128]{1,0:T(8,128)(2,1)S(1)} %collective-permute-done.12.odd_ref), custom_call_target="tpu_custom_call" | custom-call | flops 1310720 | bytes 3444736 | tf_op jit(solution)/shard_map/update/pallas_call | solution.py:318
  42.9 1.7 %collective-permute-done.11.odd_ref = bf16[1040,128]{1,0:T(8,128)(2,1)S(1)} collective-permute-done((bf16[1040,128]{1,0:T(8,128)(2,1)S(1)}, bf16[1040,128]{1,0:T(8,128)(2,1)S(1)}, u32[]{:S(2)}, u32[]{:S(2)}) %collective-permute-start.11) | collective-permute-done | bytes 266272 | tf_op jit(solution)/shard_map/ppermute | solution.py:441
  44.6 1.0 %update.3 = bf16[128,2048]{1,0:T(8,128)(2,1)} custom-call(bf16[128,2048]{1,0:T(8,128)(2,1)S(1)} %copy-done.1, bf16[3,2,1040,128]{3,2,1,0:T(8,128)(2,1)S(1)} %get-tuple-element.26.refs_2_.rest_ref, bf16[1,2,1040,128]{3,2,1,0:T(8,128)(2,1)S(1)} %collective-permute-done.9.even_ref, ...), custom_call_target="tpu_custom_call", output_to_operand_aliasing={{}: (4, {})} | custom-call | flops 1310720 | bytes 3969024 | tf_op jit(solution)/shard_map/update/pallas_call | solution.py:318
  (3 shorter events, 0.0 us)
Async XLA Ops:
  0.6 1.4 %copy-start = (bf16[384,2048]{1,0:T(8,128)(2,1)S(1)}, bf16[384,2048]{1,0:T(8,128)(2,1)}, u32[]{:S(2)}) copy-start(bf16[384,2048]{1,0:T(8,128)(2,1)} %features_ref.13) | copy-start | bytes 4718596
  0.6 0.8 %copy-start.2 = (s32[1,384]{1,0:T(1,128)S(1)}, s32[1,384]{1,0:T(1,128)}, u32[]{:S(2)}) copy-start(s32[1,384]{1,0:T(1,128)} %labels_ref.10) | copy-start | bytes 4612
  2.1 0.7 %copy-start.3 = (s32[1,384]{1,0:T(1,128)S(1)}, s32[1,384]{1,0:T(1,128)}, u32[]{:S(2)}) copy-start(s32[1,384]{1,0:T(1,128)} %labels_ref.10) | copy-start | bytes 4612
  2.5 2.0 %collective-permute-start = (bf16[1,2,1040,128]{3,2,1,0:T(8,128)(2,1)S(1)}, bf16[1,2,1040,128]{3,2,1,0:T(8,128)(2,1)S(1)}, u32[]{:S(2)}, u32[]{:S(2)}) collective-permute-start(bf16[1,2,1040,128]{3,2,1,0:T(8,128)(2,1)S(1)} %away_first.1), channel_id=1, source_target_pairs={{0,4},{4,0},{8,12},{12,8},{16,20},{20,16},{24,28},{28,24},{1,5},{5... | collective-permute-start | bytes 1597448 | tf_op jit(solution)/shard_map/ppermute | solution.py:355
  4.1 1.6 %copy-start.1 = (bf16[128,2048]{1,0:T(8,128)(2,1)S(1)}, bf16[128,2048]{1,0:T(8,128)(2,1)}, u32[]{:S(2)}) copy-start(bf16[128,2048]{1,0:T(8,128)(2,1)} %memory_ref.3) | copy-start | bytes 1572868
  4.5 4.2 %collective-permute-start.6 = (bf16[3,2,1040,128]{3,2,1,0:T(8,128)(2,1)S(1)}, bf16[3,2,1040,128]{3,2,1,0:T(8,128)(2,1)S(1)}, u32[]{:S(2)}, u32[]{:S(2)}) collective-permute-start(bf16[3,2,1040,128]{3,2,1,0:T(8,128)(2,1)S(1)} %away_rest.1), channel_id=1, source_target_pairs={{0,4},{4,0},{8,12},{12,8},{16,20},{20,16},{24,28},{28,24},{1,5},{5... | collective-permute-start | bytes 4792328 | tf_op jit(solution)/shard_map/ppermute | solution.py:377
  4.7 9.2 %collective-permute-start.3 = (bf16[1040,128]{1,0:T(8,128)(2,1)S(1)}, bf16[1040,128]{1,0:T(8,128)(2,1)S(1)}, u32[]{:S(2)}, u32[]{:S(2)}) collective-permute-start(bf16[1040,128]{1,0:T(8,128)(2,1)S(1)} %get-tuple-element.21.refs_0_), channel_id=1, source_target_pairs={{0,8},{4,12},{8,0},{12,4},{16,24},{20,28},{24,16},{28,20},{1,9},{5... | collective-permute-start | bytes 798728 | tf_op jit(solution)/shard_map/ppermute | solution.py:403
  5.7 16.1 %collective-permute-start.1 = (bf16[128,2048]{1,0:T(8,128)(2,1)S(1)}, bf16[128,2048]{1,0:T(8,128)(2,1)S(1)}, u32[]{:S(2)}, u32[]{:S(2)}) collective-permute-start(bf16[128,2048]{1,0:T(8,128)(2,1)S(1)} %copy-done.1), channel_id=1, source_target_pairs={{0,1},{1,0},{2,3},{3,2},{4,5},{5,4},{6,7},{7,6},{8,9},{9,8},{10,11... | collective-permute-start | bytes 1572872 | tf_op jit(solution)/shard_map/ppermute | solution.py:384
  5.7 16.1 %collective-permute-start.2 = (bf16[128,2048]{1,0:T(8,128)(2,1)S(1)}, bf16[128,2048]{1,0:T(8,128)(2,1)S(1)}, u32[]{:S(2)}, u32[]{:S(2)}) collective-permute-start(bf16[128,2048]{1,0:T(8,128)(2,1)S(1)} %copy-done.1), channel_id=1, source_target_pairs={{0,2},{1,3},{2,0},{3,1},{4,6},{5,7},{6,4},{7,5},{8,10},{9,11},{10,... | collective-permute-start | bytes 1572872 | tf_op jit(solution)/shard_map/ppermute | solution.py:384
  7.7 11.9 %collective-permute-start.7 = (bf16[1040,128]{1,0:T(8,128)(2,1)S(1)}, bf16[1040,128]{1,0:T(8,128)(2,1)S(1)}, u32[]{:S(2)}, u32[]{:S(2)}) collective-permute-start(bf16[1040,128]{1,0:T(8,128)(2,1)S(1)} %get-tuple-element.27.refs_1_), channel_id=1, source_target_pairs={{0,8},{4,12},{8,0},{12,4},{16,24},{20,28},{24,16},{28,20},{1,9},{5... | collective-permute-start | bytes 798728 | tf_op jit(solution)/shard_map/ppermute | solution.py:403
  10.2 20.8 %collective-permute-start.10 = (bf16[1,2,1040,128]{3,2,1,0:T(8,128)(2,1)S(1)}, bf16[1,2,1040,128]{3,2,1,0:T(8,128)(2,1)S(1)}, u32[]{:S(2)}, u32[]{:S(2)}) collective-permute-start(bf16[1,2,1040,128]{3,2,1,0:T(8,128)(2,1)S(1)} %get-tuple-element.29.mine_ref), channel_id=1, source_target_pairs={{0,8},{4,12},{8,0},{12,4},{16,24},{20,28},{24,16},{28,20},{1,9},{5... | collective-permute-start | bytes 1597448 | tf_op jit(solution)/shard_map/ppermute | solution.py:428
  14.3 7.8 %collective-permute-start.4 = (bf16[1040,128]{1,0:T(8,128)(2,1)S(1)}, bf16[1040,128]{1,0:T(8,128)(2,1)S(1)}, u32[]{:S(2)}, u32[]{:S(2)}) collective-permute-start(bf16[1040,128]{1,0:T(8,128)(2,1)S(1)} %join_half.2), channel_id=1, source_target_pairs={{8,16},{12,20},{16,8},{20,12},{0,4},{4,0},{24,28},{28,24},{9,17},{... | collective-permute-start | bytes 798728 | tf_op jit(solution)/shard_map/ppermute | solution.py:421
  20.0 7.8 %collective-permute-start.8 = (bf16[1040,128]{1,0:T(8,128)(2,1)S(1)}, bf16[1040,128]{1,0:T(8,128)(2,1)S(1)}, u32[]{:S(2)}, u32[]{:S(2)}) collective-permute-start(bf16[1040,128]{1,0:T(8,128)(2,1)S(1)} %join_half.3), channel_id=1, source_target_pairs={{8,16},{12,20},{16,8},{20,12},{0,4},{4,0},{24,28},{28,24},{9,17},{... | collective-permute-start | bytes 798728 | tf_op jit(solution)/shard_map/ppermute | solution.py:421
  22.1 12.8 %collective-permute-start.5 = (bf16[128,2048]{1,0:T(8,128)(2,1)S(1)}, bf16[128,2048]{1,0:T(8,128)(2,1)S(1)}, u32[]{:S(2)}, u32[]{:S(2)}) collective-permute-start(bf16[128,2048]{1,0:T(8,128)(2,1)S(1)} %collective-permute-done.1.rest_1_), channel_id=1, source_target_pairs={{0,2},{1,3},{2,0},{3,1},{4,6},{5,7},{6,4},{7,5},{8,10},{9,11},{10,... | collective-permute-start | bytes 1572872 | tf_op jit(solution)/shard_map/ppermute | solution.py:384
  28.0 13.9 %collective-permute-start.9 = (bf16[1,2,1040,128]{3,2,1,0:T(8,128)(2,1)S(1)}, bf16[1,2,1040,128]{3,2,1,0:T(8,128)(2,1)S(1)}, u32[]{:S(2)}, u32[]{:S(2)}) collective-permute-start(bf16[1,2,1040,128]{3,2,1,0:T(8,128)(2,1)S(1)} %join_even.1), channel_id=1, source_target_pairs={{0,8},{4,12},{8,0},{12,4},{16,24},{20,28},{24,16},{28,20},{1,9},{5... | collective-permute-start | bytes 1597448 | tf_op jit(solution)/shard_map/ppermute | solution.py:444
  31.1 3.8 %copy-start.4 = (s32[1,2]{1,0:T(1,128)S(1)}, s32[1,2]{1,0:T(1,128)}, u32[]{:S(2)}) copy-start(s32[1,2]{1,0:T(1,128)} %requests_ref.1) | copy-start | bytes 28
  31.1 3.8 %copy-start.5 = (s32[1,4]{1,0:T(1,128)S(1)}, s32[1,4]{1,0:T(1,128)}, u32[]{:S(2)}) copy-start(s32[1,4]{1,0:T(1,128)} %owners_ref.1) | copy-start | bytes 52
  31.1 10.8 %collective-permute-start.12 = (bf16[1040,128]{1,0:T(8,128)(2,1)S(1)}, bf16[1040,128]{1,0:T(8,128)(2,1)S(1)}, u32[]{:S(2)}, u32[]{:S(2)}) collective-permute-start(bf16[1040,128]{1,0:T(8,128)(2,1)S(1)} %join_second.3), channel_id=1, source_target_pairs={{8,16},{12,20},{16,8},{20,12},{0,4},{4,0},{24,28},{28,24},{9,17},{... | collective-permute-start | bytes 798728 | tf_op jit(solution)/shard_map/ppermute | solution.py:441
  32.9 11.7 %collective-permute-start.11 = (bf16[1040,128]{1,0:T(8,128)(2,1)S(1)}, bf16[1040,128]{1,0:T(8,128)(2,1)S(1)}, u32[]{:S(2)}, u32[]{:S(2)}) collective-permute-start(bf16[1040,128]{1,0:T(8,128)(2,1)S(1)} %join_second.2), channel_id=1, source_target_pairs={{8,16},{12,20},{16,8},{20,12},{0,4},{4,0},{24,28},{28,24},{9,17},{... | collective-permute-start | bytes 798728 | tf_op jit(solution)/shard_map/ppermute | solution.py:441

commit v10 on v9

--- a/solution.py
+++ b/solution.py
@@ -436,7 +436,7 @@
                     "join_second",
                     jax.ShapeDtypeStruct((pay_rows, LANES), bf16),
                     (second, *even_came),
-                    10**9,
+                    2 * 10**9,
                 )
                 odd_came.append(lax.ppermute(leaves, "region", odd))
         else:

time: 46 us -> 46 us (level)
    ppermute x3, waiting for transfers between devices: 1.55 us -> 5.19 us  [fetch(): lax.ppermute(block, 'group', [(g, g ^ step) for g in range(group_count)])]
    ppermute x4, waiting for transfers between devices: 6.21 us -> 4.16 us  [on_device(): odd_came.append(lax.ppermute(leaves, 'region', odd))]
    ppermute x1, waiting for transfers between devices: 3.11 us -> 1.43 us  [on_device(): even_came = [lax.ppermute(even_next, 'region', even)]]
    ppermute x1, waiting for transfers between devices: 0.01 us -> 1.26 us  [on_device(): lax.ppermute(away_rest, 'region', swap)]
    ppermute x2, waiting for transfers between devices: 6.21 us -> 5.48 us  [on_device(): even_came = [lax.ppermute(x, 'region', even) for x in first]]
    ppermute x1, starting transfers between devices: 1.05 us -> 0.51 us  [on_device(): even_came = [lax.ppermute(second, 'region', even)]]
  transfers between devices with their start and end apart: 13 -> 13, of which waited for: 9 -> 11; matrix products, arithmetic and copies ran while one was open for 0% -> 0% of each run, Pallas kernels for 19% -> 19%
where the time goes in v10:
time: 46 us; the launch traced here: 45.6 us
  waiting for transfers between devices  20.9 us (45%)
  starting transfers between devices  12.1 us (26%)
  Pallas kernels  10.3 us (22%)
  local copies, waits for them, and re-layouts  1.52 us (3%)
  between operations  0.74 us (2%)
    pallas_call x13, Pallas kernels, call(): pl.pallas_call(kernel, out_shape=out_shape, in_specs=specs, out_specs=[ou...  10.3 us
    ppermute x4, starting transfers between devices, on_device(): odd_came.append(lax.ppermute(leaves, 'region', odd))  5.63 us
    ppermute x2, waiting for transfers between devices, on_device(): even_came = [lax.ppermute(x, 'region', even) for x in first]  5.48 us
    ppermute x3, waiting for transfers between devices, fetch(): lax.ppermute(block, 'group', [(g, g ^ step) for g in range(group_count)])  5.19 us
    ppermute x4, waiting for transfers between devices, on_device(): odd_came.append(lax.ppermute(leaves, 'region', odd))  4.16 us
    ppermute x3, starting transfers between devices, fetch(): lax.ppermute(block, 'group', [(g, g ^ step) for g in range(group_count)])  3.68 us
    ppermute x1, waiting for transfers between devices, on_device(): even_came = [lax.ppermute(second, 'region', even)]  2.96 us
    ppermute x2, starting transfers between devices, on_device(): even_came = [lax.ppermute(x, 'region', even) for x in first]  2.04 us
  transfers between devices with their start and end apart: 13, of which 11 were waited for; matrix products, arithmetic and copies ran while one was open for 0% of the time, Pallas kernels for 19%

profile of v10, /device:TPU:10, one launch (start us, length us, event | category | flops | bytes accessed | tf_op | source)
XLA Modules:
  0.0 45.6 jit_solution(13616015409561244913)
XLA Ops:
  0.6 0.0 copy-start
  0.6 0.0 copy-start.2
  0.7 0.8 %copy-done.2 = s32[1,384]{1,0:T(1,128)S(1)} copy-done((s32[1,384]{1,0:T(1,128)S(1)}, s32[1,384]{1,0:T(1,128)}, u32[]{:S(2)}) %copy-start.2) | copy-done | bytes 1560
  1.5 0.6 %copy-done = bf16[384,2048]{1,0:T(8,128)(2,1)S(1)} copy-done((bf16[384,2048]{1,0:T(8,128)(2,1)S(1)}, bf16[384,2048]{1,0:T(8,128)(2,1)}, u32[]{:S(2)}) %copy-start) | copy-done | bytes 1572888
  2.1 0.0 copy-start.3
  2.1 0.5 %away_first.1 = bf16[1,2,1040,128]{3,2,1,0:T(8,128)(2,1)S(1)} custom-call(bf16[128,384]{1,0:T(8,128)(2,1)S(1)} %match_first.1.match_ref, bf16[384,2048]{1,0:T(8,128)(2,1)S(1)} %copy-done), custom_call_target="tpu_custom_call" | custom-call | flops 201326592 | bytes 2203648 | tf_op jit(solution)/shard_map/away_first/pallas_call | solution.py:318
  2.5 0.1 collective-permute-start
  2.6 0.1 copy-done.3
  2.7 1.3 %away_rest.1 = bf16[3,2,1040,128]{3,2,1,0:T(8,128)(2,1)S(1)} custom-call(s32[1,384]{1,0:T(1,128)S(1)} %copy-done.3, bf16[384,2048]{1,0:T(8,128)(2,1)S(1)} %copy-done), custom_call_target="tpu_custom_call" | custom-call | flops 603979776 | bytes 3171072 | tf_op jit(solution)/shard_map/away_rest/pallas_call | solution.py:318
  4.1 0.4 collective-permute-done.came_ref.sibling_ref
  4.5 0.1 collective-permute-start.6
  4.7 1.0 %collective-permute-start.3 = (bf16[1040,128]{1,0:T(8,128)(2,1)S(1)}, bf16[1040,128]{1,0:T(8,128)(2,1)S(1)}, u32[]{:S(2)}, u32[]{:S(2)}) collective-permute-start(bf16[1040,128]{1,0:T(8,128)(2,1)S(1)} %get-tuple-element.21.refs_0_), channel_id=1, source_target_pairs={{0,8},{4,12},{8,0},{12,4},{16,24},{20,28},{24,16},{28,20},{1,9},{5... | collective-permute-start | bytes 798728 | tf_op jit(solution)/shard_map/ppermute | solution.py:403
  5.7 1.0 %collective-permute-start.7 = (bf16[1040,128]{1,0:T(8,128)(2,1)S(1)}, bf16[1040,128]{1,0:T(8,128)(2,1)S(1)}, u32[]{:S(2)}, u32[]{:S(2)}) collective-permute-start(bf16[1040,128]{1,0:T(8,128)(2,1)S(1)} %get-tuple-element.27.refs_1_), channel_id=1, source_target_pairs={{0,8},{4,12},{8,0},{12,4},{16,24},{20,28},{24,16},{28,20},{1,9},{5... | collective-permute-start | bytes 798728 | tf_op jit(solution)/shard_map/ppermute | solution.py:403
  6.7 1.3 %collective-permute-done.6.came_ref = bf16[3,2,1040,128]{3,2,1,0:T(8,128)(2,1)S(1)} collective-permute-done((bf16[3,2,1040,128]{3,2,1,0:T(8,128)(2,1)S(1)}, bf16[3,2,1040,128]{3,2,1,0:T(8,128)(2,1)S(1)}, u32[]{:S(2)}, u32[]{:S(2)}) %collective-permute-start.6) | collective-permute-done | bytes 1597472 | tf_op jit(solution)/shard_map/ppermute | solution.py:377
  8.0 1.4 %chip_rest.1 = (bf16[1,2,1040,128]{3,2,1,0:T(8,128)(2,1)S(1)}, bf16[3,2,1040,128]{3,2,1,0:T(8,128)(2,1)S(1)}) custom-call(s32[1,384]{1,0:T(1,128)S(1)} %copy-done.3, bf16[384,2048]{1,0:T(8,128)(2,1)S(1)} %copy-done, bf16[3,2,1040,128]{3,2,1,0:T(8,128)(2,1)S(1)} %collective-permute-done.6.came_ref), custom_call_target="tpu_custom_call" | custom-call | flops 603979776 | bytes 5300992 | tf_op jit(solution)/shard_map/chip_rest/pallas_call | solution.py:318
  9.4 0.5 %collective-permute-start.10 = (bf16[1,2,1040,128]{3,2,1,0:T(8,128)(2,1)S(1)}, bf16[1,2,1040,128]{3,2,1,0:T(8,128)(2,1)S(1)}, u32[]{:S(2)}, u32[]{:S(2)}) collective-permute-start(bf16[1,2,1040,128]{3,2,1,0:T(8,128)(2,1)S(1)} %get-tuple-element.29.mine_ref), channel_id=1, source_target_pairs={{0,8},{4,12},{8,0},{12,4},{16,24},{20,28},{24,16},{28,20},{1,9},{5... | collective-permute-start | bytes 1597448 | tf_op jit(solution)/shard_map/ppermute | solution.py:428
  9.9 0.0 copy-done.1
  9.9 0.2 collective-permute-start.1
  10.1 1.9 %collective-permute-start.2 = (bf16[128,2048]{1,0:T(8,128)(2,1)S(1)}, bf16[128,2048]{1,0:T(8,128)(2,1)S(1)}, u32[]{:S(2)}, u32[]{:S(2)}) collective-permute-start(bf16[128,2048]{1,0:T(8,128)(2,1)S(1)} %copy-done.1), channel_id=1, source_target_pairs={{0,2},{1,3},{2,0},{3,1},{4,6},{5,7},{6,4},{7,5},{8,10},{9,11},{10,... | collective-permute-start | bytes 1572872 | tf_op jit(solution)/shard_map/ppermute | solution.py:384
  11.9 1.9 %collective-permute-done.3.came_ref = bf16[1040,128]{1,0:T(8,128)(2,1)S(1)} collective-permute-done((bf16[1040,128]{1,0:T(8,128)(2,1)S(1)}, bf16[1040,128]{1,0:T(8,128)(2,1)S(1)}, u32[]{:S(2)}, u32[]{:S(2)}) %collective-permute-start.3) | collective-permute-done | bytes 266272 | tf_op jit(solution)/shard_map/ppermute | solution.py:403
  13.9 0.4 join_half.2
  14.3 1.7 %collective-permute-start.4 = (bf16[1040,128]{1,0:T(8,128)(2,1)S(1)}, bf16[1040,128]{1,0:T(8,128)(2,1)S(1)}, u32[]{:S(2)}, u32[]{:S(2)}) collective-permute-start(bf16[1040,128]{1,0:T(8,128)(2,1)S(1)} %join_half.2), channel_id=1, source_target_pairs={{8,16},{12,20},{16,8},{20,12},{0,4},{4,0},{24,28},{28,24},{9,17},{... | collective-permute-start | bytes 798728 | tf_op jit(solution)/shard_map/ppermute | solution.py:421
  16.1 3.5 %collective-permute-done.7.came_ref = bf16[1040,128]{1,0:T(8,128)(2,1)S(1)} collective-permute-done((bf16[1040,128]{1,0:T(8,128)(2,1)S(1)}, bf16[1040,128]{1,0:T(8,128)(2,1)S(1)}, u32[]{:S(2)}, u32[]{:S(2)}) %collective-permute-start.7) | collective-permute-done | bytes 266272 | tf_op jit(solution)/shard_map/ppermute | solution.py:403
  19.6 0.4 join_half.3
  20.0 1.7 %collective-permute-start.8 = (bf16[1040,128]{1,0:T(8,128)(2,1)S(1)}, bf16[1040,128]{1,0:T(8,128)(2,1)S(1)}, u32[]{:S(2)}, u32[]{:S(2)}) collective-permute-start(bf16[1040,128]{1,0:T(8,128)(2,1)S(1)} %join_half.3), channel_id=1, source_target_pairs={{8,16},{12,20},{16,8},{20,12},{0,4},{4,0},{24,28},{28,24},{9,17},{... | collective-permute-start | bytes 798728 | tf_op jit(solution)/shard_map/ppermute | solution.py:421
  21.8 1.8 %collective-permute-done.1.rest_1_ = bf16[128,2048]{1,0:T(8,128)(2,1)S(1)} collective-permute-done((bf16[128,2048]{1,0:T(8,128)(2,1)S(1)}, bf16[128,2048]{1,0:T(8,128)(2,1)S(1)}, u32[]{:S(2)}, u32[]{:S(2)}) %collective-permute-start.1) | collective-permute-done | bytes 524320 | tf_op jit(solution)/shard_map/ppermute | solution.py:384
  23.6 0.2 collective-permute-done.2.rest_2_
  23.7 0.0 collective-permute-done.4.refs_3_
  23.7 1.6 %collective-permute-start.5 = (bf16[128,2048]{1,0:T(8,128)(2,1)S(1)}, bf16[128,2048]{1,0:T(8,128)(2,1)S(1)}, u32[]{:S(2)}, u32[]{:S(2)}) collective-permute-start(bf16[128,2048]{1,0:T(8,128)(2,1)S(1)} %collective-permute-done.1.rest_1_), channel_id=1, source_target_pairs={{0,2},{1,3},{2,0},{3,1},{4,6},{5,7},{6,4},{7,5},{8,10},{9,11},{10,... | collective-permute-start | bytes 1572872 | tf_op jit(solution)/shard_map/ppermute | solution.py:384
  25.4 2.4 %collective-permute-done.8.refs_4_ = bf16[1040,128]{1,0:T(8,128)(2,1)S(1)} collective-permute-done((bf16[1040,128]{1,0:T(8,128)(2,1)S(1)}, bf16[1040,128]{1,0:T(8,128)(2,1)S(1)}, u32[]{:S(2)}, u32[]{:S(2)}) %collective-permute-start.8) | collective-permute-done | bytes 266272 | tf_op jit(solution)/shard_map/ppermute | solution.py:421
  27.8 0.2 join_even.1
  28.0 0.1 collective-permute-start.9
  28.0 3.0 %collective-permute-done.10.came_ref = bf16[1,2,1040,128]{3,2,1,0:T(8,128)(2,1)S(1)} collective-permute-done((bf16[1,2,1040,128]{3,2,1,0:T(8,128)(2,1)S(1)}, bf16[1,2,1040,128]{3,2,1,0:T(8,128)(2,1)S(1)}, u32[]{:S(2)}, u32[]{:S(2)}) %collective-permute-start.10) | collective-permute-done | bytes 532512 | tf_op jit(solution)/shard_map/ppermute | solution.py:428
  31.0 0.1 join_second.3
  31.1 0.0 copy-start.4
  31.1 0.0 copy-start.5
  31.1 1.8 %collective-permute-start.12 = (bf16[1040,128]{1,0:T(8,128)(2,1)S(1)}, bf16[1040,128]{1,0:T(8,128)(2,1)S(1)}, u32[]{:S(2)}, u32[]{:S(2)}) collective-permute-start(bf16[1040,128]{1,0:T(8,128)(2,1)S(1)} %join_second.3), channel_id=1, source_target_pairs={{8,16},{12,20},{16,8},{20,12},{0,4},{4,0},{24,28},{28,24},{9,17},{... | collective-permute-start | bytes 798728 | tf_op jit(solution)/shard_map/ppermute | solution.py:441
  32.9 0.1 join_second.2
  32.9 0.4 collective-permute-start.11
  33.3 3.2 %collective-permute-done.5.rest_3_ = bf16[128,2048]{1,0:T(8,128)(2,1)S(1)} collective-permute-done((bf16[128,2048]{1,0:T(8,128)(2,1)S(1)}, bf16[128,2048]{1,0:T(8,128)(2,1)S(1)}, u32[]{:S(2)}, u32[]{:S(2)}) %collective-permute-start.5) | collective-permute-done | bytes 524320 | tf_op jit(solution)/shard_map/ppermute | solution.py:384
  36.5 0.0 copy-done.4
  36.5 0.0 copy-done.5
  36.6 3.9 %feat_grad.1 = bf16[384,2048]{1,0:T(8,128)(2,1)} custom-call(s32[1,2]{1,0:T(1,128)S(1)} %copy-done.4, s32[1,4]{1,0:T(1,128)S(1)} %copy-done.5, bf16[384,2048]{1,0:T(8,128)(2,1)S(1)} %copy-done, bf16[128,2048]{1,0:T(8,128)(2,1)S(1)} %copy-done.1, bf16[128,2048]{1,0:T(8,128)(2,1)S(1)} %collective-permute-done.1.rest_1_, ...), custom_call_target="tpu_custom_call" | custom-call | flops 805306368 | bytes 5242892 | tf_op jit(solution)/shard_map/feat_grad/pallas_call | solution.py:318
  40.4 1.4 %collective-permute-done.9.even_ref = bf16[1,2,1040,128]{3,2,1,0:T(8,128)(2,1)S(1)} collective-permute-done((bf16[1,2,1040,128]{3,2,1,0:T(8,128)(2,1)S(1)}, bf16[1,2,1040,128]{3,2,1,0:T(8,128)(2,1)S(1)}, u32[]{:S(2)}, u32[]{:S(2)}) %collective-permute-start.9) | collective-permute-done | bytes 532512 | tf_op jit(solution)/shard_map/ppermute | solution.py:444
  41.9 0.0 collective-permute-done.12.odd_ref
  41.9 1.0 %update.2.rest_0_ = bf16[128,2048]{1,0:T(8,128)(2,1)} custom-call(bf16[128,2048]{1,0:T(8,128)(2,1)S(1)} %copy-done.1, bf16[3,2,1040,128]{3,2,1,0:T(8,128)(2,1)S(1)} %get-tuple-element.26.refs_2_.rest_ref, bf16[1,2,1040,128]{3,2,1,0:T(8,128)(2,1)S(1)} %collective-permute-done.9.even_ref, bf16[1040,128]{1,0:T(8,128)(2,1)S(1)} %collective-permute-done.12.odd_ref), custom_call_target="tpu_custom_call" | custom-call | flops 1310720 | bytes 3444736 | tf_op jit(solution)/shard_map/update/pallas_call | solution.py:318
  42.9 1.7 %collective-permute-done.11.odd_ref = bf16[1040,128]{1,0:T(8,128)(2,1)S(1)} collective-permute-done((bf16[1040,128]{1,0:T(8,128)(2,1)S(1)}, bf16[1040,128]{1,0:T(8,128)(2,1)S(1)}, u32[]{:S(2)}, u32[]{:S(2)}) %collective-permute-start.11) | collective-permute-done | bytes 266272 | tf_op jit(solution)/shard_map/ppermute | solution.py:441
  44.6 1.0 %update.3 = bf16[128,2048]{1,0:T(8,128)(2,1)} custom-call(bf16[128,2048]{1,0:T(8,128)(2,1)S(1)} %copy-done.1, bf16[3,2,1040,128]{3,2,1,0:T(8,128)(2,1)S(1)} %get-tuple-element.26.refs_2_.rest_ref, bf16[1,2,1040,128]{3,2,1,0:T(8,128)(2,1)S(1)} %collective-permute-done.9.even_ref, ...), custom_call_target="tpu_custom_call", output_to_operand_aliasing={{}: (4, {})} | custom-call | flops 1310720 | bytes 3969024 | tf_op jit(solution)/shard_map/update/pallas_call | solution.py:318
  (3 shorter events, 0.0 us)
Async XLA Ops:
  0.6 1.4 %copy-start = (bf16[384,2048]{1,0:T(8,128)(2,1)S(1)}, bf16[384,2048]{1,0:T(8,128)(2,1)}, u32[]{:S(2)}) copy-start(bf16[384,2048]{1,0:T(8,128)(2,1)} %features_ref.13) | copy-start | bytes 4718596
  0.6 0.8 %copy-start.2 = (s32[1,384]{1,0:T(1,128)S(1)}, s32[1,384]{1,0:T(1,128)}, u32[]{:S(2)}) copy-start(s32[1,384]{1,0:T(1,128)} %labels_ref.10) | copy-start | bytes 4612
  2.1 0.7 %copy-start.3 = (s32[1,384]{1,0:T(1,128)S(1)}, s32[1,384]{1,0:T(1,128)}, u32[]{:S(2)}) copy-start(s32[1,384]{1,0:T(1,128)} %labels_ref.10) | copy-start | bytes 4612
  2.5 2.0 %collective-permute-start = (bf16[1,2,1040,128]{3,2,1,0:T(8,128)(2,1)S(1)}, bf16[1,2,1040,128]{3,2,1,0:T(8,128)(2,1)S(1)}, u32[]{:S(2)}, u32[]{:S(2)}) collective-permute-start(bf16[1,2,1040,128]{3,2,1,0:T(8,128)(2,1)S(1)} %away_first.1), channel_id=1, source_target_pairs={{0,4},{4,0},{8,12},{12,8},{16,20},{20,16},{24,28},{28,24},{1,5},{5... | collective-permute-start | bytes 1597448 | tf_op jit(solution)/shard_map/ppermute | solution.py:355
  4.5 3.4 %collective-permute-start.6 = (bf16[3,2,1040,128]{3,2,1,0:T(8,128)(2,1)S(1)}, bf16[3,2,1040,128]{3,2,1,0:T(8,128)(2,1)S(1)}, u32[]{:S(2)}, u32[]{:S(2)}) collective-permute-start(bf16[3,2,1040,128]{3,2,1,0:T(8,128)(2,1)S(1)} %away_rest.1), channel_id=1, source_target_pairs={{0,4},{4,0},{8,12},{12,8},{16,20},{20,16},{24,28},{28,24},{1,5},{5... | collective-permute-start | bytes 4792328 | tf_op jit(solution)/shard_map/ppermute | solution.py:377
  4.7 5.2 %copy-start.1 = (bf16[128,2048]{1,0:T(8,128)(2,1)S(1)}, bf16[128,2048]{1,0:T(8,128)(2,1)}, u32[]{:S(2)}) copy-start(bf16[128,2048]{1,0:T(8,128)(2,1)} %memory_ref.3) | copy-start | bytes 1572868
  4.7 9.2 %collective-permute-start.3 = (bf16[1040,128]{1,0:T(8,128)(2,1)S(1)}, bf16[1040,128]{1,0:T(8,128)(2,1)S(1)}, u32[]{:S(2)}, u32[]{:S(2)}) collective-permute-start(bf16[1040,128]{1,0:T(8,128)(2,1)S(1)} %get-tuple-element.21.refs_0_), channel_id=1, source_target_pairs={{0,8},{4,12},{8,0},{12,4},{16,24},{20,28},{24,16},{28,20},{1,9},{5... | collective-permute-start | bytes 798728 | tf_op jit(solution)/shard_map/ppermute | solution.py:403
  5.7 13.9 %collective-permute-start.7 = (bf16[1040,128]{1,0:T(8,128)(2,1)S(1)}, bf16[1040,128]{1,0:T(8,128)(2,1)S(1)}, u32[]{:S(2)}, u32[]{:S(2)}) collective-permute-start(bf16[1040,128]{1,0:T(8,128)(2,1)S(1)} %get-tuple-element.27.refs_1_), channel_id=1, source_target_pairs={{0,8},{4,12},{8,0},{12,4},{16,24},{20,28},{24,16},{28,20},{1,9},{5... | collective-permute-start | bytes 798728 | tf_op jit(solution)/shard_map/ppermute | solution.py:403
  9.4 21.6 %collective-permute-start.10 = (bf16[1,2,1040,128]{3,2,1,0:T(8,128)(2,1)S(1)}, bf16[1,2,1040,128]{3,2,1,0:T(8,128)(2,1)S(1)}, u32[]{:S(2)}, u32[]{:S(2)}) collective-permute-start(bf16[1,2,1040,128]{3,2,1,0:T(8,128)(2,1)S(1)} %get-tuple-element.29.mine_ref), channel_id=1, source_target_pairs={{0,8},{4,12},{8,0},{12,4},{16,24},{20,28},{24,16},{28,20},{1,9},{5... | collective-permute-start | bytes 1597448 | tf_op jit(solution)/shard_map/ppermute | solution.py:428
  9.9 13.7 %collective-permute-start.1 = (bf16[128,2048]{1,0:T(8,128)(2,1)S(1)}, bf16[128,2048]{1,0:T(8,128)(2,1)S(1)}, u32[]{:S(2)}, u32[]{:S(2)}) collective-permute-start(bf16[128,2048]{1,0:T(8,128)(2,1)S(1)} %copy-done.1), channel_id=1, source_target_pairs={{0,1},{1,0},{2,3},{3,2},{4,5},{5,4},{6,7},{7,6},{8,9},{9,8},{10,11... | collective-permute-start | bytes 1572872 | tf_op jit(solution)/shard_map/ppermute | solution.py:384
  10.1 13.7 %collective-permute-start.2 = (bf16[128,2048]{1,0:T(8,128)(2,1)S(1)}, bf16[128,2048]{1,0:T(8,128)(2,1)S(1)}, u32[]{:S(2)}, u32[]{:S(2)}) collective-permute-start(bf16[128,2048]{1,0:T(8,128)(2,1)S(1)} %copy-done.1), channel_id=1, source_target_pairs={{0,2},{1,3},{2,0},{3,1},{4,6},{5,7},{6,4},{7,5},{8,10},{9,11},{10,... | collective-permute-start | bytes 1572872 | tf_op jit(solution)/shard_map/ppermute | solution.py:384
  14.3 9.4 %collective-permute-start.4 = (bf16[1040,128]{1,0:T(8,128)(2,1)S(1)}, bf16[1040,128]{1,0:T(8,128)(2,1)S(1)}, u32[]{:S(2)}, u32[]{:S(2)}) collective-permute-start(bf16[1040,128]{1,0:T(8,128)(2,1)S(1)} %join_half.2), channel_id=1, source_target_pairs={{8,16},{12,20},{16,8},{20,12},{0,4},{4,0},{24,28},{28,24},{9,17},{... | collective-permute-start | bytes 798728 | tf_op jit(solution)/shard_map/ppermute | solution.py:421
  20.0 7.8 %collective-permute-start.8 = (bf16[1040,128]{1,0:T(8,128)(2,1)S(1)}, bf16[1040,128]{1,0:T(8,128)(2,1)S(1)}, u32[]{:S(2)}, u32[]{:S(2)}) collective-permute-start(bf16[1040,128]{1,0:T(8,128)(2,1)S(1)} %join_half.3), channel_id=1, source_target_pairs={{8,16},{12,20},{16,8},{20,12},{0,4},{4,0},{24,28},{28,24},{9,17},{... | collective-permute-start | bytes 798728 | tf_op jit(solution)/shard_map/ppermute | solution.py:421
  23.7 12.8 %collective-permute-start.5 = (bf16[128,2048]{1,0:T(8,128)(2,1)S(1)}, bf16[128,2048]{1,0:T(8,128)(2,1)S(1)}, u32[]{:S(2)}, u32[]{:S(2)}) collective-permute-start(bf16[128,2048]{1,0:T(8,128)(2,1)S(1)} %collective-permute-done.1.rest_1_), channel_id=1, source_target_pairs={{0,2},{1,3},{2,0},{3,1},{4,6},{5,7},{6,4},{7,5},{8,10},{9,11},{10,... | collective-permute-start | bytes 1572872 | tf_op jit(solution)/shard_map/ppermute | solution.py:384
  28.0 13.9 %collective-permute-start.9 = (bf16[1,2,1040,128]{3,2,1,0:T(8,128)(2,1)S(1)}, bf16[1,2,1040,128]{3,2,1,0:T(8,128)(2,1)S(1)}, u32[]{:S(2)}, u32[]{:S(2)}) collective-permute-start(bf16[1,2,1040,128]{3,2,1,0:T(8,128)(2,1)S(1)} %join_even.1), channel_id=1, source_target_pairs={{0,8},{4,12},{8,0},{12,4},{16,24},{20,28},{24,16},{28,20},{1,9},{5... | collective-permute-start | bytes 1597448 | tf_op jit(solution)/shard_map/ppermute | solution.py:444
  31.1 5.5 %copy-start.4 = (s32[1,2]{1,0:T(1,128)S(1)}, s32[1,2]{1,0:T(1,128)}, u32[]{:S(2)}) copy-start(s32[1,2]{1,0:T(1,128)} %requests_ref.1) | copy-start | bytes 28
  31.1 5.5 %copy-start.5 = (s32[1,4]{1,0:T(1,128)S(1)}, s32[1,4]{1,0:T(1,128)}, u32[]{:S(2)}) copy-start(s32[1,4]{1,0:T(1,128)} %owners_ref.1) | copy-start | bytes 52
  31.1 10.8 %collective-permute-start.12 = (bf16[1040,128]{1,0:T(8,128)(2,1)S(1)}, bf16[1040,128]{1,0:T(8,128)(2,1)S(1)}, u32[]{:S(2)}, u32[]{:S(2)}) collective-permute-start(bf16[1040,128]{1,0:T(8,128)(2,1)S(1)} %join_second.3), channel_id=1, source_target_pairs={{8,16},{12,20},{16,8},{20,12},{0,4},{4,0},{24,28},{28,24},{9,17},{... | collective-permute-start | bytes 798728 | tf_op jit(solution)/shard_map/ppermute | solution.py:441
  32.9 11.7 %collective-permute-start.11 = (bf16[1040,128]{1,0:T(8,128)(2,1)S(1)}, bf16[1040,128]{1,0:T(8,128)(2,1)S(1)}, u32[]{:S(2)}, u32[]{:S(2)}) collective-permute-start(bf16[1040,128]{1,0:T(8,128)(2,1)S(1)} %join_second.2), channel_id=1, source_target_pairs={{8,16},{12,20},{16,8},{20,12},{0,4},{4,0},{24,28},{28,24},{9,17},{... | collective-permute-start | bytes 798728 | tf_op jit(solution)/shard_map/ppermute | solution.py:441
